TPU v7x, 32 devices: a whole 2x2x4 slice. The times are simulated.
32 devices in a mesh: ctx: 8 (over y, x, core), fsdp: 4 (over z).
Axes of the slice: x: 2, y: 2, z: 4, core: 2. Of those that a mesh axis runs over, the one named last changes fastest.
Arguments:
- tokens: bfloat16 [4, 1024, 2048], P('fsdp', 'ctx'), may hold values from -6 to 6
- gain_attn: bfloat16 [2048], P(('ctx', 'fsdp')), may hold values from 0.5 to 1.5
- w_qkv: bfloat16 [2048, 6144], P(('ctx', 'fsdp')), may hold values from -0.1875 to 0.1875
- w_out: bfloat16 [2048, 2048], P(('ctx', 'fsdp')), may hold values from -0.5 to 0.5
- gain_ffn: bfloat16 [2048], P(('ctx', 'fsdp')), may hold values from 0.5 to 1.5
- w_router: bfloat16 [2048, 64], P(('ctx', 'fsdp')), may hold values from -0.0625 to 0.0625
- w_shared_in: bfloat16 [2048, 5632], P(('ctx', 'fsdp')), may hold values from -0.125 to 0.125
- w_shared_down: bfloat16 [2816, 2048], P(('ctx', 'fsdp')), may hold values from -0.109375 to 0.109375
- w_expert_in: bfloat16 [128, 2048, 1408], P(('ctx', 'fsdp')), may hold values from -0.125 to 0.125
- w_expert_down: bfloat16 [128, 704, 2048], P(('ctx', 'fsdp')), may hold values from -0.15625 to 0.15625
- routes: int32 [4, 1024, 6], P('fsdp', 'ctx'), may hold values from 0 to 63, all different within a row; in each aligned block of 128 rows (0 to 127, 128 to 255, ..., all dimensions but the last counted through in order) at most 20 rows name the same one
- plan: int32 [16], replicated, may hold values from 0 to 15, each once
- cotangent: bfloat16 [4, 1024, 2048], P('fsdp', 'ctx'), may hold values from -6 to 6
Outputs:
- result: bfloat16 [4, 1024, 2048], P('fsdp', 'ctx')
- tokens_grad: float32 [4, 1024, 2048], P('fsdp', 'ctx')
- gain_attn_grad: float32 [2048], P(('ctx', 'fsdp'))
- qkv_grad: float32 [2048, 6144], P(('ctx', 'fsdp'))
- out_grad: float32 [2048, 2048], P(('ctx', 'fsdp'))
- gain_ffn_grad: float32 [2048], P(('ctx', 'fsdp'))
- router_grad: float32 [2048, 64], P(('ctx', 'fsdp'))
- shared_in_grad: float32 [2048, 5632], P(('ctx', 'fsdp'))
- shared_down_grad: float32 [2816, 2048], P(('ctx', 'fsdp'))
- expert_in_grad: float32 [128, 2048, 1408], P(('ctx', 'fsdp'))
- expert_down_grad: float32 [128, 704, 2048], P(('ctx', 'fsdp'))
Inputs may be any that keep to these rules, and one draw needn't show every extreme that they name: `routes`: each token names 6 different experts; among the rows of one device (aligned blocks of 128 tokens) no expert is named more than 20 times, a bound that some block reaches. `plan`: each half-block of positions once.
All inputs are finite; a program needn't handle non-finite values.
Results may differ from a plain program's by a relative error of at most 0.022.
Values may be sent and summed in bfloat16 or wider, within the bound.
No kernel may reach another device: no remote copies, remote signals or barrier semaphores. Data moves between devices by JAX's collectives and lax.ppermute only.
A program may use at most 512 MiB of HBM per device.

v0:
```python
import jax
import jax.numpy as jnp
from jax import lax
from jax.sharding import PartitionSpec as P

HEADS = 16
EXPERTS = 64
CAP = 20


EPSILON = 1e-06
ROPE_BASE = 10000.0
NEGATIVE = -1e30


def rms_scale(values, gain):
    inverse = lax.rsqrt(jnp.mean(values * values, axis=-1, keepdims=True) + EPSILON)
    return values * inverse * gain


def gating(joined):
    half_size = joined.shape[-1] // 2
    return jax.nn.silu(joined[..., :half_size]) * joined[..., half_size:]


def gating_back(joined, upstream):
    return jax.vjp(gating, joined)[1](upstream)[0]


def positions(plan, first_row, amount, per_device):
    half_block = per_device // 2
    row_ids = first_row + jnp.arange(amount, dtype=jnp.int32)
    blocks = row_ids // half_block
    block_ids = jnp.arange(plan.shape[0], dtype=jnp.int32)
    placed = jnp.sum(jnp.where(blocks[:, None] == block_ids[None, :], plan[None, :], 0), axis=1)
    return placed * half_block + row_ids % half_block


def rotate(values, places, head_count):
    amount, model_width = values.shape
    head_size = model_width // head_count
    half_size = head_size // 2
    frequency = ROPE_BASE ** (-2.0 * jnp.arange(half_size, dtype=jnp.float32) / head_size)
    angles = places.astype(jnp.float32)[:, None] * frequency[None, :]
    cosine = jnp.cos(angles)[:, None, :]
    sine_part = jnp.sin(angles)[:, None, :]
    split_heads = values.reshape(amount, head_count, head_size)
    first_part = split_heads[..., :half_size]
    second = split_heads[..., half_size:]
    turned = jnp.concatenate(
        [first_part * cosine - second * sine_part, second * cosine + first_part * sine_part],
        axis=-1,
    )
    return turned.reshape(amount, model_width)


def contract_rows(left, right):
    return lax.dot_general(
        left, right, (((0,), (0,)), ((), ())), preferred_element_type=jnp.float32
    )


def contract_cols(left, right):
    return lax.dot_general(
        left, right, (((1,), (1,)), ((), ())), preferred_element_type=jnp.float32
    )


def first_weights(gain_attn, w_qkv, w_out):
    return (
        lax.all_gather(gain_attn, ("ctx", "fsdp"), axis=0, tiled=True),
        lax.all_gather(w_qkv, ("ctx", "fsdp"), axis=0, tiled=True),
        lax.all_gather(w_out, ("ctx", "fsdp"), axis=0, tiled=True),
    )


def second_weights(gain_ffn, w_router, w_shared_in, w_shared_down):
    return (
        lax.all_gather(gain_ffn, ("ctx", "fsdp"), axis=0, tiled=True),
        lax.all_gather(w_router, ("ctx", "fsdp"), axis=0, tiled=True),
        lax.all_gather(w_shared_in, ("ctx", "fsdp"), axis=0, tiled=True),
        lax.all_gather(w_shared_down, ("ctx", "fsdp"), axis=0, tiled=True),
    )


def place_rows(values, slot_index, slot_total):
    model_width = values.shape[-1]
    empty_rows = jnp.zeros((slot_total, model_width), values.dtype)
    return empty_rows.at[slot_index].set(values.reshape(-1, model_width))


def scores_of(query_b, key_piece, score_scale, head_count):
    amount = key_piece.shape[0]
    head_size = query_b.shape[2]
    key_heads = key_piece.reshape(amount, head_count, head_size)
    return (
        jnp.einsum("qhd,khd->qhk", query_b, key_heads, preferred_element_type=jnp.float32)
        * score_scale
    )


def local(
    tokens,
    gain_attn,
    w_qkv,
    w_out,
    gain_ffn,
    w_router,
    w_shared_in,
    w_shared_down,
    w_expert_in,
    w_expert_down,
    routes,
    plan,
    cotangent,
):
    head_count = HEADS
    per_device = tokens.shape[1]
    model_width = tokens.shape[2]
    head_size = model_width // head_count
    score_scale = head_size ** (-0.5)
    ctx_count = lax.axis_size("ctx")
    devices = ctx_count * lax.axis_size("fsdp")
    experts = EXPERTS
    capacity = CAP
    top_k = routes.shape[2]
    per_owner = w_expert_in.shape[0]
    slot_total = experts * capacity
    local_rows = tokens[0].astype(jnp.float32)
    own_pos = positions(plan, lax.axis_index("ctx") * per_device, per_device, per_device)
    gain_one, qkv_full, out_full = first_weights(gain_attn, w_qkv, w_out)
    gain_one = gain_one.astype(jnp.float32)
    normed_b = rms_scale(local_rows, gain_one).astype(jnp.bfloat16)
    projected = jnp.dot(normed_b, qkv_full, preferred_element_type=jnp.float32)
    query_b = (
        rotate(projected[:, :model_width], own_pos, head_count)
        .astype(jnp.bfloat16)
        .reshape(per_device, head_count, head_size)
    )
    key_b = rotate(projected[:, model_width : 2 * model_width], own_pos, head_count).astype(
        jnp.bfloat16
    )
    value_b = projected[:, 2 * model_width :].astype(jnp.bfloat16)

    def visible_of(first_row, amount):
        key_pos = positions(plan, first_row, amount, per_device)
        return key_pos[None, None, :] <= own_pos[:, None, None]

    attend_row_top = jnp.full((per_device, head_count), NEGATIVE, jnp.float32)
    key_piece = lax.all_gather(key_b, "ctx", axis=0, tiled=True)
    val_piece = lax.all_gather(value_b, "ctx", axis=0, tiled=True)
    amount = key_piece.shape[0]
    visible = visible_of(jnp.int32(0), amount)
    scores = jnp.where(visible, scores_of(query_b, key_piece, score_scale, head_count), NEGATIVE)
    new_top = jnp.maximum(attend_row_top, jnp.max(scores, axis=2))
    weights_exp = jnp.where(visible, jnp.exp(scores - new_top[..., None]), 0.0)
    row_total = jnp.sum(weights_exp, axis=2)
    val_heads = val_piece.reshape(amount, head_count, head_size)
    accumulated = jnp.einsum(
        "qhk,khd->qhd",
        weights_exp.astype(jnp.bfloat16),
        val_heads,
        preferred_element_type=jnp.float32,
    )
    row_top, row_total, accumulated = (new_top, row_total, accumulated)
    mixed_out = accumulated / row_total[..., None]
    mixed_b = mixed_out.reshape(per_device, model_width).astype(jnp.bfloat16)
    residual = local_rows + jnp.dot(mixed_b, out_full, preferred_element_type=jnp.float32)
    gain_two, router_full, shared_in_full, shared_down_full = second_weights(
        gain_ffn, w_router, w_shared_in, w_shared_down
    )
    gain_two = gain_two.astype(jnp.float32)
    ffn_b = rms_scale(residual, gain_two).astype(jnp.bfloat16)
    logits = jnp.dot(ffn_b, router_full, preferred_element_type=jnp.float32)
    chosen_mask = (
        routes[0][:, :, None] == jnp.arange(experts, dtype=jnp.int32)[None, None, :]
    ).astype(jnp.float32)
    chosen = jnp.sum(chosen_mask * logits[:, None, :], axis=2)
    gate_weights = jax.nn.softmax(chosen, axis=1)
    shared_joined = jnp.dot(ffn_b, shared_in_full, preferred_element_type=jnp.float32)
    shared_hidden = gating(shared_joined).astype(jnp.bfloat16)
    shared_out = jnp.dot(shared_hidden, shared_down_full, preferred_element_type=jnp.float32)
    flat_routes = routes[0].reshape(-1)
    matches = (flat_routes[:, None] == jnp.arange(experts, dtype=jnp.int32)[None, :]).astype(
        jnp.int32
    )
    ranking = jnp.sum((jnp.cumsum(matches, axis=0) - matches) * matches, axis=1)
    slot_index = flat_routes * capacity + ranking
    sent_rows = place_rows(
        jnp.broadcast_to(ffn_b[:, None, :], (per_device, top_k, model_width)),
        slot_index,
        slot_total,
    )
    outgoing = jnp.concatenate([sent_rows, sent_rows], axis=0).reshape(devices, -1, model_width)
    arrived = lax.all_to_all(outgoing, ("ctx", "fsdp"), split_axis=0, concat_axis=0, tiled=True)
    rows_in = arrived.reshape(devices, per_owner, capacity, model_width)
    joined = jnp.einsum("sjcd,jdf->sjcf", rows_in, w_expert_in, preferred_element_type=jnp.float32)
    hidden_b = gating(joined).astype(jnp.bfloat16)
    partial_b = jnp.einsum(
        "sjcf,jfd->sjcd", hidden_b, w_expert_down, preferred_element_type=jnp.float32
    ).astype(jnp.bfloat16)
    going_back = partial_b.reshape(devices, -1, model_width)
    returned = lax.all_to_all(going_back, ("ctx", "fsdp"), split_axis=0, concat_axis=0, tiled=True)
    halves = returned.reshape(2, slot_total, model_width).astype(jnp.float32)
    expert_out = (halves[0] + halves[1]).astype(jnp.bfloat16)
    picked = expert_out[slot_index].reshape(per_device, top_k, model_width).astype(jnp.float32)
    routed = jnp.sum(gate_weights[:, :, None] * picked, axis=1)
    result = (residual + shared_out + routed).astype(jnp.bfloat16)
    gain_two, router_full, shared_in_full, shared_down_full = second_weights(
        gain_ffn, w_router, w_shared_in, w_shared_down
    )
    gain_two = gain_two.astype(jnp.float32)
    dout_b = cotangent[0]
    dout_f = dout_b.astype(jnp.float32)
    dgates = jnp.sum(dout_f[:, None, :] * picked, axis=2)
    dchosen = gate_weights * (dgates - jnp.sum(gate_weights * dgates, axis=1, keepdims=True))
    dlogits_b = jnp.sum(chosen_mask * dchosen[:, :, None], axis=1).astype(jnp.bfloat16)
    grad_rows = place_rows(
        (gate_weights[:, :, None] * dout_f[:, None, :]).astype(jnp.bfloat16), slot_index, slot_total
    )
    grad_out = jnp.concatenate([grad_rows, grad_rows], axis=0).reshape(devices, -1, model_width)
    grad_arrived = lax.all_to_all(
        grad_out, ("ctx", "fsdp"), split_axis=0, concat_axis=0, tiled=True
    )
    dy_rows = grad_arrived.reshape(devices, per_owner, capacity, model_width)
    expert_down_grad = jnp.einsum(
        "sjcf,sjcd->jfd", hidden_b, dy_rows, preferred_element_type=jnp.float32
    )
    d_hidden = jnp.einsum(
        "sjcd,jfd->sjcf", dy_rows, w_expert_down, preferred_element_type=jnp.float32
    )
    d_joined_b = gating_back(joined, d_hidden).astype(jnp.bfloat16)
    expert_in_grad = jnp.einsum(
        "sjcd,sjcf->jdf", rows_in, d_joined_b, preferred_element_type=jnp.float32
    )
    d_rows_b = jnp.einsum(
        "sjcf,jdf->sjcd", d_joined_b, w_expert_in, preferred_element_type=jnp.float32
    ).astype(jnp.bfloat16)
    grad_back = d_rows_b.reshape(devices, -1, model_width)
    grad_home = lax.all_to_all(grad_back, ("ctx", "fsdp"), split_axis=0, concat_axis=0, tiled=True)
    grad_halves = grad_home.reshape(2, slot_total, model_width).astype(jnp.float32)
    d_slots = (grad_halves[0] + grad_halves[1]).astype(jnp.bfloat16)
    d_ffn = jnp.sum(
        d_slots[slot_index].reshape(per_device, top_k, model_width).astype(jnp.float32), axis=1
    )
    shared_down_grad = contract_rows(shared_hidden, dout_b)
    d_shared_hidden = contract_cols(dout_b, shared_down_full)
    d_shared_b = gating_back(shared_joined, d_shared_hidden).astype(jnp.bfloat16)
    shared_in_grad = contract_rows(ffn_b, d_shared_b)
    router_grad = contract_rows(ffn_b, dlogits_b)
    d_ffn = (
        d_ffn + contract_cols(d_shared_b, shared_in_full) + contract_cols(dlogits_b, router_full)
    )
    second_back = jax.vjp(rms_scale, residual, gain_two)[1](d_ffn)
    d_residual = dout_f + second_back[0]
    gain_ffn_grad, router_grad, shared_in_grad, shared_down_grad = (
        lax.psum_scatter(second_back[1], ("ctx", "fsdp"), scatter_dimension=0, tiled=True),
        lax.psum_scatter(router_grad, ("ctx", "fsdp"), scatter_dimension=0, tiled=True),
        lax.psum_scatter(shared_in_grad, ("ctx", "fsdp"), scatter_dimension=0, tiled=True),
        lax.psum_scatter(shared_down_grad, ("ctx", "fsdp"), scatter_dimension=0, tiled=True),
    )
    gain_one, qkv_full, out_full = first_weights(gain_attn, w_qkv, w_out)
    gain_one = gain_one.astype(jnp.float32)
    d_attn_b = d_residual.astype(jnp.bfloat16)
    out_grad = contract_rows(mixed_b, d_attn_b)
    d_mixed = (
        contract_cols(d_attn_b, out_full)
        .astype(jnp.bfloat16)
        .astype(jnp.float32)
        .reshape(per_device, head_count, head_size)
    )
    grad_num = (d_mixed / row_total[..., None]).astype(jnp.bfloat16)
    shift = jnp.sum(d_mixed * mixed_out, axis=2) / row_total
    key_piece = lax.all_gather(key_b, "ctx", axis=0, tiled=True)
    val_piece = lax.all_gather(value_b, "ctx", axis=0, tiled=True)
    amount = key_piece.shape[0]
    visible = visible_of(jnp.int32(0), amount)
    scores = jnp.where(visible, scores_of(query_b, key_piece, score_scale, head_count), NEGATIVE)
    weights_exp = jnp.where(visible, jnp.exp(scores - row_top[..., None]), 0.0)
    val_heads = val_piece.reshape(amount, head_count, head_size)
    key_heads = key_piece.reshape(amount, head_count, head_size)
    d_prob = jnp.einsum("qhd,khd->qhk", grad_num, val_heads, preferred_element_type=jnp.float32)
    d_score = (weights_exp * (d_prob - shift[..., None])).astype(jnp.bfloat16)
    grad_query = jnp.einsum("qhk,khd->qhd", d_score, key_heads, preferred_element_type=jnp.float32)
    part_key = jnp.einsum(
        "qhk,qhd->khd", d_score, query_b, preferred_element_type=jnp.float32
    ).reshape(amount, model_width)
    part_value = jnp.einsum(
        "qhk,qhd->khd",
        weights_exp.astype(jnp.bfloat16),
        grad_num,
        preferred_element_type=jnp.float32,
    ).reshape(amount, model_width)
    grad_key = part_key
    grad_value = part_value
    grad_query, grad_key, grad_value = (grad_query, grad_key, grad_value)
    grad_key, grad_value = (
        lax.psum_scatter(
            grad_key.astype(jnp.bfloat16), "ctx", scatter_dimension=0, tiled=True
        ).astype(jnp.float32),
        lax.psum_scatter(
            grad_value.astype(jnp.bfloat16), "ctx", scatter_dimension=0, tiled=True
        ).astype(jnp.float32),
    )
    d_query = rotate(
        grad_query.reshape(per_device, model_width) * score_scale, -own_pos, head_count
    )
    d_key = rotate(grad_key * score_scale, -own_pos, head_count)
    d_projected = jnp.concatenate([d_query, d_key, grad_value], axis=1).astype(jnp.bfloat16)
    qkv_grad = contract_rows(normed_b, d_projected)
    d_normed = contract_cols(d_projected, qkv_full)
    first_back = jax.vjp(rms_scale, local_rows, gain_one)[1](d_normed)
    tokens_grad = d_residual + first_back[0]
    gain_attn_grad, qkv_grad, out_grad = (
        lax.psum_scatter(first_back[1], ("ctx", "fsdp"), scatter_dimension=0, tiled=True),
        lax.psum_scatter(qkv_grad, ("ctx", "fsdp"), scatter_dimension=0, tiled=True),
        lax.psum_scatter(out_grad, ("ctx", "fsdp"), scatter_dimension=0, tiled=True),
    )
    return (
        result[None],
        tokens_grad[None],
        gain_attn_grad,
        qkv_grad,
        out_grad,
        gain_ffn_grad,
        router_grad,
        shared_in_grad,
        shared_down_grad,
        expert_in_grad,
        expert_down_grad,
    )


def solution(mesh):
    placed = (
        P("fsdp", "ctx", None),
        P(("ctx", "fsdp")),
        P(("ctx", "fsdp"), None),
        P(("ctx", "fsdp"), None),
        P(("ctx", "fsdp")),
        P(("ctx", "fsdp"), None),
        P(("ctx", "fsdp"), None),
        P(("ctx", "fsdp"), None),
        P(("ctx", "fsdp"), None, None),
        P(("ctx", "fsdp"), None, None),
        P("fsdp", "ctx", None),
        P(),
        P("fsdp", "ctx", None),
    )
    return jax.shard_map(
        local,
        mesh=mesh,
        in_specs=placed,
        out_specs=(
            P("fsdp", "ctx", None),
            P("fsdp", "ctx", None),
            P(("ctx", "fsdp")),
            P(("ctx", "fsdp"), None),
            P(("ctx", "fsdp"), None),
            P(("ctx", "fsdp")),
            P(("ctx", "fsdp"), None),
            P(("ctx", "fsdp"), None),
            P(("ctx", "fsdp"), None),
            P(("ctx", "fsdp"), None, None),
            P(("ctx", "fsdp"), None, None),
        ),
        check_vma=False,
    )
```

profile of v0, /device:TPU:0, one launch (start us, length us, event | category | flops | bytes accessed | tf_op | source)
XLA Modules:
  0.0 4284.8 jit_solution(8700315540823761772)
XLA Ops:
  9.7 43.3 %all-reduce.9 = (bf16[2048]{0:T(1024)(128)(2,1)S(1)}, bf16[2048]{0:T(1024)(128)(2,1)S(1)}) all-reduce(bf16[2048]{0:T(1024)(128)(2,1)S(1)} %dynamic-update-slice, bf16[2048]{0:T(1024)(128)(2,1)S(1)} %dynamic-update-slice.1), channel_id=1, replica_groups=mesh['ctx'=8,'fsdp'=4] {'ctx','fsdp'}, use_global_device_ids=true, to_apply=%add.4 | all-reduce | flops 4096 | bytes 16384
  56.7 112.8 %all-gather.7.cloned.1.call-done = bf16[2048,6144]{1,0:T(8,128)(2,1)} async-done(((bf16[64,6144]{1,0:T(8,128)(2,1)}), bf16[2048,6144]{1,0:T(8,128)(2,1)}) %all-gather.7.cloned.1.call-update) | async-done | bytes 25165840 | tf_op jit(solution)/shard_map/all_gather | solution.py:72
  169.5 10.2 fusion.79
  191.4 30.9 all-gather.11.cloned.1.call-done
  232.6 28.9 all-gather.9.cloned.1.call-done
  261.6 8.8 fusion.112
  270.4 71.4 %all-gather.13.cloned.1.call-done = bf16[2048,2048]{1,0:T(8,128)(2,1)} async-done(((bf16[64,2048]{1,0:T(8,128)(2,1)}), bf16[2048,2048]{1,0:T(8,128)(2,1)}) %all-gather.13.cloned.1.call-update) | async-done | bytes 8388624 | tf_op jit(solution)/shard_map/all_gather | solution.py:73
  356.7 11.3 scatter_custom_fusion
  368.0 12.6 pad_maximum_fusion
  390.1 8.3 mul.511
  398.3 282.1 %all_gather.44 = bf16[2048,64]{1,0:T(8,128)(2,1)S(1)} all-gather(bf16[64,64]{1,0:T(8,128)(2,1)S(1)} %copy-done.53), channel_id=1, replica_groups=mesh['ctx'=8,'fsdp'=4] {'ctx','fsdp'}, dimensions={0}, use_global_device_ids=true | all-gather | bytes 270336 | tf_op jit(solution)/shard_map/all_gather | solution.py:80
  682.7 15.6 scatter_custom_fusion.1
  698.3 12.6 pad_maximum_fusion.1
  715.3 14.0 copy.169
  729.3 315.9 %all-to-all-done.2 = bf16[32,80,2048]{2,1,0:T(8,128)(2,1)} async-done(((bf16[32,80,2048]{2,1,0:T(8,128)(2,1)}), bf16[32,80,2048]{2,1,0:T(8,128)(2,1)}, u32[]{:S(2)}, u32[]{:S(2)}) %all-to-all-start.2) | async-done | bytes 10485792 | tf_op jit(solution)/shard_map/all_to_all | solution.py:222
  1045.2 14.1 copy.172
  1059.2 25.0 fusion.15
  1084.3 25.9 bitcast_multiply_fusion.1
  1110.1 15.1 fusion.19
  1125.2 13.7 copy.170
  1138.9 11.3 all-to-all-start.1
  1150.7 26.7 fusion.22
  1177.4 13.7 copy.173
  1191.1 237.0 %all-to-all-done.1 = bf16[32,80,2048]{2,1,0:T(8,128)(2,1)} async-done(((bf16[32,80,2048]{2,1,0:T(8,128)(2,1)}), bf16[32,80,2048]{2,1,0:T(8,128)(2,1)}, u32[]{:S(2)}, u32[]{:S(2)}) %all-to-all-start.1) | async-done | bytes 10485792 | tf_op jit(solution)/shard_map/all_to_all | solution.py:203
  1428.1 10.4 all-to-all-start.3
  1438.8 12.4 fusion.113
  1451.2 10.6 fusion.77
  1461.8 14.7 convert_element_type.193
  1476.5 11.2 fusion.9
  1487.8 10.7 gather_fusion
  1512.3 152.3 %all-to-all-done.3 = bf16[32,80,2048]{2,1,0:T(8,128)(2,1)} async-done(((bf16[32,80,2048]{2,1,0:T(8,128)(2,1)}), bf16[32,80,2048]{2,1,0:T(8,128)(2,1)}, u32[]{:S(2)}, u32[]{:S(2)}) %all-to-all-start.3) | async-done | bytes 10485792 | tf_op jit(solution)/shard_map/all_to_all | solution.py:240
  1664.7 14.2 convert_element_type.204
  1678.9 11.2 fusion.8
  1690.0 10.3 gather_fusion.1
  1714.2 13.3 convolution_add_fusion.1
  1739.8 8.4 convolution_convert_fusion
  1778.7 9.8 fusion.65
  1799.2 19.3 fusion.72
  1825.7 41.0 reduce-scatter.22.cloned.1.call-done
  1868.5 20.8 fusion.63
  1889.3 17.5 convolution_bitcast_fusion.1
  1906.9 35.7 convolution_bitcast_fusion
  1949.5 13.8 fusion.54
  1963.3 39.6 all-reduce.8
  2005.4 493.5 %reduce-scatter.20.cloned.1.call-done = f32[88,2048]{1,0:T(8,128)} async-done(((f32[2816,2048]{1,0:T(8,128)}), f32[88,2048]{1,0:T(8,128)}) %reduce-scatter.20.cloned.1.call-update) | async-done | bytes 720912 | tf_op jit(solution)/shard_map/reduce_scatter | solution.py:260
  2498.9 365.9 %reduce-scatter.14.cloned.1.call-done = f32[64,2048]{1,0:T(8,128)} async-done(((f32[2048,2048]{1,0:T(8,128)}), f32[64,2048]{1,0:T(8,128)}) %reduce-scatter.14.cloned.1.call-update) | async-done | bytes 524304 | tf_op jit(solution)/shard_map/reduce_scatter | solution.py:317
  2864.8 973.2 %reduce-scatter.18.cloned.1.call-done = f32[64,5632]{1,0:T(8,128)} async-done(((f32[2048,5632]{1,0:T(8,128)}), f32[64,5632]{1,0:T(8,128)}) %reduce-scatter.18.cloned.1.call-update) | async-done | bytes 1441808 | tf_op jit(solution)/shard_map/reduce_scatter | solution.py:259
  3838.0 440.1 %reduce-scatter.12.cloned.1.call-done = f32[64,6144]{1,0:T(8,128)} async-done(((f32[2048,6144]{1,0:T(8,128)}), f32[64,6144]{1,0:T(8,128)}) %reduce-scatter.12.cloned.1.call-update) | async-done | bytes 1572880 | tf_op jit(solution)/shard_map/reduce_scatter | solution.py:316
  (255 shorter events, 158.6 us)
Async XLA Ops:
  7.2 162.3 %all-gather.7.cloned.1.call-start = ((), (), s32[]{:S(2)}) async-start(), calls=%async_computation.11 | async-start | bytes 25952256 | tf_op jit(solution)/shard_map/all_gather | solution.py:72
  7.9 214.4 %all-gather.11.cloned.1.call-start = ((), (), s32[]{:S(2)}) async-start(), calls=%async_computation.13 | async-start | bytes 4718592 | tf_op jit(solution)/shard_map/all_gather | solution.py:150
  53.0 126.8 %copy-start.33 = (f32[2048]{0:T(1024)}, f32[2048]{0:T(1024)S(1)}, u32[]{:S(2)}) copy-start(f32[2048]{0:T(1024)S(1)} %convert_element_type.178) | copy-start | bytes 24580
  56.7 123.1 %copy-start.50 = (f32[128]{0:T(128)}, f32[128]{0:T(128)S(1)}, u32[]{:S(2)}) copy-start(f32[128]{0:T(128)S(1)} %fusion.97) | copy-start | bytes 1540
  186.6 75.0 %all-gather.9.cloned.1.call-start = ((), (), s32[]{:S(2)}) async-start(), calls=%async_computation.12 | async-start | bytes 4718592 | tf_op jit(solution)/shard_map/all_gather | solution.py:151
  187.5 154.3 %all-gather.13.cloned.1.call-start = ((), (), s32[]{:S(2)}) async-start(), calls=%async_computation.14 | async-start | bytes 8650752 | tf_op jit(solution)/shard_map/all_gather | solution.py:73
  190.9 155.7 %copy-start.39 = (f32[2048]{0:T(1024)}, f32[2048]{0:T(1024)S(1)}, u32[]{:S(2)}) copy-start(f32[2048]{0:T(1024)S(1)} %convert_element_type.185) | copy-start | bytes 24580
  191.1 491.6 %copy-start.54 = (s32[768]{0:T(1024)}, s32[768]{0:T(1024)S(1)}, u32[]{:S(2)}) copy-start(s32[768]{0:T(1024)S(1)} %fusion.95) | copy-start | bytes 9220
  191.4 70.1 %copy-start.30 = (pred[128,1024]{0,1:T(8,128)(4,1)}, pred[128,1024]{0,1:T(8,128)(4,1)S(1)}, u32[]{:S(2)}) copy-start(pred[128,1024]{0,1:T(8,128)(4,1)S(1)} %broadcast_compare_fusion) | copy-start | bytes 393220
  227.2 43.2 %copy-start.47 = (f32[128,16]{0,1:T(8,128)}, f32[128,16]{0,1:T(8,128)S(1)}, u32[]{:S(2)}) copy-start(f32[128,16]{0,1:T(8,128)S(1)} %broadcast_maximum_fusion) | copy-start | bytes 24580
  232.6 37.8 copy-start.45
  232.6 109.2 %copy-start.9 = (bf16[1,128,2048]{2,1,0:T(8,128)(2,1)S(1)}, bf16[1,128,2048]{2,1,0:T(8,128)(2,1)}, u32[]{:S(2)}) copy-start(bf16[1,128,2048]{2,1,0:T(8,128)(2,1)} %param.13) | copy-start | bytes 1572868
  270.4 76.1 %copy-start.23 = (bf16[128,16,128]{0,2,1:T(8,128)(2,1)}, bf16[128,16,128]{0,2,1:T(8,128)(2,1)S(1)}, u32[]{:S(2)}) copy-start(bf16[128,16,128]{0,2,1:T(8,128)(2,1)S(1)} %get-tuple-element.55) | copy-start | bytes 1572868
  346.5 21.5 copy-start.61
  346.6 21.5 copy-start.60
  347.7 332.8 %copy-start.4 = (bf16[128,2048]{1,0:T(8,128)(2,1)}, bf16[128,2048]{1,0:T(8,128)(2,1)S(1)}, u32[]{:S(2)}) copy-start(bf16[128,2048]{1,0:T(8,128)(2,1)S(1)} %multiply_convert_fusion.4) | copy-start | bytes 1572868
  380.6 330.3 %all-to-all-start = ((bf16[32,80,2048]{2,1,0:T(8,128)(2,1)}), bf16[32,80,2048]{2,1,0:T(8,128)(2,1)}, u32[]{:S(2)}, u32[]{:S(2)}) async-start(bf16[32,80,2048]{2,1,0:T(8,128)(2,1)} %bitcast.196), calls=%async_computation | async-start | bytes 20971520 | tf_op jit(solution)/shard_map/all_to_all | solution.py:195
  384.5 296.8 %copy-start.42 = (s32[1,128,6]{1,2,0:T(8,128)}, s32[1,128,6]{1,2,0:T(8,128)S(1)}, u32[]{:S(2)}) copy-start(s32[1,128,6]{1,2,0:T(8,128)S(1)} %copy.233) | copy-start | bytes 9220
  682.5 28.4 copy-start.32
  710.9 334.2 %all-to-all-start.2 = ((bf16[32,80,2048]{2,1,0:T(8,128)(2,1)}), bf16[32,80,2048]{2,1,0:T(8,128)(2,1)}, u32[]{:S(2)}, u32[]{:S(2)}) async-start(bf16[32,80,2048]{2,1,0:T(8,128)(2,1)} %bitcast.197), calls=%async_computation.2 | async-start | bytes 20971520 | tf_op jit(solution)/shard_map/all_to_all | solution.py:222
  714.7 724.1 %all-gather.15.cloned.1.call-start = ((), (), s32[]{:S(2)}) async-start(), calls=%async_computation.15 | async-start | bytes 23789568 | tf_op jit(solution)/shard_map/all_gather | solution.py:81
  1138.9 289.2 %all-to-all-start.1 = ((bf16[32,80,2048]{2,1,0:T(8,128)(2,1)}), bf16[32,80,2048]{2,1,0:T(8,128)(2,1)}, u32[]{:S(2)}, u32[]{:S(2)}) async-start(bf16[32,80,2048]{2,1,0:T(8,128)(2,1)} %copy.170), calls=%async_computation.1 | async-start | bytes 20971520 | tf_op jit(solution)/shard_map/all_to_all | solution.py:203
  1150.1 301.0 %all-gather.17.cloned.1.call-start = ((), (), s32[]{:S(2)}) async-start(), calls=%async_computation.16 | async-start | bytes 11894784 | tf_op jit(solution)/shard_map/all_gather | solution.py:82
  1191.1 247.6 %copy-start.55 = (s32[768]{0:T(1024)S(1)}, s32[768]{0:T(1024)}, u32[]{:S(2)}) copy-start(s32[768]{0:T(1024)} %copy-done.54) | copy-start | bytes 9220
  1191.1 247.7 %copy-start.5 = (bf16[128,2048]{1,0:T(8,128)(2,1)S(1)}, bf16[128,2048]{1,0:T(8,128)(2,1)}, u32[]{:S(2)}) copy-start(bf16[128,2048]{1,0:T(8,128)(2,1)} %copy-done.4) | copy-start | bytes 1572868
  1428.1 236.6 %all-to-all-start.3 = ((bf16[32,80,2048]{2,1,0:T(8,128)(2,1)}), bf16[32,80,2048]{2,1,0:T(8,128)(2,1)}, u32[]{:S(2)}, u32[]{:S(2)}) async-start(bf16[32,80,2048]{2,1,0:T(8,128)(2,1)} %copy.173), calls=%async_computation.3 | async-start | bytes 20971520 | tf_op jit(solution)/shard_map/all_to_all | solution.py:240
  1438.5 385.8 %reduce-scatter.24.cloned.1.call-start = ((), (), s32[]{:S(2)}) async-start(), calls=%async_computation.23 | async-start | bytes 4718592
  1461.8 252.4 %copy-start.14 = (f32[128,2816]{1,0:T(8,128)}, f32[128,2816]{1,0:T(8,128)S(1)}, u32[]{:S(2)}) copy-start(f32[128,2816]{1,0:T(8,128)S(1)} %get-tuple-element.26) | copy-start | bytes 4325380
  1731.8 56.8 %copy-start.7 = (f32[128,2048]{1,0:T(8,128)}, f32[128,2048]{1,0:T(8,128)S(1)}, u32[]{:S(2)}) copy-start(f32[128,2048]{1,0:T(8,128)S(1)} %fusion.55) | copy-start | bytes 3145732
  1754.9 111.8 %reduce-scatter.22.cloned.1.call-start = ((), (), s32[]{:S(2)}) async-start(), calls=%async_computation.22 | async-start | bytes 4718592
  1777.2 228.1 %reduce-scatter.16.cloned.1.call-start = ((), (), s32[]{:S(2)}) async-start(), calls=%async_computation.19 | async-start | bytes 1081344 | tf_op jit(solution)/shard_map/reduce_scatter | solution.py:258
  1778.7 720.2 %reduce-scatter.20.cloned.1.call-start = ((), (), s32[]{:S(2)}) async-start(), calls=%async_computation.21 | async-start | bytes 23789568 | tf_op jit(solution)/shard_map/reduce_scatter | solution.py:260
  1788.6 1076.2 %reduce-scatter.14.cloned.1.call-start = ((), (), s32[]{:S(2)}) async-start(), calls=%async_computation.18 | async-start | bytes 17301504 | tf_op jit(solution)/shard_map/reduce_scatter | solution.py:317
  1797.9 2040.1 %reduce-scatter.18.cloned.1.call-start = ((), (), s32[]{:S(2)}) async-start(), calls=%async_computation.20 | async-start | bytes 47579136 | tf_op jit(solution)/shard_map/reduce_scatter | solution.py:259
  1818.6 49.5 %copy-start.40 = (f32[128,64]{0,1:T(8,128)S(1)}, f32[128,64]{0,1:T(8,128)}, u32[]{:S(2)}) copy-start(f32[128,64]{0,1:T(8,128)} %get-tuple-element.47) | copy-start | bytes 98308
  1818.6 49.5 %copy-start.41 = (f32[128,64]{0,1:T(8,128)S(1)}, f32[128,64]{0,1:T(8,128)}, u32[]{:S(2)}) copy-start(f32[128,64]{0,1:T(8,128)} %get-tuple-element.48) | copy-start | bytes 98308
  1818.6 49.9 %copy-start.10 = (bf16[1,128,2048]{2,1,0:T(8,128)(2,1)S(1)}, bf16[1,128,2048]{2,1,0:T(8,128)(2,1)}, u32[]{:S(2)}) copy-start(bf16[1,128,2048]{2,1,0:T(8,128)(2,1)} %param.13) | copy-start | bytes 1572868
  1818.6 49.9 %copy-start.34 = (f32[2048]{0:T(1024)S(1)}, f32[2048]{0:T(1024)}, u32[]{:S(2)}) copy-start(f32[2048]{0:T(1024)} %copy-done.33) | copy-start | bytes 24580
  1818.6 49.9 %copy-start.51 = (f32[128]{0:T(128)S(1)}, f32[128]{0:T(128)}, u32[]{:S(2)}) copy-start(f32[128]{0:T(128)} %copy-done.50) | copy-start | bytes 1540
  1818.6 2459.5 %reduce-scatter.12.cloned.1.call-start = ((), (), s32[]{:S(2)}) async-start(), calls=%async_computation.17 | async-start | bytes 51904512 | tf_op jit(solution)/shard_map/reduce_scatter | solution.py:316
  1825.7 63.6 %copy-start.27 = (bf16[128,2048]{0,1:T(8,128)(2,1)}, bf16[128,2048]{0,1:T(8,128)(2,1)S(1)}, u32[]{:S(2)}) copy-start(bf16[128,2048]{0,1:T(8,128)(2,1)S(1)} %copy.197) | copy-start | bytes 1572868
  1868.4 20.9 copy-start.28
  1868.5 20.8 copy-start.29
  1906.9 35.7 copy-start.3
  1906.9 35.7 copy-start.22
  1906.9 35.7 copy-start.26
  1949.5 54.6 %copy-start.63 = (f32[128]{0:T(128)S(1)}, f32[128]{0:T(128)}, u32[]{:S(2)}) copy-start(f32[128]{0:T(128)} %copy-done.62) | copy-start | bytes 1540
  1949.5 54.6 %copy-start.8 = (f32[128,2048]{1,0:T(8,128)S(1)}, f32[128,2048]{1,0:T(8,128)}, u32[]{:S(2)}) copy-start(f32[128,2048]{1,0:T(8,128)} %copy-done.7) | copy-start | bytes 3145732
  (34 other events, 205.4 us)
Sparse Core Ops, SparseCore 0:
  10.9 158.5 all-gather.6
  186.7 35.5 all-gather.10
  224.8 36.7 all-gather.8
  264.3 77.3 all-gather.12
  718.0 299.0 all-gather.14
  1153.5 222.8 all-gather.16
  1755.0 56.4 reduce-scatter.23
  1815.2 51.3 reduce-scatter.21
  1869.5 135.3 reduce-scatter.15
  2007.7 491.1 reduce-scatter.19
  2501.9 362.8 reduce-scatter.13
  2867.6 970.2 reduce-scatter.17
  3846.1 431.9 reduce-scatter.11
where the time goes:
time: 4290 us; the launch traced here: 4280 us
  waiting for transfers between devices  3270 us (76%)
  blocking collectives  365 us (9%)
  matrix products  326 us (8%)
  local copies, waits for them, and re-layouts  160 us (4%)
  other arithmetic  122 us (3%)
    reduce_scatter x1, waiting for transfers between devices, local(): lax.psum_scatter(shared_in_grad, ('ctx', 'fsdp'), scatter_dimension=0, ti...  973 us
    reduce_scatter x1, waiting for transfers between devices, local(): lax.psum_scatter(shared_down_grad, ('ctx', 'fsdp'), scatter_dimension=0,...  494 us
    reduce_scatter x1, waiting for transfers between devices, local(): lax.psum_scatter(qkv_grad, ('ctx', 'fsdp'), scatter_dimension=0, tiled=True)  440 us
    reduce_scatter x1, waiting for transfers between devices, local(): lax.psum_scatter(out_grad, ('ctx', 'fsdp'), scatter_dimension=0, tiled=True)  366 us
    all_to_all x1, waiting for transfers between devices, local(): lax.all_to_all(grad_out, ('ctx', 'fsdp'), split_axis=0, concat_axis=0, ti...  316 us
    all_gather x1, blocking collectives, second_weights(): lax.all_gather(w_router, ('ctx', 'fsdp'), axis=0, tiled=True)  282 us
    all_to_all x1, waiting for transfers between devices, local(): lax.all_to_all(going_back, ('ctx', 'fsdp'), split_axis=0, concat_axis=0,...  237 us
    all_to_all x1, waiting for transfers between devices, local(): lax.all_to_all(grad_back, ('ctx', 'fsdp'), split_axis=0, concat_axis=0, t...  152 us
  transfers between devices with their start and end apart: 17, of which 12 were waited for; matrix products, arithmetic and copies ran while one was open for 11% of the time, Pallas kernels for 0%

commit v1 on v0

v1 whole, which is shorter than its diff:
```python
import functools

import jax
import jax.numpy as jnp
from jax import lax
from jax.experimental import pallas as pl
from jax.experimental.pallas import tpu as pltpu
from jax.sharding import PartitionSpec as P

HEADS = 16
EXPERTS = 64
CAP = 20
BLOCK = 128
GROUP = 4
VMEM = 60 * 1024 * 1024

EPSILON = 1e-06
ROPE_BASE = 10000.0
NEGATIVE = -1e30
BOTH = ("ctx", "fsdp")


def rms_scale(values, gain):
    inverse = lax.rsqrt(jnp.mean(values * values, axis=-1, keepdims=True) + EPSILON)
    return values * inverse * gain


def rotate(values, places, head_count):
    amount, width = values.shape
    head_size = width // head_count
    half_size = head_size // 2
    frequency = ROPE_BASE ** (-2.0 * jnp.arange(half_size, dtype=jnp.float32) / head_size)
    angles = places.astype(jnp.float32)[:, None] * frequency[None, :]
    cosine = jnp.cos(angles)
    sine = jnp.sin(angles)
    turned = []
    for head in range(head_count):
        first = values[:, head * head_size : head * head_size + half_size]
        second = values[:, head * head_size + half_size : (head + 1) * head_size]
        turned += [first * cosine - second * sine, second * cosine + first * sine]
    return jnp.concatenate(turned, axis=-1)


def dot(left, right):
    return jnp.dot(left, right, preferred_element_type=jnp.float32)


def contract_rows(left, right):
    return lax.dot_general(
        left, right, (((0,), (0,)), ((), ())), preferred_element_type=jnp.float32
    )


def contract_cols(left, right):
    return lax.dot_general(
        left, right, (((1,), (1,)), ((), ())), preferred_element_type=jnp.float32
    )


def plane_order():
    count = lax.axis_size("ctx")
    return list(range(0, count, 2)) + list(range(1, count, 2))


def ctx_bits():
    count = lax.axis_size("ctx")
    return [1 << i for i in range(1, count.bit_length() - 1)]


def swap(values, bit):
    count = lax.axis_size("ctx")
    return lax.ppermute(values, "ctx", [(i, i ^ bit) for i in range(count)])


def turn(values):
    count = lax.axis_size("fsdp")
    return lax.ppermute(values, "fsdp", [(i, (i + 1) % count) for i in range(count)])


def ring(block):
    held = [block]
    for _ in range(lax.axis_size("fsdp") - 1):
        held.append(turn(held[-1]))
    return held


def ring_sum(pieces):
    if len(pieces) == 1:
        return pieces[0]
    total = pieces[1]
    for piece in pieces[2:]:
        total = add(piece, turn(total))
    return add(pieces[0], turn(total))


def gather_small(block):
    held = jnp.stack(ring(block))[:, None]
    for bit in ctx_bits() + [1]:
        held = jnp.concatenate([held, swap(held, bit)], axis=1)
    return held


def gather_plane(block):
    bits = ctx_bits()
    half = block.shape[0] // 2
    if len(bits) == 2:
        x_bit, y_bit = bits
        over_x = swap(block, x_bit)
        over_y = swap(block, y_bit)
        corner_a = swap(over_x[:half], y_bit)
        corner_b = swap(over_y[half:], x_bit)
        near = jnp.concatenate([block, over_x, over_y, corner_a, corner_b], axis=0)
    else:
        near = block
        for bit in bits:
            near = jnp.concatenate([near, swap(near, bit)], axis=0)
    return near, swap(near, 1)


def add(left, right):
    return (left.astype(jnp.float32) + right.astype(jnp.float32)).astype(left.dtype)


def scatter_plane(near, far):
    bits = ctx_bits()
    near_too = swap(far, 1)
    size = near.shape[0] >> len(bits)
    if len(bits) == 2:
        x_bit, y_bit = bits
        half = size // 2
        own, part_x, part_y, corner = (
            add(near[i * size : (i + 1) * size], near_too[i * size : (i + 1) * size])
            for i in range(4)
        )
        for_y, for_x = swap(corner[:half], x_bit), swap(corner[half:], y_bit)
        back_x = swap(jnp.concatenate([part_x[:half], add(part_x[half:], for_x)], axis=0), x_bit)
        back_y = swap(jnp.concatenate([add(part_y[:half], for_y), part_y[half:]], axis=0), y_bit)
        return add(add(own, back_x), back_y)
    held = add(near, near_too)
    for bit in reversed(bits):
        middle = held.shape[0] // 2
        held = add(held[:middle], swap(held[middle:], bit))
    return held


def by_plane(pieces, axis):
    count, me = lax.axis_size("fsdp"), lax.axis_index("fsdp")
    shape = list(pieces[0].shape)
    shape.insert(axis, count)
    whole = jnp.zeros(shape, pieces[0].dtype)
    for k, piece in enumerate(pieces):
        place = lax.rem(me - k + count, count)
        whole = lax.dynamic_update_slice_in_dim(whole, jnp.expand_dims(piece, axis), place, axis)
    return whole


def from_plane(whole, axis):
    count, me = lax.axis_size("fsdp"), lax.axis_index("fsdp")
    return [
        jnp.squeeze(
            lax.dynamic_slice_in_dim(whole, lax.rem(me - k + count, count), 1, axis), axis
        )
        for k in range(count)
    ]


def gate_parts(first, second):
    sigmoid = 1.0 / (1.0 + jnp.exp(-first))
    return sigmoid, first * sigmoid * second


def gate_back(first, second, sigmoid, upstream):
    silu = first * sigmoid
    return upstream * second * (sigmoid + silu * (1.0 - sigmoid)), upstream * silu


def pick(slot_ref, owner, span):
    tokens = GROUP * BLOCK
    slots = slot_ref[pl.ds(owner, 1), span * tokens : (span + 1) * tokens]
    ids = lax.broadcasted_iota(jnp.int32, (GROUP * CAP, tokens), 0).astype(jnp.float32)
    return ids == slots


def pick_all(slot_ref, span):
    chosen = [pick(slot_ref, owner, span).astype(jnp.bfloat16) for owner in range(slot_ref.shape[0])]
    return jnp.concatenate(chosen, axis=0)


def spans_of(first_ref, second_ref):
    tokens = GROUP * BLOCK
    per_side = first_ref.shape[0] // tokens
    return [
        (ref, slice(n * tokens, (n + 1) * tokens))
        for ref in (first_ref, second_ref)
        for n in range(per_side)
    ]


def slots_at(span):
    return slice(span * GROUP * CAP, (span + 1) * GROUP * CAP)


def tokens_at(span):
    return slice(span * GROUP * BLOCK, (span + 1) * GROUP * BLOCK)


def early_kernel(*refs, carried):
    ga_ref, gb_ref, slot_ref, down_ref, s_down_ref = refs[:5]
    rows_ref, dh_ref, dhs_ref, kept_ref = refs[5 + carried :]
    owners = slot_ref.shape[0]
    step = pl.program_id(0)

    @pl.when(step == 0)
    def _():
        for span, (ref, at) in enumerate(spans_of(ga_ref, gb_ref)):
            values = ref[at, :]
            taken = dot(pick_all(slot_ref, span), values).astype(jnp.bfloat16)
            for owner in range(owners):
                kept_ref[owner, slots_at(span), :] = taken[slots_at(owner)]
            dhs_ref[tokens_at(span), :] = contract_cols(values, s_down_ref[...])

    rows = kept_ref[step]
    rows_ref[0] = rows
    dh_ref[0] = contract_cols(rows, down_ref[0])


def middle_kernel(*refs, carried):
    (first_ref, xa_ref, xb_ref, router_ref, mask_ref, slot_ref, in_ref, s_in_ref, dh_ref, dhs_ref) = refs[:10]
    (rows_ref, hidden_ref, dj_ref, da_ref, db_ref, gates_ref, sh_ref, ds_ref, r_ref, z_ref, gate_ref) = refs[10 + carried :]
    bf16 = jnp.bfloat16
    owners = slot_ref.shape[0]
    step = pl.program_id(0)
    spans = spans_of(xa_ref, xb_ref)

    @pl.when(step == 0)
    def _():
        for span, (ref, at) in enumerate(spans):
            x = ref[at, :]
            lanes = tokens_at(span)
            mask = mask_ref[:, lanes] > 0
            logits = jnp.where(mask, contract_cols(router_ref[...], x), NEGATIVE)
            gates = jnp.where(mask, jnp.exp(logits - jnp.max(logits, axis=0, keepdims=True)), 0.0)
            gates = gates / jnp.sum(gates, axis=0, keepdims=True)
            gates_ref[:, lanes] = gates
            expert = lax.broadcasted_iota(jnp.int32, gates.shape, 0)
            for owner in range(owners):
                own = jnp.sum(jnp.where(expert == first_ref[0] + owner, gates, 0.0), axis=0, keepdims=True)
                gate_ref[owner, slots_at(span), :] = jnp.sum(
                    jnp.where(pick(slot_ref, owner, span), own, 0.0), axis=1, keepdims=True
                )
            taken = dot(pick_all(slot_ref, span), x).astype(bf16)
            for owner in range(owners):
                r_ref[owner, slots_at(span), :] = taken[slots_at(owner)]
            joined = dot(x, s_in_ref[...])
            units = joined.shape[1] // 2
            first, second = joined[:, :units], joined[:, units:]
            sigmoid, hidden = gate_parts(first, second)
            sh_ref[lanes, :] = hidden.astype(bf16)
            back = gate_back(first, second, sigmoid, dhs_ref[lanes, :])
            ds_ref[lanes, :] = jnp.concatenate(back, axis=1).astype(bf16)

    rows = r_ref[step]
    joined = dot(rows, in_ref[0])
    units = joined.shape[1] // 2
    first, second = joined[:, :units], joined[:, units:]
    sigmoid, hidden = gate_parts(first, second)
    back = gate_back(first, second, sigmoid, gate_ref[step] * dh_ref[0])
    d_joined = jnp.concatenate(back, axis=1).astype(bf16)
    z_ref[step] = contract_cols(d_joined, in_ref[0]).astype(bf16)
    rows_ref[0] = rows
    hidden_ref[0] = hidden.astype(bf16)
    dj_ref[0] = d_joined

    @pl.when(step == owners - 1)
    def _():
        for span, (ref, at) in enumerate(spans_of(da_ref, db_ref)):
            made = jnp.concatenate([z_ref[owner, slots_at(span), :] for owner in range(owners)], axis=0)
            total = contract_rows(pick_all(slot_ref, span), made)
            total = total + contract_cols(ds_ref[tokens_at(span), :], s_in_ref[...])
            ref[at, :] = total.astype(bf16)


def late_kernel(*refs, carried):
    (first_ref, hidden_ref, rows_ref, slot_ref, gates_ref, sh_ref, down_ref, s_down_ref) = refs[:8]
    (oa_ref, ob_ref, dgate_ref, dy_ref, y_ref) = refs[8 + carried :]
    bf16 = jnp.bfloat16
    owners = slot_ref.shape[0]
    step = pl.program_id(0)
    spans = spans_of(oa_ref, ob_ref)
    partial = dot(hidden_ref[0], down_ref[0])
    rows = rows_ref[0].astype(jnp.float32)
    d_gate = jnp.sum(rows * partial, axis=1, keepdims=True)
    gates = []
    for span in range(len(spans)):
        chosen = pick(slot_ref, step, span)
        lanes = tokens_at(span)
        own = gates_ref[pl.ds(first_ref[0] + step, 1), lanes]
        gates.append(jnp.sum(jnp.where(chosen, own, 0.0), axis=1, keepdims=True))
        dgate_ref[pl.ds(step, 1), lanes] = jnp.sum(
            jnp.where(chosen, d_gate[slots_at(span)], 0.0), axis=0, keepdims=True
        )
    gate = jnp.concatenate(gates, axis=0)
    y_ref[step] = (gate * partial).astype(bf16)
    dy_ref[0] = (gate * rows).astype(bf16)

    @pl.when(step == owners - 1)
    def _():
        for span, (ref, at) in enumerate(spans):
            made = jnp.concatenate([y_ref[owner, slots_at(span), :] for owner in range(owners)], axis=0)
            total = contract_rows(pick_all(slot_ref, span), made)
            total = total + dot(sh_ref[tokens_at(span), :], s_down_ref[...])
            ref[at, :] = total.astype(bf16)


def held_whole(*shape):
    return pl.BlockSpec(shape, lambda j: (0,) * len(shape), pipeline_mode=pl.Buffered(1))


def expert_call(kernel, owners, operands, specs, outs, out_specs, kept, scratch, flops, moved):
    return pl.pallas_call(
        functools.partial(kernel, carried=len(kept)),
        grid=(owners,),
        in_specs=specs + [pl.BlockSpec(memory_space=pl.ANY)] * len(kept),
        out_specs=out_specs,
        out_shape=[jax.ShapeDtypeStruct(shape, kind) for shape, kind in outs],
        scratch_shapes=scratch,
        input_output_aliases={len(operands) + i: i for i in range(len(kept))},
        compiler_params=pltpu.CompilerParams(vmem_limit_bytes=VMEM),
        cost_estimate=pl.CostEstimate(flops=flops, bytes_accessed=moved, transcendentals=0),
    )(*operands, *kept)


def growing(k, rows, columns):
    return pl.BlockSpec((1, rows, columns), lambda j: (j, k, 0))


def weights_of(array):
    depth = 2 if array.shape[0] > 1 else 1
    return pl.BlockSpec(
        (1,) + array.shape[1:], lambda j: (j, 0, 0), pipeline_mode=pl.Buffered(depth)
    )


def early(k, planes, grads, slots, w_down, s_down, kept):
    bf16, f32 = jnp.bfloat16, jnp.float32
    owners, units, width = w_down.shape
    half = grads[0].shape[0]
    rows, lane = 2 * half // BLOCK * CAP, s_down.shape[0]
    outs = [
        ((owners, planes * rows, width), bf16),
        ((owners, planes * rows, units), f32),
        ((2 * half, lane), f32),
    ]
    taken, dh, dhs = expert_call(
        early_kernel,
        owners,
        [*grads, slots, w_down, s_down],
        [held_whole(half, width)] * 2
        + [held_whole(*slots.shape), weights_of(w_down), held_whole(*s_down.shape)],
        outs,
        [growing(k, rows, width), growing(k, rows, units), held_whole(2 * half, lane)],
        kept,
        [pltpu.VMEM((owners, rows, width), bf16)],
        2 * owners * rows * width * (units + GROUP * BLOCK) + 4 * half * width * lane,
        2 * owners * width * (units + 2 * rows) + 4 * half * width,
    )
    return [taken, dh], dhs


def middle(k, planes, first, rows_x, router_t, mask, slots, w_in, s_in, dh, dhs, kept):
    bf16, f32 = jnp.bfloat16, jnp.float32
    owners, width, joined = w_in.shape
    half = rows_x[0].shape[0]
    rows, lane = 2 * half // BLOCK * CAP, dhs.shape[1]
    outs = [
        ((owners, planes * rows, width), bf16),
        ((owners, planes * rows, joined // 2), bf16),
        ((owners, planes * rows, joined), bf16),
        ((half, width), bf16),
        ((half, width), bf16),
        ((EXPERTS, 2 * half), f32),
        ((2 * half, lane), bf16),
        ((2 * half, 2 * lane), bf16),
    ]
    made = expert_call(
        middle_kernel,
        owners,
        [first, *rows_x, router_t, mask, slots, w_in, s_in, dh, dhs],
        [pl.BlockSpec(memory_space=pltpu.SMEM)]
        + [held_whole(half, width)] * 2
        + [held_whole(*a.shape) for a in (router_t, mask, slots)]
        + [weights_of(w_in), held_whole(*s_in.shape), growing(k, rows, joined // 2)]
        + [held_whole(*dhs.shape)],
        outs,
        [growing(k, rows, width), growing(k, rows, joined // 2), growing(k, rows, joined)]
        + [held_whole(*shape) for shape, _ in outs[3:]],
        kept,
        [
            pltpu.VMEM((owners, rows, width), bf16),
            pltpu.VMEM((owners, rows, width), bf16),
            pltpu.VMEM((owners, rows, 1), f32),
        ],
        4 * owners * rows * width * (joined + GROUP * BLOCK) + 16 * half * width * lane,
        2 * owners * width * (joined + 2 * rows) + 8 * half * width,
    )
    return list(made[:3]), made[3:5], made[5], made[6], made[7]


def late(k, planes, first, hidden, taken, slots, gates, shared, w_down, s_down, kept):
    bf16, f32 = jnp.bfloat16, jnp.float32
    owners, units, width = w_down.shape
    half = shared.shape[0] // 2
    rows = 2 * half // BLOCK * CAP
    outs = [
        ((half, width), bf16),
        ((half, width), bf16),
        ((owners, 2 * half), f32),
        ((owners, rows, width), bf16),
    ]
    made = expert_call(
        late_kernel,
        owners,
        [first, hidden, taken, slots, gates, shared, w_down, s_down],
        [pl.BlockSpec(memory_space=pltpu.SMEM), growing(k, rows, units), growing(k, rows, width)]
        + [held_whole(*a.shape) for a in (slots, gates, shared)]
        + [weights_of(w_down), held_whole(*s_down.shape)],
        outs,
        [held_whole(*shape) for shape, _ in outs[:3]] + [growing(0, rows, width)],
        [],
        [pltpu.VMEM((owners, rows, width), bf16)],
        2 * owners * rows * width * (units + GROUP * BLOCK) + 4 * half * width * s_down.shape[0],
        2 * owners * width * (units + 2 * rows) + 4 * half * width,
    )
    return made[:2], made[2], made[3]


def local(
    tokens,
    gain_attn,
    w_qkv,
    w_out,
    gain_ffn,
    w_router,
    w_shared_in,
    w_shared_down,
    w_expert_in,
    w_expert_down,
    routes,
    plan,
    cotangent,
):
    n_ctx, planes = lax.axis_size("ctx"), lax.axis_size("fsdp")
    devices = n_ctx * planes
    ctx, plane = lax.axis_index("ctx"), lax.axis_index("fsdp")
    device = ctx * planes + plane
    amount, width = tokens.shape[1:]
    head_size = width // HEADS
    heads = HEADS // n_ctx
    part = heads * head_size
    scale = head_size ** (-0.5)
    rows = width // devices
    per_owner = w_expert_in.shape[0]
    units = w_shared_down.shape[0]
    bf16, f32 = jnp.bfloat16, jnp.float32
    order = jnp.array(plane_order(), jnp.int32)
    places = order ^ ctx

    def to_all(values):
        return lax.all_to_all(values, BOTH, split_axis=0, concat_axis=0, tiled=True)

    qkv_part = w_qkv.reshape(rows, 3, n_ctx, part).transpose(2, 0, 1, 3).reshape(n_ctx, rows, 3 * part)
    qkv_part = lax.all_to_all(qkv_part, "ctx", split_axis=0, concat_axis=0, tiled=True)
    seq_rows = jnp.concatenate(gather_plane(tokens[0]), axis=0)

    expert_ids = jnp.arange(EXPERTS, dtype=jnp.int32)
    own_mask = jnp.sum((expert_ids[:, None, None] == routes[0].T[None]).astype(f32), axis=1)
    small = jnp.concatenate([w_router, gain_attn[:, None], gain_ffn[:, None]], axis=1)
    small = jnp.pad(small, ((0, 0), (0, amount - EXPERTS - 2)))
    small = gather_small(jnp.concatenate([own_mask.astype(bf16), small], axis=0))
    masks = small[:, :, :EXPERTS].transpose(0, 2, 1, 3).reshape(planes, EXPERTS, n_ctx * amount)
    masks = masks.astype(f32)
    sources = jnp.arange(n_ctx, dtype=jnp.int32) ^ ctx
    sources = sources // 2 + (sources % 2) * (n_ctx // 2)
    back = lax.rem(plane - jnp.arange(planes, dtype=jnp.int32) + planes, planes)
    sources = (back[None, :] * n_ctx + sources[:, None]).reshape(-1)
    small = small[:, :, EXPERTS:].reshape(devices, rows, amount)
    small = jnp.take(small, sources, axis=0).reshape(width, amount)
    router_full = small[:, :EXPERTS]
    router_t = router_full.T
    gain_one = small[:, EXPERTS].astype(f32)
    gain_two = small[:, EXPERTS + 1].astype(f32)

    qkv_w = by_plane(ring(qkv_part), 1).reshape(width, 3 * part)
    out_w = by_plane(ring(w_out), 0).reshape(part, width)
    shared_in = w_shared_in.reshape(rows, 2, devices, units).transpose(2, 0, 1, 3)
    shared_in = to_all(shared_in.reshape(devices, rows, 2 * units)).reshape(width, 2, units)
    lane = -(-units // BLOCK) * BLOCK
    s_in = jnp.pad(shared_in, ((0, 0), (0, 0), (0, lane - units))).reshape(width, 2 * lane)
    s_down = jnp.pad(w_shared_down, ((0, lane - units), (0, 0)))

    first_expert = lax.rem(device * per_owner, EXPERTS)
    mask_own = lax.dynamic_slice_in_dim(masks, first_expert, per_owner, 1)
    mask_own = mask_own.reshape(planes, per_owner, n_ctx, amount)
    ranking = jnp.cumsum(mask_own, axis=3) - mask_own
    slots = ranking + (CAP * (jnp.arange(n_ctx) % GROUP)).astype(f32)[:, None]
    slots = jnp.where(mask_own > 0, slots, -1.0).reshape(planes, per_owner, n_ctx * amount)
    first = first_expert.reshape(1).astype(jnp.int32)

    grads = [gather_plane(block) for block in ring(cotangent[0])]
    kept, dhs = [], []
    for k in range(planes):
        kept, made = early(k, planes, grads[k], slots[k], w_expert_down, s_down, kept)
        dhs.append(made)
    taken, dh = kept

    half_block = amount // 2
    half_ids = (places[:, None] * 2 + jnp.arange(2, dtype=jnp.int32)[None, :]).reshape(-1)
    placed = jnp.sum(
        jnp.where(half_ids[:, None] == jnp.arange(plan.shape[0])[None, :], plan[None, :], 0), axis=1
    )
    pos = (placed[:, None] * half_block + jnp.arange(half_block)[None, :]).reshape(-1)
    visible = pos[None, :] <= pos[:, None]

    own_rows = tokens[0].astype(f32)
    normed = rms_scale(seq_rows.astype(f32), gain_one).astype(bf16)
    projected = dot(normed, qkv_w)
    query = rotate(projected[:, :part], pos, heads).astype(bf16)
    key = rotate(projected[:, part : 2 * part], pos, heads).astype(bf16)
    value = projected[:, 2 * part :].astype(bf16)

    def head_of(values, head):
        return values[:, head * head_size : (head + 1) * head_size]

    expos, totals, mixes = [], [], []
    for head in range(heads):
        scores = contract_cols(head_of(query, head), head_of(key, head)) * scale
        scores = jnp.where(visible, scores, NEGATIVE)
        top = jnp.max(scores, axis=1, keepdims=True)
        expo = jnp.where(visible, jnp.exp(scores - top), 0.0)
        total = jnp.sum(expo, axis=1, keepdims=True)
        expos.append(expo)
        totals.append(total)
        mixes.append(dot(expo.astype(bf16), head_of(value, head)) / total)
    mixed_b = jnp.concatenate(mixes, axis=1).astype(bf16)
    middle_row = n_ctx * amount // 2
    attended = [dot(side, out_w).astype(bf16) for side in (mixed_b[:middle_row], mixed_b[middle_row:])]
    residual = own_rows + scatter_plane(*attended).astype(f32)
    ffn_own = rms_scale(residual, gain_two).astype(bf16)

    ffn = [gather_plane(block) for block in ring(ffn_own)]
    kept, d_parts, gates, hidden_s, d_joined_s = [], [], [], [], []
    for k in range(planes):
        kept, pair, *made = middle(
            k, planes, first, ffn[k], router_t, masks[k], slots[k], w_expert_in, s_in, dh, dhs[k], kept
        )
        d_parts.append(scatter_plane(*pair))
        for some, one in zip((gates, hidden_s, d_joined_s), made, strict=True):
            some.append(one)
    rows_in, hidden, d_joined = kept
    d_ffn = ring_sum(d_parts)
    out_pairs, dgates, dys = [], [], []
    for k in range(planes):
        pair, dgate, dy = late(
            k, planes, first, hidden, taken, slots[k], gates[k], hidden_s[k], w_expert_down, s_down, []
        )
        out_pairs.append(pair)
        dgates.append(dgate)
        dys.append(dy)

    dgate = jnp.stack(dgates).reshape(planes, per_owner, n_ctx, amount).transpose(0, 2, 1, 3)
    dgate = jnp.take(dgate.reshape(devices, per_owner * amount), sources, axis=0)
    dgate = to_all(dgate).reshape(2, EXPERTS, amount)
    dgate = dgate[0] + dgate[1]
    gates_own = gates[0][:, :amount]
    dlogits = gates_own * (dgate - jnp.sum(gates_own * dgate, axis=0, keepdims=True))
    dlogits_b = dlogits.astype(bf16).T

    def small_sum(values):
        flat = to_all(values.reshape(devices, -1))
        return jnp.sum(flat, axis=0).reshape(values.shape[1:])

    d_ffn = d_ffn.astype(f32) + contract_cols(dlogits_b, router_full)
    router_grad = small_sum(contract_rows(ffn_own, dlogits_b).reshape(devices, rows, EXPERTS))
    second_back = jax.vjp(rms_scale, residual, gain_two)[1](d_ffn)
    d_residual = cotangent[0].astype(f32) + second_back[0]
    gain_ffn_grad = small_sum(second_back[1].reshape(devices, rows))

    out_parts = [scatter_plane(*pair) for pair in out_pairs]
    result = (residual + ring_sum(out_parts).astype(f32)).astype(bf16)

    d_attn = jnp.concatenate(gather_plane(d_residual.astype(bf16)), axis=0)
    out_grad = contract_rows(mixed_b, d_attn).astype(bf16).reshape(planes, rows, width)
    out_grad = ring_sum(from_plane(out_grad, 0)).astype(f32)
    d_mixed = contract_cols(d_attn, out_w).astype(bf16).astype(f32)
    d_query, d_key, d_value = [], [], []
    for head in range(heads):
        d_head = head_of(d_mixed, head)
        total, expo = totals[head], expos[head]
        grad_num = (d_head / total).astype(bf16)
        shift = jnp.sum(d_head * mixes[head], axis=1, keepdims=True) / total
        d_prob = contract_cols(grad_num, head_of(value, head))
        d_score = (expo * (d_prob - shift)).astype(bf16)
        d_value.append(contract_rows(expo.astype(bf16), grad_num))
        d_query.append(dot(d_score, head_of(key, head)) * scale)
        d_key.append(contract_rows(d_score, head_of(query, head)) * scale)
    d_query = rotate(jnp.concatenate(d_query, axis=1), -pos, heads)
    d_key = rotate(jnp.concatenate(d_key, axis=1), -pos, heads)
    d_projected = jnp.concatenate([d_query, d_key] + d_value, axis=1).astype(bf16)
    qkv_grad = contract_rows(normed, d_projected).astype(bf16)
    qkv_grad = qkv_grad.reshape(n_ctx, planes, rows, 3 * part)
    qkv_grad = ring_sum(from_plane(qkv_grad, 1))
    qkv_grad = lax.all_to_all(qkv_grad, "ctx", split_axis=0, concat_axis=0, tiled=True)
    qkv_grad = qkv_grad.reshape(n_ctx, rows, 3, part).transpose(1, 2, 0, 3)
    qkv_grad = qkv_grad.reshape(rows, 3 * width).astype(f32)
    d_normed = [
        contract_cols(side, qkv_w).astype(bf16)
        for side in (d_projected[:middle_row], d_projected[middle_row:])
    ]
    d_normed = scatter_plane(*d_normed).astype(f32)
    first_back = jax.vjp(rms_scale, own_rows, gain_one)[1](d_normed)
    tokens_grad = d_residual + first_back[0]
    gain_attn_grad = small_sum(first_back[1].reshape(devices, rows))

    dy = jnp.concatenate(dys, axis=1)
    expert_in_grad = jnp.einsum("jcd,jcf->jdf", rows_in, d_joined, preferred_element_type=f32)
    expert_down_grad = jnp.einsum("jcf,jcd->jfd", hidden, dy, preferred_element_type=f32)
    shared_down_grad, shared_in_grad = 0.0, 0.0
    for k in range(planes):
        at = 0
        for rows_x, rows_g in zip(ffn[k], grads[k], strict=True):
            span = slice(at, at + rows_x.shape[0])
            at += rows_x.shape[0]
            shared_down_grad += contract_rows(hidden_s[k][span], rows_g)
            shared_in_grad += contract_rows(d_joined_s[k][span], rows_x)
    shared_down_grad = shared_down_grad[:units]
    shared_in_grad = shared_in_grad.reshape(2, lane, width)[:, :units].reshape(2 * units, width)
    shared_in_grad = shared_in_grad.T.astype(bf16).reshape(devices, rows, 2 * units)
    shared_in_grad = to_all(shared_in_grad).reshape(devices, rows, 2, units).transpose(1, 2, 0, 3)
    shared_in_grad = shared_in_grad.reshape(rows, 2 * devices * units).astype(f32)
    return (
        result[None],
        tokens_grad[None],
        gain_attn_grad,
        qkv_grad,
        out_grad,
        gain_ffn_grad,
        router_grad,
        shared_in_grad,
        shared_down_grad,
        expert_in_grad,
        expert_down_grad,
    )


def solution(mesh):
    split = P(BOTH)
    matrix = P(BOTH, None)
    cube = P(BOTH, None, None)
    batch = P("fsdp", "ctx", None)
    return jax.shard_map(
        local,
        mesh=mesh,
        in_specs=(
            batch,
            split,
            matrix,
            matrix,
            split,
            matrix,
            matrix,
            matrix,
            cube,
            cube,
            batch,
            P(),
            batch,
        ),
        out_specs=(
            batch,
            batch,
            split,
            matrix,
            matrix,
            split,
            matrix,
            matrix,
            matrix,
            cube,
            cube,
        ),
        check_vma=False,
    )
```

time: 4290 us -> 1060 us (0.25)
  waiting for transfers between devices: 3270 us -> 312 us
  blocking collectives: 365 us -> 0 us
  Pallas kernels: 0 us -> 217 us
  matrix products: 326 us -> 132 us
  starting transfers between devices: 31 us -> 172 us
    reduce_scatter x5 -> x0, waiting for transfers between devices: 2270 us -> none  [the longest x1 973 us: local(): lax.psum_scatter(shared_in_grad, ('ctx', 'fsdp'), scatter_dimension=0, ti...]
    all_to_all x4 -> x8, waiting for transfers between devices: 705 us -> 28.7 us  [the longest x6 20.9 us: to_all(): return lax.all_to_all(values, BOTH, split_axis=0, concat_axis=0, tiled=True)]
    ppermute x0 -> x130, waiting for transfers between devices: none -> 283 us  [the longest x27 145 us: turn(): lax.ppermute(values, 'fsdp', [(i, (i + 1) % count) for i in range(count)])]
    all_gather x1 -> x0, blocking collectives: 282 us -> none  [second_weights(): lax.all_gather(w_router, ('ctx', 'fsdp'), axis=0, tiled=True)]
    all_gather x6 -> x0, waiting for transfers between devices: 244 us -> none  [the longest x1 113 us: first_weights(): lax.all_gather(w_qkv, ('ctx', 'fsdp'), axis=0, tiled=True)]
    pallas_call x0 -> x12, Pallas kernels: none -> 217 us  [expert_call(): pl.pallas_call(functools.partial(kernel, carried=len(kept)), grid=(owners...]
    dot_general x17 -> x9, matrix products: 220 us -> 59.1 us  [the longest x1 28.1 us: local(): jnp.einsum('jcd,jcf->jdf', rows_in, d_joined, preferred_element_type=f32)]
    ppermute x0 -> x130, starting transfers between devices: none -> 135 us  [the longest x103 113 us: swap(): return lax.ppermute(values, 'ctx', [(i, i ^ bit) for i in range(count)])]
  transfers between devices with their start and end apart: 17 -> 138, of which waited for: 12 -> 47; matrix products, arithmetic and copies ran while one was open for 11% -> 31% of each run, Pallas kernels for 0% -> 21%
where the time goes in v1:
time: 1060 us; the launch traced here: 1050 us
  waiting for transfers between devices  312 us (29%)
  Pallas kernels  217 us (20%)
  starting transfers between devices  172 us (16%)
  local copies, waits for them, and re-layouts  134 us (13%)
  matrix products  132 us (12%)
  other arithmetic  81.6 us (8%)
    pallas_call x12, Pallas kernels, expert_call(): pl.pallas_call(functools.partial(kernel, carried=len(kept)), grid=(owners...  217 us
    ppermute x27, waiting for transfers between devices, turn(): lax.ppermute(values, 'fsdp', [(i, (i + 1) % count) for i in range(count)])  145 us
    ppermute x103, waiting for transfers between devices, swap(): return lax.ppermute(values, 'ctx', [(i, i ^ bit) for i in range(count)])  138 us
    ppermute x103, starting transfers between devices, swap(): return lax.ppermute(values, 'ctx', [(i, i ^ bit) for i in range(count)])  113 us
    unnamed x304, local copies, waits for them, and re-layouts  57.5 us
    dot_general x23, matrix products, contract_rows(): lax.dot_general(left, right, (((0,), (0,)), ((), ())), preferred_element_...  55.3 us
    convert_element_type x41, other arithmetic, add(): (left.astype(jnp.float32) + right.astype(jnp.float32)).astype(left.dtype)  32.3 us
    all_to_all x6, starting transfers between devices, to_all(): return lax.all_to_all(values, BOTH, split_axis=0, concat_axis=0, tiled=True)  29 us
  transfers between devices with their start and end apart: 138, of which 47 were waited for; matrix products, arithmetic and copies ran while one was open for 31% of the time, Pallas kernels for 21%

profile of v1, /device:TPU:0, one launch (start us, length us, event | category | flops | bytes accessed | tf_op | source)
XLA Modules:
  0.0 1052.6 jit_solution(6983673012990366930)
XLA Ops:
  30.3 5.7 collective-permute-done.7
  58.1 5.8 collective-permute-done.30
  81.9 5.2 all-to-all-start.1
  100.5 14.1 %collective-permute-done.16 = bf16[64,2048]{1,0:T(8,128)(2,1)S(1)} collective-permute-done((bf16[64,2048]{1,0:T(8,128)(2,1)S(1)}, bf16[64,2048]{1,0:T(8,128)(2,1)S(1)}, u32[]{:S(2)}, u32[]{:S(2)}) %collective-permute-start.16) | collective-permute-done | bytes 262176 | tf_op jit(solution)/shard_map/ppermute | solution.py:77
  128.4 4.5 reduce_window_sum.11
  158.0 12.0 %collective-permute-done.12 = bf16[8,64,768]{2,1,0:T(8,128)(2,1)S(1)} collective-permute-done((bf16[8,64,768]{2,1,0:T(8,128)(2,1)}, bf16[8,64,768]{2,1,0:T(8,128)(2,1)S(1)}, u32[]{:S(2)}, u32[]{:S(2)}) %collective-permute-start.12) | collective-permute-done | bytes 786464 | tf_op jit(solution)/shard_map/ppermute | solution.py:77
  174.0 27.5 %collective-permute-done.13 = bf16[8,64,768]{2,1,0:T(8,128)(2,1)S(1)} collective-permute-done((bf16[8,64,768]{2,1,0:T(8,128)(2,1)S(1)}, bf16[8,64,768]{2,1,0:T(8,128)(2,1)S(1)}, u32[]{:S(2)}, u32[]{:S(2)}) %collective-permute-start.13) | collective-permute-done | bytes 786464 | tf_op jit(solution)/shard_map/ppermute | solution.py:77
  239.2 8.6 collective-permute-done.34
  256.6 5.0 collective-permute-done.35
  263.5 5.7 collective-permute-done.20
  270.8 5.1 collective-permute-done.18
  279.4 12.5 %shard_map.221 = (bf16[4,640,2048]{2,1,0:T(8,128)(2,1)}, f32[4,640,704]{2,1,0:T(8,128)}, f32[1024,128]{1,0:T(8,128)}) custom-call(bf16[512,2048]{1,0:T(8,128)(2,1)} %copy-done.4, bf16[512,2048]{1,0:T(8,128)(2,1)} %copy-done.8, f32[4,1024]{1,0:T(4,128)} %bitcast.303, bf16[4,704,2048]{2,1,0:T(8,128)(2,1)} %refs_6_.15, bf16[128,2048]{1,0:T(8,128)(2,1)} %pad.14.refs_4_.refs_7_), custom_call_target="tpu_custom_call" | custom-call | flops 3724541952 | bytes 20971520 | tf_op jit(solution)/shard_map/pallas_call | solution.py:320
  291.9 12.1 %shard_map.222 = (bf16[4,640,2048]{2,1,0:T(8,128)(2,1)}, f32[4,640,704]{2,1,0:T(8,128)}, f32[1024,128]{1,0:T(8,128)}) custom-call(bf16[512,2048]{1,0:T(8,128)(2,1)} %constant_dynamic-update-slice_fusion.26.refs_0_, bf16[512,2048]{1,0:T(8,128)(2,1)} %collective-permute-done.47.refs_1_, ...), custom_call_target="tpu_custom_call", output_to_operand_aliasing={{0}: (5, {}), {1}: (6, {})} | custom-call | flops 3724541952 | bytes 20971520 | tf_op jit(solution)/shard_map/pallas_call | solution.py:320
  309.0 12.3 %shard_map.223 = (bf16[4,640,2048]{2,1,0:T(8,128)(2,1)}, f32[4,640,704]{2,1,0:T(8,128)}, f32[1024,128]{1,0:T(8,128)}) custom-call(bf16[512,2048]{1,0:T(8,128)(2,1)} %constant_dynamic-update-slice_fusion.21.refs_0_, bf16[512,2048]{1,0:T(8,128)(2,1)} %collective-permute-done.42.refs_1_, ...), custom_call_target="tpu_custom_call", output_to_operand_aliasing={{0}: (5, {}), {1}: (6, {})} | custom-call | flops 3724541952 | bytes 20971520 | tf_op jit(solution)/shard_map/pallas_call | solution.py:320
  321.4 12.1 %shard_map.224 = (bf16[4,640,2048]{2,1,0:T(8,128)(2,1)}, f32[4,640,704]{2,1,0:T(8,128)}, f32[1024,128]{1,0:T(8,128)}) custom-call(bf16[512,2048]{1,0:T(8,128)(2,1)} %constant_dynamic-update-slice_fusion.16.refs_0_, bf16[512,2048]{1,0:T(8,128)(2,1)} %collective-permute-done.37.refs_1_, ...), custom_call_target="tpu_custom_call", output_to_operand_aliasing={{0}: (5, {}), {1}: (6, {})} | custom-call | flops 3724541952 | bytes 20971520 | tf_op jit(solution)/shard_map/pallas_call | solution.py:320
  337.9 5.5 collective-permute-done.65
  343.5 6.9 collective-permute-done.59
  356.2 4.8 collective-permute-done.60
  361.1 6.5 collective-permute-done.54
  395.0 28.1 %shard_map.225 = (bf16[4,640,2048]{2,1,0:T(8,128)(2,1)}, bf16[4,640,704]{2,1,0:T(8,128)(2,1)}, bf16[4,640,1408]{2,1,0:T(8,128)(2,1)}, bf16[512,2048]{1,0:T(8,128...) custom-call(s32[1]{0:T(128)} %bitcast.28.refs_0_, ...), custom_call_target="tpu_custom_call" | custom-call | flops 12213813248 | bytes 36700160 | tf_op jit(solution)/shard_map/pallas_call | solution.py:320
  430.1 28.4 %shard_map.226 = (bf16[4,640,2048]{2,1,0:T(8,128)(2,1)}, bf16[4,640,704]{2,1,0:T(8,128)(2,1)}, bf16[4,640,1408]{2,1,0:T(8,128)(2,1)}, bf16[512,2048]{1,0:T(8,128...) custom-call(s32[1]{0:T(128)} %bitcast.28.refs_0_, ...), custom_call_target="tpu_custom_call", output_to_operand_aliasing={{0}: (10, {}), {1}: (11, {}), {2}: (12, {})} | custom-call | flops 12213813248 | bytes 36700160 | tf_op jit(solution)/shard_map/pallas_call | solution.py:320
  468.4 28.2 %shard_map.227 = (bf16[4,640,2048]{2,1,0:T(8,128)(2,1)}, bf16[4,640,704]{2,1,0:T(8,128)(2,1)}, bf16[4,640,1408]{2,1,0:T(8,128)(2,1)}, bf16[512,2048]{1,0:T(8,128...) custom-call(s32[1]{0:T(128)} %bitcast.28.refs_0_, ...), custom_call_target="tpu_custom_call", output_to_operand_aliasing={{0}: (10, {}), {1}: (11, {}), {2}: (12, {})} | custom-call | flops 12213813248 | bytes 36700160 | tf_op jit(solution)/shard_map/pallas_call | solution.py:320
  510.6 28.2 %shard_map.228 = (bf16[4,640,2048]{2,1,0:T(8,128)(2,1)}, bf16[4,640,704]{2,1,0:T(8,128)(2,1)}, bf16[4,640,1408]{2,1,0:T(8,128)(2,1)}, bf16[512,2048]{1,0:T(8,128...) custom-call(s32[1]{0:T(128)} %bitcast.28.refs_0_, ...), custom_call_target="tpu_custom_call", output_to_operand_aliasing={{0}: (10, {}), {1}: (11, {}), {2}: (12, {})} | custom-call | flops 12213813248 | bytes 36700160 | tf_op jit(solution)/shard_map/pallas_call | solution.py:320
  545.7 14.1 %shard_map.230 = (bf16[512,2048]{1,0:T(8,128)(2,1)}, bf16[512,2048]{1,0:T(8,128)(2,1)}, f32[4,1024]{1,0:T(4,128)}, bf16[4,160,2048]{2,1,0:T(8,128)(2,1)}) custom-call(s32[1]{0:T(128)} %bitcast.28.refs_0_, bf16[4,640,704]{2,1,0:T(8,128)(2,1)} %get-tuple-element.91.refs_1_, bf16[4,640,2048]{2,1,0:T(8,128)(2,1)} %get-tuple-element.92.refs_2_, ...), custom_call_target="tpu_custom_call" | custom-call | flops 3724541952 | bytes 20971520 | tf_op jit(solution)/shard_map/pallas_call | solution.py:320
  560.9 13.6 %shard_map.232 = (bf16[512,2048]{1,0:T(8,128)(2,1)}, bf16[512,2048]{1,0:T(8,128)(2,1)}, f32[4,1024]{1,0:T(4,128)}, bf16[4,160,2048]{2,1,0:T(8,128)(2,1)}) custom-call(s32[1]{0:T(128)} %bitcast.28.refs_0_, bf16[4,640,704]{2,1,0:T(8,128)(2,1)} %get-tuple-element.91.refs_1_, bf16[4,640,2048]{2,1,0:T(8,128)(2,1)} %get-tuple-element.92.refs_2_, ...), custom_call_target="tpu_custom_call" | custom-call | flops 3724541952 | bytes 20971520 | tf_op jit(solution)/shard_map/pallas_call | solution.py:320
  575.2 13.7 %shard_map.231 = (bf16[512,2048]{1,0:T(8,128)(2,1)}, bf16[512,2048]{1,0:T(8,128)(2,1)}, f32[4,1024]{1,0:T(4,128)}, bf16[4,160,2048]{2,1,0:T(8,128)(2,1)}) custom-call(s32[1]{0:T(128)} %bitcast.28.refs_0_, bf16[4,640,704]{2,1,0:T(8,128)(2,1)} %get-tuple-element.91.refs_1_, bf16[4,640,2048]{2,1,0:T(8,128)(2,1)} %get-tuple-element.92.refs_2_, ...), custom_call_target="tpu_custom_call" | custom-call | flops 3724541952 | bytes 20971520 | tf_op jit(solution)/shard_map/pallas_call | solution.py:320
  588.9 13.7 %shard_map.229 = (bf16[512,2048]{1,0:T(8,128)(2,1)}, bf16[512,2048]{1,0:T(8,128)(2,1)}, f32[4,1024]{1,0:T(4,128)}, bf16[4,160,2048]{2,1,0:T(8,128)(2,1)}) custom-call(s32[1]{0:T(128)} %bitcast.28.refs_0_, bf16[4,640,704]{2,1,0:T(8,128)(2,1)} %get-tuple-element.91.refs_1_, bf16[4,640,2048]{2,1,0:T(8,128)(2,1)} %get-tuple-element.92.refs_2_, ...), custom_call_target="tpu_custom_call" | custom-call | flops 3724541952 | bytes 20971520 | tf_op jit(solution)/shard_map/pallas_call | solution.py:320
  604.8 4.8 all-to-all-start.2
  609.7 28.1 %fusion.197 = f32[4,2048,1408]{2,1,0:T(8,128)} fusion(bf16[4,640,2048]{2,1,0:T(8,128)(2,1)} %get-tuple-element.125, bf16[4,640,1408]{2,1,0:T(8,128)(2,1)} %get-tuple-element.126), kind=kOutput, calls=%fused_computation.517 | convolution fusion | flops 14763950080 | bytes 63832064 | tf_op jit(solution)/shard_map/jcd,jcf->jdf/dot_general | solution.py:625
  637.8 16.9 %fusion = f32[4,704,2048]{2,1,0:T(8,128)} fusion(bf16[4,640,704]{2,1,0:T(8,128)(2,1)} %get-tuple-element.91.refs_1_, bf16[4,160,2048]{2,1,0:T(8,128)(2,1)} %get-tuple-element.130, bf16[4,160,2048]{2,1,0:T(8,128)(2,1)} %get-tuple-element.129, bf16[4,160,2048]{2,1,0:T(8,128)(2,1)} %get-tuple-element.128, bf16[4,160,2048]{2,1,0:T(8,128)(2,1)} %get-tuple-element.127), kind=kOutput, calls=%fused_computation.4 | convolution fusion | flops 7423918080 | bytes 37158912 | tf_op jit(solution)/shard_map/jcf,jcd->jfd/dot_general | solution.py:626
  659.7 4.5 fusion.19
  675.0 4.6 all-to-all-start.6
  681.6 11.4 %collective-permute-done.94 = bf16[64,2048]{1,0:T(8,128)(2,1)S(1)} collective-permute-done((bf16[64,2048]{1,0:T(8,128)(2,1)S(1)}, bf16[64,2048]{1,0:T(8,128)(2,1)S(1)}, u32[]{:S(2)}, u32[]{:S(2)}) %collective-permute-start.94) | collective-permute-done | bytes 262176 | tf_op jit(solution)/shard_map/ppermute | solution.py:72
  699.6 5.3 all-to-all-start.7
  715.8 14.2 %all-to-all-done.7 = bf16[32,64,176]{2,1,0:T(8,128)(2,1)S(1)} async-done(((bf16[32,64,176]{2,1,0:T(8,128)(2,1)}), bf16[32,64,176]{2,1,0:T(8,128)(2,1)S(1)}, u32[]{:S(2)}, u32[]{:S(2)}) %all-to-all-start.7) | async-done | bytes 720928 | tf_op jit(solution)/shard_map/all_to_all | solution.py:469
  740.4 6.0 collective-permute-done.104
  763.3 5.7 collective-permute-done.111
  770.9 4.7 collective-permute-done.105
  801.9 6.5 collective-permute-done.100
  821.7 6.3 collective-permute-done.113
  835.3 15.6 %collective-permute-done.115 = bf16[128,2048]{1,0:T(8,128)(2,1)S(1)} collective-permute-done((bf16[128,2048]{1,0:T(8,128)(2,1)S(1)}, bf16[128,2048]{1,0:T(8,128)(2,1)S(1)}, u32[]{:S(2)}, u32[]{:S(2)}) %collective-permute-start.115) | collective-permute-done | bytes 524320 | tf_op jit(solution)/shard_map/ppermute | solution.py:72
  925.8 24.1 %collective-permute-done.128 = bf16[64,2048]{1,0:T(8,128)(2,1)S(1)} collective-permute-done((bf16[64,2048]{1,0:T(8,128)(2,1)S(1)}, bf16[64,2048]{1,0:T(8,128)(2,1)S(1)}, u32[]{:S(2)}, u32[]{:S(2)}) %collective-permute-start.128) | collective-permute-done | bytes 262176 | tf_op jit(solution)/shard_map/ppermute | solution.py:77
  951.6 30.9 %collective-permute-done.125 = bf16[8,64,768]{2,1,0:T(8,128)(2,1)S(1)} collective-permute-done((bf16[8,64,768]{2,1,0:T(8,128)(2,1)S(1)}, bf16[8,64,768]{2,1,0:T(8,128)(2,1)S(1)}, u32[]{:S(2)}, u32[]{:S(2)}) %collective-permute-start.125) | collective-permute-done | bytes 786464 | tf_op jit(solution)/shard_map/ppermute | solution.py:77
  984.5 4.7 collective-permute-done.120
  991.0 4.6 collective-permute-done.122
  1015.0 5.6 all-to-all-start.3
  1026.0 6.7 all-to-all-done.3
  1041.0 7.8 all-to-all-done.4
  (819 shorter events, 489.7 us)
Async XLA Ops:
  0.6 65.1 %collective-permute-start = (bf16[128,2048]{1,0:T(8,128)(2,1)}, bf16[128,2048]{1,0:T(8,128)(2,1)}, u32[]{:S(2)}, u32[]{:S(2)}) collective-permute-start(bf16[128,2048]{1,0:T(8,128)(2,1)} %bitcast.250), channel_id=1, source_target_pairs={{0,8},{4,12},{8,0},{12,4},{16,24},{20,28},{24,16},{28,20},{1,9},{5... | collective-permute-start | bytes 1572872 | tf_op jit(solution)/shard_map/ppermute | solution.py:72
  3.6 63.8 %collective-permute-start.1 = (bf16[128,2048]{1,0:T(8,128)(2,1)}, bf16[128,2048]{1,0:T(8,128)(2,1)}, u32[]{:S(2)}, u32[]{:S(2)}) collective-permute-start(bf16[128,2048]{1,0:T(8,128)(2,1)} %bitcast.251), channel_id=1, source_target_pairs={{0,16},{4,20},{8,24},{12,28},{16,0},{20,4},{24,8},{28,12},{1,17},{... | collective-permute-start | bytes 1572872 | tf_op jit(solution)/shard_map/ppermute | solution.py:72
  9.9 40.8 %collective-permute-start.14 = (bf16[64,2048]{1,0:T(8,128)(2,1)}, bf16[64,2048]{1,0:T(8,128)(2,1)}, u32[]{:S(2)}, u32[]{:S(2)}) collective-permute-start(bf16[64,2048]{1,0:T(8,128)(2,1)} %param.17), channel_id=1, source_target_pairs={{0,1},{1,2},{2,3},{3,0},{4,5},{5,6},{6,7},{7,4},{8,9},{9,10},{10,1... | collective-permute-start | bytes 786440 | tf_op jit(solution)/shard_map/ppermute | solution.py:77
  11.4 59.2 %collective-permute-start.49 = (bf16[128,2048]{1,0:T(8,128)(2,1)}, bf16[128,2048]{1,0:T(8,128)(2,1)}, u32[]{:S(2)}, u32[]{:S(2)}) collective-permute-start(bf16[128,2048]{1,0:T(8,128)(2,1)} %bitcast.259), channel_id=1, source_target_pairs={{0,16},{4,20},{8,24},{12,28},{16,0},{20,4},{24,8},{28,12},{1,17},{... | collective-permute-start | bytes 1572872 | tf_op jit(solution)/shard_map/ppermute | solution.py:72
  15.4 66.5 %all-to-all-start = ((bf16[8,64,768]{2,1,0:T(8,128)(2,1)}), bf16[8,64,768]{2,1,0:T(8,128)(2,1)}, u32[]{:S(2)}, u32[]{:S(2)}) async-start(bf16[8,64,768]{2,1,0:T(8,128)(2,1)} %reshape.425), calls=%async_computation | async-start | bytes 1572864 | tf_op jit(solution)/shard_map/all_to_all | solution.py:472
  65.8 52.6 %collective-permute-start.10 = (bf16[4,4,128,128]{3,2,0,1:T(8,128)(2,1)}, bf16[4,4,128,128]{3,2,0,1:T(8,128)(2,1)}, u32[]{:S(2)}, u32[]{:S(2)}) collective-permute-start(bf16[4,4,128,128]{3,2,0,1:T(8,128)(2,1)} %pad_maximum_fusion.3), channel_id=1, source_target_pairs={{0,4},{4,0},{8,12},{12,8},{16,20},{20,16},{24,28},{28,24},{1,5},{5... | collective-permute-start | bytes 1572872 | tf_op jit(solution)/shard_map/ppermute | solution.py:72
  81.9 138.9 %all-to-all-start.1 = ((bf16[32,64,176]{2,1,0:T(8,128)(2,1)}), bf16[32,64,176]{2,1,0:T(8,128)(2,1)}, u32[]{:S(2)}, u32[]{:S(2)}) async-start(bf16[32,64,176]{2,1,0:T(8,128)(2,1)} %reshape.431), calls=%async_computation.1 | async-start | bytes 2097152 | tf_op jit(solution)/shard_map/all_to_all | solution.py:469
  92.2 49.1 %collective-permute-start.44 = (bf16[128,2048]{1,0:T(8,128)(2,1)}, bf16[128,2048]{1,0:T(8,128)(2,1)}, u32[]{:S(2)}, u32[]{:S(2)}) collective-permute-start(bf16[128,2048]{1,0:T(8,128)(2,1)} %collective-permute-done.30), channel_id=1, source_target_pairs={{0,16},{4,20},{8,24},{12,28},{16,0},{20,4},{24,8},{28,12},{1,17},{... | collective-permute-start | bytes 1572872 | tf_op jit(solution)/shard_map/ppermute | solution.py:72
  95.5 48.5 %collective-permute-start.43 = (bf16[128,2048]{1,0:T(8,128)(2,1)}, bf16[128,2048]{1,0:T(8,128)(2,1)}, u32[]{:S(2)}, u32[]{:S(2)}) collective-permute-start(bf16[128,2048]{1,0:T(8,128)(2,1)} %collective-permute-done.30), channel_id=1, source_target_pairs={{0,8},{4,12},{8,0},{12,4},{16,24},{20,28},{24,16},{28,20},{1,9},{5... | collective-permute-start | bytes 1572872 | tf_op jit(solution)/shard_map/ppermute | solution.py:72
  97.9 48.5 %collective-permute-start.31 = (bf16[128,2048]{1,0:T(8,128)(2,1)}, bf16[128,2048]{1,0:T(8,128)(2,1)}, u32[]{:S(2)}, u32[]{:S(2)}) collective-permute-start(bf16[128,2048]{1,0:T(8,128)(2,1)} %collective-permute-done.30), channel_id=1, source_target_pairs={{0,1},{1,2},{2,3},{3,0},{4,5},{5,6},{6,7},{7,4},{8,9},{9,10},{10,1... | collective-permute-start | bytes 1572872 | tf_op jit(solution)/shard_map/ppermute | solution.py:77
  114.6 34.4 %collective-permute-start.11 = (bf16[8,64,768]{2,1,0:T(8,128)(2,1)}, bf16[8,64,768]{2,1,0:T(8,128)(2,1)}, u32[]{:S(2)}, u32[]{:S(2)}) collective-permute-start(bf16[8,64,768]{2,1,0:T(8,128)(2,1)} %all-to-all-done), channel_id=1, source_target_pairs={{0,1},{1,2},{2,3},{3,0},{4,5},{5,6},{6,7},{7,4},{8,9},{9,10},{10,1... | collective-permute-start | bytes 2359304 | tf_op jit(solution)/shard_map/ppermute | solution.py:77
  118.4 52.4 %collective-permute-start.4 = (bf16[512,2048]{1,0:T(8,128)(2,1)}, bf16[512,2048]{1,0:T(8,128)(2,1)}, u32[]{:S(2)}, u32[]{:S(2)}) collective-permute-start(bf16[512,2048]{1,0:T(8,128)(2,1)} %get-tuple-element.233), channel_id=1, source_target_pairs={{0,4},{4,0},{8,12},{12,8},{16,20},{20,16},{24,28},{28,24},{1,5},{5... | collective-permute-start | bytes 6291464 | tf_op jit(solution)/shard_map/ppermute | solution.py:72
  142.3 77.7 %collective-permute-start.46 = (bf16[64,2048]{1,0:T(8,128)(2,1)S(1)}, bf16[64,2048]{1,0:T(8,128)(2,1)S(1)}, u32[]{:S(2)}, u32[]{:S(2)}) collective-permute-start(bf16[64,2048]{1,0:T(8,128)(2,1)S(1)} %slice.970), channel_id=1, source_target_pairs={{0,8},{4,12},{8,0},{12,4},{16,24},{20,28},{24,16},{28,20},{1,9},{5... | collective-permute-start | bytes 786440 | tf_op jit(solution)/shard_map/ppermute | solution.py:72
  146.5 80.0 %collective-permute-start.39 = (bf16[128,2048]{1,0:T(8,128)(2,1)}, bf16[128,2048]{1,0:T(8,128)(2,1)S(1)}, u32[]{:S(2)}, u32[]{:S(2)}) collective-permute-start(bf16[128,2048]{1,0:T(8,128)(2,1)} %collective-permute-done.31), channel_id=1, source_target_pairs={{0,16},{4,20},{8,24},{12,28},{16,0},{20,4},{24,8},{28,12},{1,17},{... | collective-permute-start | bytes 1572872 | tf_op jit(solution)/shard_map/ppermute | solution.py:72
  155.4 71.7 %collective-permute-start.38 = (bf16[128,2048]{1,0:T(8,128)(2,1)}, bf16[128,2048]{1,0:T(8,128)(2,1)}, u32[]{:S(2)}, u32[]{:S(2)}) collective-permute-start(bf16[128,2048]{1,0:T(8,128)(2,1)} %collective-permute-done.31), channel_id=1, source_target_pairs={{0,8},{4,12},{8,0},{12,4},{16,24},{20,28},{24,16},{28,20},{1,9},{5... | collective-permute-start | bytes 1572872 | tf_op jit(solution)/shard_map/ppermute | solution.py:72
  170.1 59.6 %collective-permute-start.32 = (bf16[128,2048]{1,0:T(8,128)(2,1)}, bf16[128,2048]{1,0:T(8,128)(2,1)}, u32[]{:S(2)}, u32[]{:S(2)}) collective-permute-start(bf16[128,2048]{1,0:T(8,128)(2,1)} %collective-permute-done.31), channel_id=1, source_target_pairs={{0,1},{1,2},{2,3},{3,0},{4,5},{5,6},{6,7},{7,4},{8,9},{9,10},{10,1... | collective-permute-start | bytes 1572872 | tf_op jit(solution)/shard_map/ppermute | solution.py:77
  170.8 30.7 %collective-permute-start.13 = (bf16[8,64,768]{2,1,0:T(8,128)(2,1)S(1)}, bf16[8,64,768]{2,1,0:T(8,128)(2,1)S(1)}, u32[]{:S(2)}, u32[]{:S(2)}) collective-permute-start(bf16[8,64,768]{2,1,0:T(8,128)(2,1)S(1)} %collective-permute-done.12), channel_id=1, source_target_pairs={{0,1},{1,2},{2,3},{3,0},{4,5},{5,6},{6,7},{7,4},{8,9},{9,10},{10,1... | collective-permute-start | bytes 2359304 | tf_op jit(solution)/shard_map/ppermute | solution.py:77
  220.0 33.0 %collective-permute-start.17 = (bf16[512,2048]{1,0:T(8,128)(2,1)}, bf16[512,2048]{1,0:T(8,128)(2,1)}, u32[]{:S(2)}, u32[]{:S(2)}) collective-permute-start(bf16[512,2048]{1,0:T(8,128)(2,1)} %convolution_convert_fusion.1), channel_id=1, source_target_pairs={{0,4},{4,0},{8,12},{12,8},{16,20},{20,16},{24,28},{28,24},{1,5},{5... | collective-permute-start | bytes 6291464 | tf_op jit(solution)/shard_map/ppermute | solution.py:72
  237.2 40.2 %collective-permute-start.52 = (bf16[512,2048]{1,0:T(8,128)(2,1)S(1)}, bf16[512,2048]{1,0:T(8,128)(2,1)S(1)}, u32[]{:S(2)}, u32[]{:S(2)}) collective-permute-start(bf16[512,2048]{1,0:T(8,128)(2,1)S(1)} %constant_dynamic-update-slice_fusion.31.refs_0_), channel_id=1, source_target_pairs={{0,4},{4,0},{8,12},{12,8},{16,20},{20,16},{24,28},{28,24},{1,5},{5... | collective-permute-start | bytes 6291464 | tf_op jit(solution)/shard_map/ppermute | solution.py:72
  238.0 54.0 %collective-permute-start.47 = (bf16[512,2048]{1,0:T(8,128)(2,1)}, bf16[512,2048]{1,0:T(8,128)(2,1)}, u32[]{:S(2)}, u32[]{:S(2)}) collective-permute-start(bf16[512,2048]{1,0:T(8,128)(2,1)} %constant_dynamic-update-slice_fusion.26.refs_0_), channel_id=1, source_target_pairs={{0,4},{4,0},{8,12},{12,8},{16,20},{20,16},{24,28},{28,24},{1,5},{5... | collective-permute-start | bytes 6291464 | tf_op jit(solution)/shard_map/ppermute | solution.py:72
  247.8 61.3 %collective-permute-start.42 = (bf16[512,2048]{1,0:T(8,128)(2,1)}, bf16[512,2048]{1,0:T(8,128)(2,1)}, u32[]{:S(2)}, u32[]{:S(2)}) collective-permute-start(bf16[512,2048]{1,0:T(8,128)(2,1)} %constant_dynamic-update-slice_fusion.21.refs_0_), channel_id=1, source_target_pairs={{0,4},{4,0},{8,12},{12,8},{16,20},{20,16},{24,28},{28,24},{1,5},{5... | collective-permute-start | bytes 6291464 | tf_op jit(solution)/shard_map/ppermute | solution.py:72
  263.5 57.9 %collective-permute-start.37 = (bf16[512,2048]{1,0:T(8,128)(2,1)}, bf16[512,2048]{1,0:T(8,128)(2,1)}, u32[]{:S(2)}, u32[]{:S(2)}) collective-permute-start(bf16[512,2048]{1,0:T(8,128)(2,1)} %constant_dynamic-update-slice_fusion.16.refs_0_), channel_id=1, source_target_pairs={{0,4},{4,0},{8,12},{12,8},{16,20},{20,16},{24,28},{28,24},{1,5},{5... | collective-permute-start | bytes 6291464 | tf_op jit(solution)/shard_map/ppermute | solution.py:72
  275.9 28.2 %collective-permute-start.21 = (bf16[128,2048]{1,0:T(8,128)(2,1)S(1)}, bf16[128,2048]{1,0:T(8,128)(2,1)}, u32[]{:S(2)}, u32[]{:S(2)}) collective-permute-start(bf16[128,2048]{1,0:T(8,128)(2,1)S(1)} %pad_maximum_fusion.5), channel_id=1, source_target_pairs={{0,16},{4,20},{8,24},{12,28},{16,0},{20,4},{24,8},{28,12},{1,17},{... | collective-permute-start | bytes 1572872 | tf_op jit(solution)/shard_map/ppermute | solution.py:72
  361.0 32.6 %collective-permute-start.67 = (bf16[512,2048]{1,0:T(8,128)(2,1)S(1)}, bf16[512,2048]{1,0:T(8,128)(2,1)S(1)}, u32[]{:S(2)}, u32[]{:S(2)}) collective-permute-start(bf16[512,2048]{1,0:T(8,128)(2,1)S(1)} %constant_dynamic-update-slice_fusion.46.refs_1_), channel_id=1, source_target_pairs={{0,4},{4,0},{8,12},{12,8},{16,20},{20,16},{24,28},{28,24},{1,5},{5... | collective-permute-start | bytes 6291464 | tf_op jit(solution)/shard_map/ppermute | solution.py:72
  377.9 52.2 %collective-permute-start.62 = (bf16[512,2048]{1,0:T(8,128)(2,1)S(1)}, bf16[512,2048]{1,0:T(8,128)(2,1)}, u32[]{:S(2)}, u32[]{:S(2)}) collective-permute-start(bf16[512,2048]{1,0:T(8,128)(2,1)S(1)} %constant_dynamic-update-slice_fusion.41.refs_1_), channel_id=1, source_target_pairs={{0,4},{4,0},{8,12},{12,8},{16,20},{20,16},{24,28},{28,24},{1,5},{5... | collective-permute-start | bytes 6291464 | tf_op jit(solution)/shard_map/ppermute | solution.py:72
  379.3 89.1 %collective-permute-start.57 = (bf16[512,2048]{1,0:T(8,128)(2,1)}, bf16[512,2048]{1,0:T(8,128)(2,1)}, u32[]{:S(2)}, u32[]{:S(2)}) collective-permute-start(bf16[512,2048]{1,0:T(8,128)(2,1)} %constant_dynamic-update-slice_fusion.36.refs_1_), channel_id=1, source_target_pairs={{0,4},{4,0},{8,12},{12,8},{16,20},{20,16},{24,28},{28,24},{1,5},{5... | collective-permute-start | bytes 6291464 | tf_op jit(solution)/shard_map/ppermute | solution.py:72
  393.7 117.0 %collective-permute-start.29 = (bf16[512,2048]{1,0:T(8,128)(2,1)}, bf16[512,2048]{1,0:T(8,128)(2,1)}, u32[]{:S(2)}, u32[]{:S(2)}) collective-permute-start(bf16[512,2048]{1,0:T(8,128)(2,1)} %constant_dynamic-update-slice_fusion.11.refs_1_), channel_id=1, source_target_pairs={{0,4},{4,0},{8,12},{12,8},{16,20},{20,16},{24,28},{28,24},{1,5},{5... | collective-permute-start | bytes 6291464 | tf_op jit(solution)/shard_map/ppermute | solution.py:72
  423.1 245.6 %collective-permute-start.91 = (bf16[512,2048]{1,0:T(8,128)(2,1)}, bf16[512,2048]{1,0:T(8,128)(2,1)}, u32[]{:S(2)}, u32[]{:S(2)}) collective-permute-start(bf16[512,2048]{1,0:T(8,128)(2,1)} %get-tuple-element.110), channel_id=1, source_target_pairs={{0,4},{4,0},{8,12},{12,8},{16,20},{20,16},{24,28},{28,24},{1,5},{5... | collective-permute-start | bytes 6291464 | tf_op jit(solution)/shard_map/ppermute | solution.py:72
  458.5 234.6 %collective-permute-start.106 = (bf16[512,2048]{1,0:T(8,128)(2,1)}, bf16[512,2048]{1,0:T(8,128)(2,1)}, u32[]{:S(2)}, u32[]{:S(2)}) collective-permute-start(bf16[512,2048]{1,0:T(8,128)(2,1)} %get-tuple-element.116), channel_id=1, source_target_pairs={{0,4},{4,0},{8,12},{12,8},{16,20},{20,16},{24,28},{28,24},{1,5},{5... | collective-permute-start | bytes 6291464 | tf_op jit(solution)/shard_map/ppermute | solution.py:72
  496.6 212.1 %collective-permute-start.101 = (bf16[512,2048]{1,0:T(8,128)(2,1)}, bf16[512,2048]{1,0:T(8,128)(2,1)}, u32[]{:S(2)}, u32[]{:S(2)}) collective-permute-start(bf16[512,2048]{1,0:T(8,128)(2,1)} %get-tuple-element.114), channel_id=1, source_target_pairs={{0,4},{4,0},{8,12},{12,8},{16,20},{20,16},{24,28},{28,24},{1,5},{5... | collective-permute-start | bytes 6291464 | tf_op jit(solution)/shard_map/ppermute | solution.py:72
  545.6 203.8 %collective-permute-start.96 = (bf16[512,2048]{1,0:T(8,128)(2,1)}, bf16[512,2048]{1,0:T(8,128)(2,1)}, u32[]{:S(2)}, u32[]{:S(2)}) collective-permute-start(bf16[512,2048]{1,0:T(8,128)(2,1)} %get-tuple-element.112), channel_id=1, source_target_pairs={{0,4},{4,0},{8,12},{12,8},{16,20},{20,16},{24,28},{28,24},{1,5},{5... | collective-permute-start | bytes 6291464 | tf_op jit(solution)/shard_map/ppermute | solution.py:72
  560.4 192.7 %collective-permute-start.73 = (bf16[512,2048]{1,0:T(8,128)(2,1)}, bf16[512,2048]{1,0:T(8,128)(2,1)}, u32[]{:S(2)}, u32[]{:S(2)}) collective-permute-start(bf16[512,2048]{1,0:T(8,128)(2,1)} %get-tuple-element.100), channel_id=1, source_target_pairs={{0,4},{4,0},{8,12},{12,8},{16,20},{20,16},{24,28},{28,24},{1,5},{5... | collective-permute-start | bytes 6291464 | tf_op jit(solution)/shard_map/ppermute | solution.py:72
  604.8 62.3 %all-to-all-start.2 = ((f32[32,1,512]{2,1,0:T(1,128)}), f32[32,1,512]{2,1,0:T(1,128)S(1)}, u32[]{:S(2)}, u32[]{:S(2)}) async-start(f32[32,1,512]{2,1,0:T(1,128)} %copy.170), calls=%async_computation.2 | async-start | bytes 131072 | tf_op jit(solution)/shard_map/all_to_all | solution.py:469
  699.6 30.4 %all-to-all-start.7 = ((bf16[32,64,176]{2,1,0:T(8,128)(2,1)}), bf16[32,64,176]{2,1,0:T(8,128)(2,1)S(1)}, u32[]{:S(2)}, u32[]{:S(2)}) async-start(bf16[32,64,176]{2,1,0:T(8,128)(2,1)} %bitcast.56), calls=%async_computation.7 | async-start | bytes 2097152 | tf_op jit(solution)/shard_map/all_to_all | solution.py:469
  707.0 40.0 %collective-permute-start.110 = (bf16[128,2048]{1,0:T(8,128)(2,1)}, bf16[128,2048]{1,0:T(8,128)(2,1)}, u32[]{:S(2)}, u32[]{:S(2)}) collective-permute-start(bf16[128,2048]{1,0:T(8,128)(2,1)} %pad_maximum_fusion.21), channel_id=1, source_target_pairs={{0,16},{4,20},{8,24},{12,28},{16,0},{20,4},{24,8},{28,12},{1,17},{... | collective-permute-start | bytes 1572872 | tf_op jit(solution)/shard_map/ppermute | solution.py:72
  714.1 33.0 %collective-permute-start.108 = (bf16[128,2048]{1,0:T(8,128)(2,1)}, bf16[128,2048]{1,0:T(8,128)(2,1)}, u32[]{:S(2)}, u32[]{:S(2)}) collective-permute-start(bf16[128,2048]{1,0:T(8,128)(2,1)} %pad_maximum_fusion.20), channel_id=1, source_target_pairs={{0,8},{4,12},{8,0},{12,4},{16,24},{20,28},{24,16},{28,20},{1,9},{5... | collective-permute-start | bytes 1572872 | tf_op jit(solution)/shard_map/ppermute | solution.py:72
  749.5 68.0 %collective-permute-start.95 = (bf16[128,2048]{1,0:T(8,128)(2,1)S(1)}, bf16[128,2048]{1,0:T(8,128)(2,1)S(1)}, u32[]{:S(2)}, u32[]{:S(2)}) collective-permute-start(bf16[128,2048]{1,0:T(8,128)(2,1)S(1)} %copy-done.74), channel_id=1, source_target_pairs={{0,16},{4,20},{8,24},{12,28},{16,0},{20,4},{24,8},{28,12},{1,17},{... | collective-permute-start | bytes 1572872 | tf_op jit(solution)/shard_map/ppermute | solution.py:72
  815.9 179.8 %collective-permute-start.77 = (bf16[128,2048]{1,0:T(8,128)(2,1)}, bf16[128,2048]{1,0:T(8,128)(2,1)}, u32[]{:S(2)}, u32[]{:S(2)}) collective-permute-start(bf16[128,2048]{1,0:T(8,128)(2,1)} %pad_maximum_fusion.9), channel_id=1, source_target_pairs={{0,16},{4,20},{8,24},{12,28},{16,0},{20,4},{24,8},{28,12},{1,17},{... | collective-permute-start | bytes 1572872 | tf_op jit(solution)/shard_map/ppermute | solution.py:72
  817.5 46.7 %collective-permute-start.87 = (bf16[128,2048]{1,0:T(8,128)(2,1)S(1)}, bf16[128,2048]{1,0:T(8,128)(2,1)S(1)}, u32[]{:S(2)}, u32[]{:S(2)}) collective-permute-start(bf16[128,2048]{1,0:T(8,128)(2,1)S(1)} %pad_maximum_fusion.13), channel_id=1, source_target_pairs={{0,16},{4,20},{8,24},{12,28},{16,0},{20,4},{24,8},{28,12},{1,17},{... | collective-permute-start | bytes 1572872 | tf_op jit(solution)/shard_map/ppermute | solution.py:72
  820.2 45.2 %collective-permute-start.85 = (bf16[128,2048]{1,0:T(8,128)(2,1)S(1)}, bf16[128,2048]{1,0:T(8,128)(2,1)S(1)}, u32[]{:S(2)}, u32[]{:S(2)}) collective-permute-start(bf16[128,2048]{1,0:T(8,128)(2,1)S(1)} %pad_maximum_fusion.12), channel_id=1, source_target_pairs={{0,8},{4,12},{8,0},{12,4},{16,24},{20,28},{24,16},{28,20},{1,9},{5... | collective-permute-start | bytes 1572872 | tf_op jit(solution)/shard_map/ppermute | solution.py:72
  873.7 122.2 %collective-permute-start.75 = (bf16[128,2048]{1,0:T(8,128)(2,1)}, bf16[128,2048]{1,0:T(8,128)(2,1)}, u32[]{:S(2)}, u32[]{:S(2)}) collective-permute-start(bf16[128,2048]{1,0:T(8,128)(2,1)} %pad_maximum_fusion.8), channel_id=1, source_target_pairs={{0,8},{4,12},{8,0},{12,4},{16,24},{20,28},{24,16},{28,20},{1,9},{5... | collective-permute-start | bytes 1572872 | tf_op jit(solution)/shard_map/ppermute | solution.py:72
  917.7 32.9 %collective-permute-start.119 = (bf16[512,2048]{1,0:T(8,128)(2,1)S(1)}, bf16[512,2048]{1,0:T(8,128)(2,1)S(1)}, u32[]{:S(2)}, u32[]{:S(2)}) collective-permute-start(bf16[512,2048]{1,0:T(8,128)(2,1)S(1)} %convolution_convert_fusion.3), channel_id=1, source_target_pairs={{0,4},{4,0},{8,12},{12,8},{16,20},{20,16},{24,28},{28,24},{1,5},{5... | collective-permute-start | bytes 6291464 | tf_op jit(solution)/shard_map/ppermute | solution.py:72
  922.5 27.8 %collective-permute-start.124 = (bf16[8,64,768]{2,1,0:T(8,128)(2,1)S(1)}, bf16[8,64,768]{2,1,0:T(8,128)(2,1)S(1)}, u32[]{:S(2)}, u32[]{:S(2)}) collective-permute-start(bf16[8,64,768]{2,1,0:T(8,128)(2,1)S(1)} %dynamic-slice_bitcast_fusion), channel_id=1, source_target_pairs={{0,1},{1,2},{2,3},{3,0},{4,5},{5,6},{6,7},{7,4},{8,9},{9,10},{10,1... | collective-permute-start | bytes 2359304 | tf_op jit(solution)/shard_map/ppermute | solution.py:77
  949.9 86.4 %collective-permute-start.72 = (bf16[128,2048]{1,0:T(8,128)(2,1)}, bf16[128,2048]{1,0:T(8,128)(2,1)}, u32[]{:S(2)}, u32[]{:S(2)}) collective-permute-start(bf16[128,2048]{1,0:T(8,128)(2,1)} %pad_maximum_fusion.7), channel_id=1, source_target_pairs={{0,16},{4,20},{8,24},{12,28},{16,0},{20,4},{24,8},{28,12},{1,17},{... | collective-permute-start | bytes 1572872 | tf_op jit(solution)/shard_map/ppermute | solution.py:72
  950.3 47.8 %collective-permute-start.89 = (bf16[128,2048]{1,0:T(8,128)(2,1)}, bf16[128,2048]{1,0:T(8,128)(2,1)S(1)}, u32[]{:S(2)}, u32[]{:S(2)}) collective-permute-start(bf16[128,2048]{1,0:T(8,128)(2,1)} %add_convert_fusion.36), channel_id=1, source_target_pairs={{0,1},{1,2},{2,3},{3,0},{4,5},{5,6},{6,7},{7,4},{8,9},{9,10},{10,1... | collective-permute-start | bytes 1572872 | tf_op jit(solution)/shard_map/ppermute | solution.py:77
  950.6 31.9 %collective-permute-start.125 = (bf16[8,64,768]{2,1,0:T(8,128)(2,1)S(1)}, bf16[8,64,768]{2,1,0:T(8,128)(2,1)S(1)}, u32[]{:S(2)}, u32[]{:S(2)}) collective-permute-start(bf16[8,64,768]{2,1,0:T(8,128)(2,1)S(1)} %fusion.20), channel_id=1, source_target_pairs={{0,1},{1,2},{2,3},{3,0},{4,5},{5,6},{6,7},{7,4},{8,9},{9,10},{10,1... | collective-permute-start | bytes 2359304 | tf_op jit(solution)/shard_map/ppermute | solution.py:77
  995.8 27.8 %collective-permute-start.126 = (bf16[8,64,768]{2,1,0:T(8,128)(2,1)S(1)}, bf16[8,64,768]{2,1,0:T(8,128)(2,1)}, u32[]{:S(2)}, u32[]{:S(2)}) collective-permute-start(bf16[8,64,768]{2,1,0:T(8,128)(2,1)S(1)} %fusion.21), channel_id=1, source_target_pairs={{0,1},{1,2},{2,3},{3,0},{4,5},{5,6},{6,7},{7,4},{8,9},{9,10},{10,1... | collective-permute-start | bytes 2359304 | tf_op jit(solution)/shard_map/ppermute | solution.py:77
  1006.6 29.7 %collective-permute-start.70 = (bf16[128,2048]{1,0:T(8,128)(2,1)}, bf16[128,2048]{1,0:T(8,128)(2,1)}, u32[]{:S(2)}, u32[]{:S(2)}) collective-permute-start(bf16[128,2048]{1,0:T(8,128)(2,1)} %pad_maximum_fusion.6), channel_id=1, source_target_pairs={{0,8},{4,12},{8,0},{12,4},{16,24},{20,28},{24,16},{28,20},{1,9},{5... | collective-permute-start | bytes 1572872 | tf_op jit(solution)/shard_map/ppermute | solution.py:72
  (214 other events, 2629.3 us)

commit v2 on v1

v2 whole, which is shorter than its diff:
```python
import functools

import jax
import jax.numpy as jnp
from jax import lax
from jax.experimental import pallas as pl
from jax.experimental.pallas import tpu as pltpu
from jax.sharding import PartitionSpec as P

HEADS = 16
EXPERTS = 64
CAP = 20
BLOCK = 128
EXTRA = 16
GROUP = 4
VMEM = 60 * 1024 * 1024

EPSILON = 1e-06
ROPE_BASE = 10000.0
NEGATIVE = -1e30
BOTH = ("ctx", "fsdp")


def rms_scale(values, gain):
    inverse = lax.rsqrt(jnp.mean(values * values, axis=-1, keepdims=True) + EPSILON)
    return values * inverse * gain


def dot(left, right):
    return jnp.dot(left, right, preferred_element_type=jnp.float32)


def contract_rows(left, right):
    return lax.dot_general(
        left, right, (((0,), (0,)), ((), ())), preferred_element_type=jnp.float32
    )


def contract_cols(left, right):
    return lax.dot_general(
        left, right, (((1,), (1,)), ((), ())), preferred_element_type=jnp.float32
    )


def plane_order():
    count = lax.axis_size("ctx")
    return list(range(0, count, 2)) + list(range(1, count, 2))


def ctx_bits():
    count = lax.axis_size("ctx")
    return [1 << i for i in range(1, count.bit_length() - 1)]


def swap(values, bit):
    count = lax.axis_size("ctx")
    return lax.ppermute(values, "ctx", [(i, i ^ bit) for i in range(count)])


def turn(values, step=1):
    count = lax.axis_size("fsdp")
    return lax.ppermute(values, "fsdp", [(i, (i + step) % count) for i in range(count)])


def add(left, right):
    return (left.astype(jnp.float32) + right.astype(jnp.float32)).astype(left.dtype)


class Step:
    def __init__(self, sent, make=None, beside=(), outs=()):
        self.sent, self.make, self.beside, self.outs = sent, make, list(beside), list(outs)


class Transfer:
    def __init__(self, steps):
        self.steps, self.step, self.done, self.result = steps, None, False, None
        self.advance(None)

    def advance(self, arrived):
        try:
            self.step = self.steps.send(arrived)
        except StopIteration as stop:
            self.step, self.done, self.result = None, True, stop.value


class Clock:
    def __init__(self):
        self.token = jnp.zeros((8, 128), jnp.float32)

    def now(self, values):
        return values + self.token[0, 0].astype(values.dtype)


def stage(clock, transfers, beside=()):
    active = [t for t in transfers if not t.done]
    making = [t.step for t in active if t.step.make is not None]
    passed = [clock.token, *beside]
    waited = [a for t in active if t.step.make is None for a in t.step.sent]
    taken = [a for step in making for a in step.sent + step.beside]
    outs = [jax.ShapeDtypeStruct(o, step.sent[0].dtype) for step in making for o in step.outs]
    first = len(passed) + len(waited)

    def kernel(*refs):
        inputs, made = refs[first : first + len(taken)], refs[first + len(taken) + len(passed) :]
        for step in making:
            count = len(step.sent) + len(step.beside)
            step.make(inputs[:count], made[: len(step.outs)])
            inputs, made = inputs[count:], made[len(step.outs) :]

    far, near = pl.BlockSpec(memory_space=pltpu.HBM), pl.BlockSpec(memory_space=pltpu.VMEM)
    arrays = pl.pallas_call(
        kernel,
        in_specs=[far] * first + [near] * len(taken),
        out_specs=[far] * len(passed) + [near] * len(outs),
        out_shape=[jax.ShapeDtypeStruct(a.shape, a.dtype) for a in passed] + outs,
        input_output_aliases={i: i for i in range(len(passed))},
        compiler_params=pltpu.CompilerParams(vmem_limit_bytes=VMEM),
    )(*passed, *waited, *taken)
    clock.token, given, arrays = arrays[0], arrays[1 : len(passed)], arrays[len(passed) :]
    for t in active:
        if t.step.make is None:
            t.advance(t.step.sent)
        else:
            count = len(t.step.outs)
            made, arrays = arrays[:count], arrays[count:]
            t.advance(made)
    return given


def finish(clock, *transfers):
    while not all(t.done for t in transfers):
        stage(clock, transfers)
    return [t.result for t in transfers]


CHUNK = 16


def chunks(amount, body):
    @pl.loop(0, amount // CHUNK)
    def _(i):
        body(pl.multiple_of(i * CHUNK, CHUNK))


def put(source, target, at=0, start=0, amount=None):
    def body(row):
        target[pl.ds(at + row, CHUNK), :] = source[pl.ds(start + row, CHUNK), :]

    chunks(amount or target.shape[0] - at, body)


def put_sum(target, sources, starts=None, at=0, amount=None):
    starts = starts or [0] * len(sources)

    def body(row):
        total = 0.0
        for source, start in zip(sources, starts, strict=True):
            total = total + source[pl.ds(start + row, CHUNK), :].astype(jnp.float32)
        target[pl.ds(at + row, CHUNK), :] = total.astype(target.dtype)

    chunks(amount or target.shape[0] - at, body)


def put_blocks_sum(taken, made):
    for i in range(made[0].shape[0]):
        put_sum(made[0].at[i], [ref.at[i] for ref in taken])


def put_joined(order):
    def make(taken, made):
        at = 0
        for i in order:
            put(taken[i], made[0], at, 0, taken[i].shape[0])
            at += taken[i].shape[0]

    return make


def turned(block, step=1):
    (block,) = yield Step([turn(block, step)])
    return block


def ring(block):
    held = [block]
    for _ in range(lax.axis_size("fsdp") - 1):
        (block,) = yield Step([turn(block)])
        held.append(block)
    return held


def ring_sum(pieces):
    total = pieces[min(1, len(pieces) - 1)]
    for piece in pieces[2:] + (pieces[:1] if len(pieces) > 1 else []):
        (total,) = yield Step([turn(total)], put_blocks_sum, [piece], [piece.shape])
    return total


def staged_sum(parts):
    total = parts[0].result
    for part in parts[1:]:
        (total,) = yield Step([turn(total)])
        while not part.done:
            (total,) = yield Step([total])
        total = add(part.result, total)
    return total


def to_all(values):
    return lax.all_to_all(values, BOTH, split_axis=0, concat_axis=0, tiled=True)


def exchanged(values):
    (values,) = yield Step([to_all(values)])
    return values


def gather_plane(block, direct=True):
    bits = ctx_bits()
    amount, width = block.shape
    half = -(-amount // 2 // CHUNK) * CHUNK
    if len(bits) == 2 and direct:
        others = [swap(block, place) for place in (bits[0], bits[1], bits[0] | bits[1])]
        (near,) = yield Step(others, put_joined([3, 0, 1, 2]), [block], [(4 * amount, width)])
    elif len(bits) == 2:
        x_bit, y_bit = bits
        over_x, over_y = swap(block, x_bit), swap(block, y_bit)

        def halves(taken, made):
            put(taken[0], made[0], 0, 0, half)
            put(taken[1], made[1], 0, half, amount - half)

        parts = [(half, width), (amount - half, width)]
        first, second = yield Step([over_x, over_y], halves, [], parts)
        corner = [swap(first, y_bit), swap(second, x_bit)]
        (near,) = yield Step(
            corner, put_joined([2, 3, 4, 0, 1]), [block, over_x, over_y], [(4 * amount, width)]
        )
    else:
        near = block
        for bit in bits:
            shape = (2 * near.shape[0], width)
            (near,) = yield Step([swap(near, bit)], put_joined([1, 0]), [near], [shape])
    (far,) = yield Step([swap(near, 1)])
    return near, far


def scatter_plane(near, far, direct=True):
    bits = ctx_bits()
    size, width = near.shape[0] >> len(bits), near.shape[1]
    half = size // 2
    whole, part = (size, width), (half, width)
    if len(bits) != 2:
        (held,) = yield Step([swap(far, 1)], lambda t, m: put_sum(m[0], t), [near], [near.shape])
        for bit in reversed(bits):
            middle = held.shape[0] // 2

            def fold(taken, made, middle=middle):
                put_sum(made[0], taken)

            (held,) = yield Step([swap(held[middle:], bit)], fold, [held[:middle]], [(middle, width)])
        return held
    x_bit, y_bit = bits
    if direct:

        def spread(taken, made):
            for i in range(4):
                put_sum(made[i], taken, [i * size, i * size])

        own, part_x, part_y, corner = yield Step([swap(far, 1)], spread, [near], [whole] * 4)
        back = [swap(part_x, x_bit), swap(part_y, y_bit), swap(corner, x_bit | y_bit)]
        (total,) = yield Step(back, lambda t, m: put_sum(m[0], t), [own], [whole])
        return total

    def split(taken, made):
        for i, at in enumerate((0, size, 2 * size, 3 * size, 3 * size + half)):
            put_sum(made[i], taken, [at, at])

    def join(taken, made):
        for_y, for_x, part_x, part_y = taken
        put(part_x, made[0], 0, 0, half)
        put_sum(made[0], [part_x, for_x], [half, 0], half, half)
        put_sum(made[1], [part_y, for_y], [0, 0], 0, half)
        put(part_y, made[1], half, half, half)

    own, part_x, part_y, corner_a, corner_b = yield Step(
        [swap(far, 1)], split, [near], [whole] * 3 + [part] * 2
    )
    part_x, part_y = yield Step(
        [swap(corner_a, x_bit), swap(corner_b, y_bit)], join, [part_x, part_y], [whole] * 2
    )
    (total,) = yield Step(
        [swap(part_x, x_bit), swap(part_y, y_bit)], lambda t, m: put_sum(m[0], t), [own], [whole]
    )
    return total


def gate_parts(first, second):
    sigmoid = 1.0 / (1.0 + jnp.exp(-first))
    return sigmoid, first * sigmoid * second


def gate_back(first, second, sigmoid, upstream):
    silu = first * sigmoid
    return upstream * second * (sigmoid + silu * (1.0 - sigmoid)), upstream * silu


def pick(slot_ref, owner, span):
    tokens = GROUP * BLOCK
    slots = slot_ref[pl.ds(owner, 1), span * tokens : (span + 1) * tokens]
    ids = lax.broadcasted_iota(jnp.int32, (GROUP * CAP, tokens), 0).astype(jnp.float32)
    return ids == slots


def pick_all(slot_ref, span):
    chosen = [pick(slot_ref, owner, span).astype(jnp.bfloat16) for owner in range(slot_ref.shape[0])]
    return jnp.concatenate(chosen, axis=0)


def spans_of(first_ref, second_ref, stride=BLOCK):
    per_side = first_ref.shape[0] // (GROUP * stride)
    return [
        (ref, [(n * GROUP + i) * stride for i in range(GROUP)])
        for ref in (first_ref, second_ref)
        for n in range(per_side)
    ]


def read_span(ref, starts):
    if starts[1] == starts[0] + BLOCK:
        return ref[starts[0] : starts[0] + GROUP * BLOCK, :]
    return jnp.concatenate([ref[at : at + BLOCK, :] for at in starts], axis=0)


def write_span(ref, starts, values):
    for i, at in enumerate(starts):
        ref[at : at + BLOCK, :] = values[i * BLOCK : (i + 1) * BLOCK].astype(ref.dtype)


def slots_at(span):
    return slice(span * GROUP * CAP, (span + 1) * GROUP * CAP)


def tokens_at(span):
    return slice(span * GROUP * BLOCK, (span + 1) * GROUP * BLOCK)


def early_kernel(*refs, carried):
    ga_ref, gb_ref, slot_ref, down_ref, s_down_ref = refs[:5]
    rows_ref, dh_ref, dhs_ref, kept_ref = refs[5 + carried :]
    owners = slot_ref.shape[0]
    step = pl.program_id(0)

    @pl.when(step == 0)
    def _():
        for span, place in enumerate(spans_of(ga_ref, gb_ref, BLOCK + EXTRA)):
            values = read_span(*place)
            taken = dot(pick_all(slot_ref, span), values).astype(jnp.bfloat16)
            for owner in range(owners):
                kept_ref[owner, slots_at(span), :] = taken[slots_at(owner)]
            dhs_ref[tokens_at(span), :] = contract_cols(values, s_down_ref[...])

    rows = kept_ref[step]
    rows_ref[0] = rows
    dh_ref[0] = contract_cols(rows, down_ref[0])


def gate_rows(first_ref, values, width):
    per_row = width // BLOCK
    rows = lax.broadcasted_iota(jnp.int32, (EXTRA, width), 0)
    groups = lax.broadcasted_iota(jnp.int32, (EXTRA, width), 1) // BLOCK
    leading = values.astype(jnp.bfloat16).astype(jnp.float32)
    total = jnp.zeros((EXTRA, width), jnp.float32)
    for owner in range(values.shape[0]):
        expert = first_ref[0] + owner
        for i, one in enumerate((leading, values - leading)):
            wide = jnp.concatenate([one[owner : owner + 1]] * per_row, axis=1)
            row = (2 * first_ref[1] + i) * (EXPERTS // per_row) + expert // per_row
            here = (rows == row) & (groups == expert % per_row)
            total = total + jnp.where(here, wide, 0.0)
    return total.astype(jnp.bfloat16)


def middle_kernel(*refs, carried):
    (first_ref, xa_ref, xb_ref, router_ref, mask_ref, slot_ref, in_ref, s_in_ref, dh_ref, dhs_ref) = refs[:10]
    (rows_ref, hidden_ref, dj_ref, da_ref, db_ref, gates_ref, dgate_ref, sh_ref, ds_ref, r_ref, z_ref, gate_ref) = refs[10 + carried :]
    bf16 = jnp.bfloat16
    owners = slot_ref.shape[0]
    step = pl.program_id(0)
    spans = spans_of(xa_ref, xb_ref)

    @pl.when(step == 0)
    def _():
        for span, place in enumerate(spans):
            x = read_span(*place)
            lanes = tokens_at(span)
            mask = jnp.concatenate(
                [mask_ref[span * GROUP + i].astype(jnp.float32) for i in range(GROUP)], axis=1
            )
            mask = mask >= 0
            logits = jnp.where(mask, contract_cols(router_ref[...], x), NEGATIVE)
            gates = jnp.where(mask, jnp.exp(logits - jnp.max(logits, axis=0, keepdims=True)), 0.0)
            gates = gates / jnp.sum(gates, axis=0, keepdims=True)
            gates_ref[:, lanes] = gates
            expert = lax.broadcasted_iota(jnp.int32, gates.shape, 0)
            for owner in range(owners):
                own = jnp.sum(jnp.where(expert == first_ref[0] + owner, gates, 0.0), axis=0, keepdims=True)
                gate_ref[owner, slots_at(span), :] = jnp.sum(
                    jnp.where(pick(slot_ref, owner, span), own, 0.0), axis=1, keepdims=True
                )
            taken = dot(pick_all(slot_ref, span), x).astype(bf16)
            for owner in range(owners):
                r_ref[owner, slots_at(span), :] = taken[slots_at(owner)]
            joined = dot(x, s_in_ref[...])
            units = joined.shape[1] // 2
            first, second = joined[:, :units], joined[:, units:]
            sigmoid, hidden = gate_parts(first, second)
            sh_ref[lanes, :] = hidden.astype(bf16)
            back = gate_back(first, second, sigmoid, dhs_ref[lanes, :])
            ds_ref[lanes, :] = jnp.concatenate(back, axis=1).astype(bf16)

    rows = r_ref[step]
    joined = dot(rows, in_ref[0])
    units = joined.shape[1] // 2
    first, second = joined[:, :units], joined[:, units:]
    sigmoid, hidden = gate_parts(first, second)
    back = gate_back(first, second, sigmoid, gate_ref[step] * dh_ref[0])
    d_gate = jnp.sum(hidden * dh_ref[0], axis=1, keepdims=True)
    for span in range(len(spans)):
        spread = jnp.where(pick(slot_ref, step, span), d_gate[slots_at(span)], 0.0)
        dgate_ref[pl.ds(step, 1), tokens_at(span)] = jnp.sum(spread, axis=0, keepdims=True)
    d_joined = jnp.concatenate(back, axis=1).astype(bf16)
    z_ref[step] = contract_cols(d_joined, in_ref[0]).astype(bf16)
    rows_ref[0] = rows
    hidden_ref[0] = hidden.astype(bf16)
    dj_ref[0] = d_joined

    @pl.when(step == owners - 1)
    def _():
        for span, place in enumerate(spans_of(da_ref, db_ref, BLOCK + EXTRA)):
            made = jnp.concatenate([z_ref[owner, slots_at(span), :] for owner in range(owners)], axis=0)
            total = contract_rows(pick_all(slot_ref, span), made)
            total = total + contract_cols(ds_ref[tokens_at(span), :], s_in_ref[...])
            write_span(*place, total)
            for i, at in enumerate(place[1]):
                block = span * GROUP + i
                place[0][at + BLOCK : at + BLOCK + EXTRA, :] = gate_rows(
                    first_ref, dgate_ref[:, block * BLOCK : (block + 1) * BLOCK], made.shape[1]
                )


def late_kernel(*refs, carried):
    (first_ref, hidden_ref, rows_ref, slot_ref, gates_ref, sh_ref, down_ref, s_down_ref) = refs[:8]
    (dy_ref, oa_ref, ob_ref, y_ref) = refs[8 + carried :]
    bf16 = jnp.bfloat16
    owners = slot_ref.shape[0]
    step = pl.program_id(0)
    spans = spans_of(oa_ref, ob_ref)
    partial = dot(hidden_ref[0], down_ref[0])
    rows = rows_ref[0].astype(jnp.float32)
    gates = []
    for span in range(len(spans)):
        chosen = pick(slot_ref, step, span)
        lanes = tokens_at(span)
        own = gates_ref[pl.ds(first_ref[0] + step, 1), lanes]
        gates.append(jnp.sum(jnp.where(chosen, own, 0.0), axis=1, keepdims=True))
    gate = jnp.concatenate(gates, axis=0)
    y_ref[step] = (gate * partial).astype(bf16)
    dy_ref[0] = (gate * rows).astype(bf16)

    @pl.when(step == owners - 1)
    def _():
        for span, place in enumerate(spans):
            made = jnp.concatenate([y_ref[owner, slots_at(span), :] for owner in range(owners)], axis=0)
            total = contract_rows(pick_all(slot_ref, span), made)
            total = total + dot(sh_ref[tokens_at(span), :], s_down_ref[...])
            write_span(*place, total)


ROWS = 256


def row_chunks(amount, body):
    @pl.loop(0, amount // ROWS)
    def _(i):
        body(pl.multiple_of(i * ROWS, ROWS))


def plane_copies(plane, pieces, target, sems):
    count = len(pieces)
    return [
        pltpu.make_async_copy(
            piece, target(lax.rem(plane - k + count, count)), sems.at[k]
        )
        for k, piece in enumerate(pieces)
    ]


def turn_head(values, cosine, sine):
    return values * cosine + pltpu.roll(values, values.shape[1] // 2, 1) * sine


def attend_kernel(*refs, planes, heads):
    (plane_ref, near_ref, far_ref, gain_ref, cos_ref, sin_ref, column_ref, row_ref) = refs[:8]
    w_pieces = refs[8 : 8 + planes]
    (oa_ref, ob_ref, normed_ref, q_ref, k_ref, v_ref, mixed_ref, top_ref, total_ref) = refs[
        9 + planes : 18 + planes
    ]
    w_ref, sems = refs[18 + planes :]
    bf16, f32 = jnp.bfloat16, jnp.float32
    plane = plane_ref[0]
    width = near_ref.shape[1]
    blocks, part = w_ref.shape[0], w_ref.shape[3] // 4
    size = part // heads
    half = near_ref.shape[0]
    amount = 2 * half
    copies = plane_copies(plane, w_pieces, lambda at: w_ref.at[:, at], sems.at[0])
    for copy in copies:
        copy.start()
    for copy in copies:
        copy.wait()

    for base, ref in ((0, near_ref), (half, far_ref)):

        def project(row, base=base, ref=ref):
            at = pl.ds(base + row, ROWS)
            x = ref[pl.ds(row, ROWS), :].astype(f32)
            normed = rms_scale(x, gain_ref[...]).astype(bf16)
            normed_ref[at, :] = normed
            projected = dot(normed, w_ref[:, :, :, : 3 * part].reshape(width, 3 * part))
            cosine, sine = cos_ref[at, :], sin_ref[at, :]
            for head in range(heads):
                mine = slice(head * size, (head + 1) * size)
                for target, start in ((q_ref, 0), (k_ref, part)):
                    values = projected[:, start + head * size : start + (head + 1) * size]
                    target[at, mine] = turn_head(values, cosine, sine).astype(bf16)
            v_ref[at, :] = projected[:, 2 * part :].astype(bf16)

        row_chunks(half, project)

    for head in range(heads):
        mine = slice(head * size, (head + 1) * size)

        def attend(row, mine=mine, head=head):
            at = pl.ds(row, ROWS)
            scores = contract_cols(q_ref[at, mine], k_ref[:, mine]) * size**-0.5
            visible = row_ref[...] <= column_ref[at, :]
            scores = jnp.where(visible, scores, NEGATIVE)
            top = jnp.max(scores, axis=1, keepdims=True)
            expo = jnp.where(visible, jnp.exp(scores - top), 0.0)
            total = jnp.sum(expo, axis=1, keepdims=True)
            top_ref[head, at, :] = top
            total_ref[head, at, :] = total
            mixed_ref[at, mine] = dot(expo.astype(bf16), v_ref[:, mine]) / total

        row_chunks(amount, attend)

    for base, ref in ((0, oa_ref), (half, ob_ref)):

        def project_out(row, base=base, ref=ref):
            mixed = mixed_ref[pl.ds(base + row, ROWS), :].astype(bf16)
            for i in range(blocks):
                weights = w_ref[i, :, :, 3 * part :].reshape(part, width // blocks)
                into = slice(i * width // blocks, (i + 1) * width // blocks)
                ref[pl.ds(row, ROWS), into] = dot(mixed, weights).astype(bf16)

        row_chunks(half, project_out)


def attend_back_kernel(*refs, planes, heads):
    (plane_ref, near_ref, far_ref, normed_ref, q_ref, k_ref, v_ref, mixed_ref, top_ref, total_ref) = refs[:10]
    (cos_ref, sin_ref, column_ref, row_ref) = refs[10:14]
    w_pieces = refs[14 : 14 + planes]
    rest = refs[15 + planes :]
    (da_ref, db_ref), w_grads = rest[:2], rest[2 : 2 + planes]
    (w_ref, gw_ref, dm_ref, dp_ref, dk_ref, dv_ref, sems) = rest[2 + planes :]
    bf16, f32 = jnp.bfloat16, jnp.float32
    plane = plane_ref[0]
    width = near_ref.shape[1]
    blocks, part = w_ref.shape[0], w_ref.shape[3] // 4
    size = part // heads
    half = near_ref.shape[0]
    amount = 2 * half
    w_copies = plane_copies(plane, w_pieces, lambda at: w_ref.at[:, at], sems.at[0])
    for copy in w_copies:
        copy.start()
    for copy in w_copies:
        copy.wait()

    for base, ref in ((0, near_ref), (half, far_ref)):

        def back_out(row, base=base, ref=ref):
            values = 0.0
            for i in range(blocks):
                weights = w_ref[i, :, :, 3 * part :].reshape(part, width // blocks)
                into = slice(i * width // blocks, (i + 1) * width // blocks)
                values = values + contract_cols(ref[pl.ds(row, ROWS), into], weights)
            dm_ref[pl.ds(base + row, ROWS), :] = values.astype(bf16).astype(f32)

        row_chunks(half, back_out)
    sides = [(mixed_ref[:half, :].astype(bf16), near_ref), (mixed_ref[half:, :].astype(bf16), far_ref)]
    for i in range(blocks):
        into = slice(i * width // blocks, (i + 1) * width // blocks)
        grad = sum(contract_rows(mixed, ref[:, into]) for mixed, ref in sides)
        grad = grad.astype(bf16).reshape(planes, part // planes, width // blocks)
        gw_ref[i, :, :, 3 * part :] = grad

    for head in range(heads):
        mine = slice(head * size, (head + 1) * size)
        dk_ref[...] = jnp.zeros_like(dk_ref)
        dv_ref[...] = jnp.zeros_like(dv_ref)

        def attend_back(row, mine=mine, head=head):
            at = pl.ds(row, ROWS)
            query, key, value = q_ref[at, mine], k_ref[:, mine], v_ref[:, mine]
            d_mixed, total = dm_ref[at, mine], total_ref[head, at, :]
            grad_num = (d_mixed / total).astype(bf16)
            shift = jnp.sum(d_mixed * mixed_ref[at, mine], axis=1, keepdims=True) / total
            scores = contract_cols(query, key) * size**-0.5
            visible = row_ref[...] <= column_ref[at, :]
            scores = jnp.where(visible, scores, NEGATIVE)
            expo = jnp.where(visible, jnp.exp(scores - top_ref[head, at, :]), 0.0)
            d_score = (expo * (contract_cols(grad_num, value) - shift)).astype(bf16)
            d_query = dot(d_score, key) * size**-0.5
            dp_ref[at, mine] = turn_head(d_query, cos_ref[at, :], -sin_ref[at, :]).astype(bf16)
            dk_ref[...] += contract_rows(d_score, query)
            dv_ref[...] += contract_rows(expo.astype(bf16), grad_num)

        row_chunks(amount, attend_back)
        d_key = turn_head(dk_ref[...] * size**-0.5, cos_ref[...], -sin_ref[...])
        dp_ref[:, part + head * size : part + (head + 1) * size] = d_key.astype(bf16)
        dp_ref[:, 2 * part + head * size : 2 * part + (head + 1) * size] = dv_ref[...].astype(bf16)

    pieces = 4
    step, count = width // pieces, blocks // pieces
    for i in range(pieces):
        grad = contract_rows(normed_ref[:, i * step : (i + 1) * step], dp_ref[...]).astype(bf16)
        grad = grad.reshape(count, *gw_ref.shape[1:3], 3 * part)
        gw_ref[i * count : (i + 1) * count, :, :, : 3 * part] = grad
    w_back = [
        pltpu.make_async_copy(
            gw_ref.at[:, lax.rem(plane - k + planes, planes)], w_grads[k], sems.at[1, k]
        )
        for k in range(planes)
    ]
    for copy in w_back:
        copy.start()
    for base, ref in ((0, da_ref), (half, db_ref)):

        def back_project(row, base=base, ref=ref):
            values = contract_cols(
                dp_ref[pl.ds(base + row, ROWS), :], w_ref[:, :, :, : 3 * part].reshape(width, 3 * part)
            )
            ref[pl.ds(row, ROWS), :] = values.astype(bf16)

        row_chunks(half, back_project)
    for copy in w_back:
        copy.wait()


def attend_call(kernel, small, blocks, pieces, outs, piece_outs, scratch, after, flops):
    far, near = pl.BlockSpec(memory_space=pltpu.HBM), pl.BlockSpec(memory_space=pltpu.VMEM)
    return pl.pallas_call(
        kernel,
        in_specs=[pl.BlockSpec(memory_space=pltpu.SMEM)]
        + [near] * len(blocks)
        + [far] * (len(pieces) + 1),
        out_specs=[near] * len(outs) + [far] * len(piece_outs),
        out_shape=[jax.ShapeDtypeStruct(shape, kind) for shape, kind in outs + piece_outs],
        scratch_shapes=scratch,
        compiler_params=pltpu.CompilerParams(vmem_limit_bytes=VMEM),
        cost_estimate=pl.CostEstimate(flops=flops, bytes_accessed=30_000_000, transcendentals=0),
    )(small, *blocks, *pieces, after)


def attend(plane, rows, gain, tables, pieces, heads, after):
    bf16, f32 = jnp.bfloat16, jnp.float32
    half, width = rows[0].shape
    planes = len(pieces)
    n_ctx, depth, four = pieces[0].shape
    part = four // 4
    outs = [((half, width), bf16)] * 2 + [((2 * half, width), bf16)]
    outs += [((2 * half, part), bf16)] * 3 + [((2 * half, part), f32)]
    outs += [((heads, 2 * half, 1), f32)] * 2
    return attend_call(
        functools.partial(attend_kernel, planes=planes, heads=heads),
        plane,
        [*rows, gain, *tables],
        pieces,
        outs,
        [],
        [
            pltpu.VMEM((n_ctx, planes, depth, four), bf16),
            pltpu.SemaphoreType.DMA((1, planes)),
        ],
        after,
        4 * half * width * 4 * part + 16 * half * half * part,
    )


def attend_back(plane, rows, saved, tables, pieces, heads, after):
    bf16, f32 = jnp.bfloat16, jnp.float32
    half, width = rows[0].shape
    planes = len(pieces)
    n_ctx, depth, four = pieces[0].shape
    part = four // 4
    made = attend_call(
        functools.partial(attend_back_kernel, planes=planes, heads=heads),
        plane,
        [*rows, *saved, *tables],
        pieces,
        [((half, width), bf16)] * 2,
        [(pieces[0].shape, bf16)] * planes,
        [
            pltpu.VMEM((n_ctx, planes, depth, four), bf16),
            pltpu.VMEM((n_ctx, planes, depth, four), bf16),
            pltpu.VMEM((2 * half, part), f32),
            pltpu.VMEM((2 * half, 3 * part), bf16),
            pltpu.VMEM((2 * half, part // heads), f32),
            pltpu.VMEM((2 * half, part // heads), f32),
            pltpu.SemaphoreType.DMA((2, planes)),
        ],
        after,
        4 * half * width * 8 * part + 40 * half * half * part,
    )
    return made[:2], list(made[2:])


def rows_kernel(left_ref, right_ref, *refs):
    refs[-1][0] = contract_rows(left_ref[0], right_ref[0])


def shared_kernel(xa_ref, xb_ref, ga_ref, gb_ref, hidden_ref, joined_ref, *refs):
    into_ref, down_ref = refs[-2:]
    size = GROUP * BLOCK
    places = spans_of(ga_ref, gb_ref, BLOCK + EXTRA)
    for i, (x_place, g_place) in enumerate(zip(spans_of(xa_ref, xb_ref), places, strict=True)):
        at = slice(i * size, (i + 1) * size)
        into = contract_rows(joined_ref[at, :], read_span(*x_place))
        down = contract_rows(hidden_ref[at, :], read_span(*g_place))
        into_ref[...] = into if i == 0 else into_ref[...] + into
        down_ref[...] = down if i == 0 else down_ref[...] + down


def held_whole(*shape):
    return pl.BlockSpec(shape, lambda j: (0,) * len(shape), pipeline_mode=pl.Buffered(1))


def expert_call(
    kernel, owners, operands, specs, outs, out_specs, kept, after, scratch, flops, moved
):
    return pl.pallas_call(
        functools.partial(kernel, carried=len(kept) + 1),
        grid=(owners,),
        in_specs=specs + [pl.BlockSpec(memory_space=pl.ANY)] * (len(kept) + 1),
        out_specs=out_specs,
        out_shape=[jax.ShapeDtypeStruct(shape, kind) for shape, kind in outs],
        scratch_shapes=scratch,
        input_output_aliases={len(operands) + i: i for i in range(len(kept))},
        compiler_params=pltpu.CompilerParams(vmem_limit_bytes=VMEM),
        cost_estimate=pl.CostEstimate(flops=flops, bytes_accessed=moved, transcendentals=0),
    )(*operands, *kept, after)


def growing(k, rows, columns):
    return pl.BlockSpec((1, rows, columns), lambda j: (j, k, 0))


def weights_of(array):
    depth = 2 if array.shape[0] > 1 else 1
    return pl.BlockSpec(
        (1,) + array.shape[1:], lambda j: (j, 0, 0), pipeline_mode=pl.Buffered(depth)
    )


def early(k, planes, grads, slots, w_down, s_down, kept, after):
    bf16, f32 = jnp.bfloat16, jnp.float32
    owners, units, width = w_down.shape
    half = grads[0].shape[0] * BLOCK // (BLOCK + EXTRA)
    rows, lane = 2 * half // BLOCK * CAP, s_down.shape[0]
    outs = [
        ((owners, planes * rows, width), bf16),
        ((owners, planes * rows, units), f32),
        ((2 * half, lane), f32),
    ]
    taken, dh, dhs = expert_call(
        early_kernel,
        owners,
        [*grads, slots, w_down, s_down],
        [held_whole(*grads[0].shape)] * 2
        + [held_whole(*slots.shape), weights_of(w_down), held_whole(*s_down.shape)],
        outs,
        [growing(k, rows, width), growing(k, rows, units), held_whole(2 * half, lane)],
        kept,
        after,
        [pltpu.VMEM((owners, rows, width), bf16)],
        2 * owners * rows * width * (units + GROUP * BLOCK) + 4 * half * width * lane,
        2 * owners * width * (units + 2 * rows) + 4 * half * width,
    )
    return [taken, dh], dhs


def middle(
    k, planes, first, rows_x, router_t, mask, slots, w_in, s_in, dh, dhs, kept, after
):
    bf16, f32 = jnp.bfloat16, jnp.float32
    owners, width, joined = w_in.shape
    half = rows_x[0].shape[0]
    rows, lane = 2 * half // BLOCK * CAP, dhs.shape[1]
    outs = [
        ((owners, planes * rows, width), bf16),
        ((owners, planes * rows, joined // 2), bf16),
        ((owners, planes * rows, joined), bf16),
        ((half // BLOCK * (BLOCK + EXTRA), width), bf16),
        ((half // BLOCK * (BLOCK + EXTRA), width), bf16),
        ((EXPERTS, 2 * half), f32),
        ((owners, 2 * half), f32),
        ((2 * half, lane), bf16),
        ((2 * half, 2 * lane), bf16),
    ]
    made = expert_call(
        middle_kernel,
        owners,
        [first, *rows_x, router_t, mask, slots, w_in, s_in, dh, dhs],
        [pl.BlockSpec(memory_space=pltpu.SMEM)]
        + [held_whole(half, width)] * 2
        + [held_whole(*a.shape) for a in (router_t, mask, slots)]
        + [weights_of(w_in), held_whole(*s_in.shape), growing(k, rows, joined // 2)]
        + [held_whole(*dhs.shape)],
        outs,
        [growing(k, rows, width), growing(k, rows, joined // 2), growing(k, rows, joined)]
        + [held_whole(*shape) for shape, _ in outs[3:]],
        kept,
        after,
        [
            pltpu.VMEM((owners, rows, width), bf16),
            pltpu.VMEM((owners, rows, width), bf16),
            pltpu.VMEM((owners, rows, 1), f32),
        ],
        4 * owners * rows * width * (joined + GROUP * BLOCK) + 16 * half * width * lane,
        2 * owners * width * (joined + 2 * rows) + 8 * half * width,
    )
    return list(made[:3]), made[3:5], made[5:]


def late(k, planes, first, hidden, taken, slots, gates, shared, w_down, s_down, kept, after):
    bf16, f32 = jnp.bfloat16, jnp.float32
    owners, units, width = w_down.shape
    half = shared.shape[0] // 2
    rows = 2 * half // BLOCK * CAP
    outs = [
        ((owners, hidden.shape[1], width), bf16),
        ((half, width), bf16),
        ((half, width), bf16),
    ]
    made = expert_call(
        late_kernel,
        owners,
        [first, hidden, taken, slots, gates, shared, w_down, s_down],
        [pl.BlockSpec(memory_space=pltpu.SMEM), growing(k, rows, units), growing(k, rows, width)]
        + [held_whole(*a.shape) for a in (slots, gates, shared)]
        + [weights_of(w_down), held_whole(*s_down.shape)],
        outs,
        [growing(k, rows, width)] + [held_whole(*shape) for shape, _ in outs[1:]],
        kept,
        after,
        [pltpu.VMEM((owners, rows, width), bf16)],
        2 * owners * rows * width * (units + GROUP * BLOCK) + 4 * half * width * s_down.shape[0],
        2 * owners * width * (units + 2 * rows) + 4 * half * width,
    )
    return list(made[:1]), made[1:]


def rows_grad(left, right, owner, count, kept, after):
    owners, amount, wide = left.shape
    narrow = right.shape[2]
    depth = pl.Buffered(2 if count > 1 else 1)
    at = lambda j: (owner + j, 0, 0)
    return pl.pallas_call(
        rows_kernel,
        grid=(count,),
        in_specs=[
            pl.BlockSpec((1, amount, wide), at, pipeline_mode=depth),
            pl.BlockSpec((1, amount, narrow), at, pipeline_mode=depth),
        ]
        + [pl.BlockSpec(memory_space=pl.ANY)] * (len(kept) + 1),
        out_specs=pl.BlockSpec((1, wide, narrow), at, pipeline_mode=depth),
        out_shape=jax.ShapeDtypeStruct((owners, wide, narrow), jnp.float32),
        input_output_aliases={2: 0} if kept else {},
        compiler_params=pltpu.CompilerParams(vmem_limit_bytes=VMEM),
        cost_estimate=pl.CostEstimate(
            flops=2 * count * amount * wide * narrow,
            bytes_accessed=4 * count * wide * narrow,
            transcendentals=0,
        ),
    )(left, right, *kept, after)


def shared_grads(rows_x, rows_g, hidden, joined, after):
    half, width = rows_x[0].shape
    near = pl.BlockSpec(memory_space=pltpu.VMEM)
    outs = [(joined.shape[1], width), (hidden.shape[1], width)]
    return pl.pallas_call(
        shared_kernel,
        in_specs=[near] * 6 + [pl.BlockSpec(memory_space=pltpu.HBM)],
        out_specs=[near] * 2,
        out_shape=[jax.ShapeDtypeStruct(shape, jnp.float32) for shape in outs],
        compiler_params=pltpu.CompilerParams(vmem_limit_bytes=VMEM),
        cost_estimate=pl.CostEstimate(
            flops=4 * half * width * (joined.shape[1] + hidden.shape[1]),
            bytes_accessed=8 * half * width,
            transcendentals=0,
        ),
    )(*rows_x, *rows_g, hidden, joined, after)


def local(
    tokens,
    gain_attn,
    w_qkv,
    w_out,
    gain_ffn,
    w_router,
    w_shared_in,
    w_shared_down,
    w_expert_in,
    w_expert_down,
    routes,
    plan,
    cotangent,
):
    n_ctx, planes = lax.axis_size("ctx"), lax.axis_size("fsdp")
    devices = n_ctx * planes
    ctx, plane = lax.axis_index("ctx"), lax.axis_index("fsdp")
    device = ctx * planes + plane
    amount, width = tokens.shape[1:]
    head_size = width // HEADS
    heads = HEADS // n_ctx
    part = heads * head_size
    rows = width // devices
    per_owner = w_expert_in.shape[0]
    units = w_shared_down.shape[0]
    bf16, f32 = jnp.bfloat16, jnp.float32
    order = jnp.array(plane_order(), jnp.int32)
    places = order ^ ctx

    clock = Clock()

    expert_ids = jnp.arange(EXPERTS, dtype=jnp.int32)
    own_mask = jnp.sum((expert_ids[:, None, None] == routes[0].T[None]).astype(f32), axis=1)
    before = (jnp.arange(amount)[:, None] < jnp.arange(amount)[None, :]).astype(bf16)
    ranking = jnp.where(own_mask > 0, dot(own_mask.astype(bf16), before), -1.0)

    qkv_part = w_qkv.reshape(rows, 3, n_ctx, part).transpose(2, 0, 1, 3).reshape(n_ctx, rows, 3 * part)
    qkv_part = lax.all_to_all(qkv_part, "ctx", split_axis=0, concat_axis=0, tiled=True)
    sequence = Transfer(gather_plane(tokens[0], False))
    small = jnp.concatenate([ranking.astype(bf16), jnp.pad(w_router, ((0, 0), (0, amount - EXPERTS)))])
    small = small.reshape(-1, width)
    held = small.shape[0]
    small = jnp.pad(small, ((0, EXTRA - held), (0, 0)))
    own_grads = jnp.concatenate([cotangent[0], small], axis=0)
    grads = [Transfer(gather_plane(own_grads, False))]
    grad_blocks = [Transfer(turned(own_grads, k)) for k in range(1, min(3, planes))]
    (qkv_part,) = stage(clock, [sequence, *grads, *grad_blocks], [qkv_part])

    out_part = w_out.reshape(rows, n_ctx, part).transpose(1, 0, 2)
    ring_w = Transfer(ring(jnp.concatenate([qkv_part, out_part], axis=2)))
    gains = jnp.concatenate([gain_attn, gain_ffn])
    gains = Transfer(exchanged(clock.now(jnp.broadcast_to(gains[None], (devices, 2 * rows)))))
    shared_in = w_shared_in.reshape(rows, 2, devices, units).transpose(2, 0, 1, 3)
    shared_in = shared_in.reshape(devices, rows, 2 * units)

    half_block = amount // 2
    half_ids = (places[:, None] * 2 + jnp.arange(2, dtype=jnp.int32)[None, :]).reshape(-1)
    placed = jnp.sum(
        jnp.where(half_ids[:, None] == jnp.arange(plan.shape[0])[None, :], plan[None, :], 0), axis=1
    )
    pos = (placed[:, None] * half_block + jnp.arange(half_block)[None, :]).reshape(-1).astype(f32)
    frequency = ROPE_BASE ** (-2.0 * jnp.arange(head_size // 2, dtype=f32) / head_size)
    angles = pos[:, None] * frequency[None, :]
    cosine, sine = jnp.cos(angles), jnp.sin(angles)
    tables = [
        jnp.concatenate([cosine, cosine], axis=1),
        jnp.concatenate([-sine, sine], axis=1),
        pos[:, None],
        pos[None, :],
    ]
    shared_in, *tables = stage(clock, [ring_w, gains, sequence, *grads], [shared_in, *tables])
    if planes > 1:
        grads.append(Transfer(gather_plane(grad_blocks[0].result, False)))
    stage(clock, [ring_w, gains, sequence, *grads])
    gain_one, gain_two = (
        gains.result[:, at : at + rows].reshape(width).astype(f32) for at in (0, rows)
    )
    seq_rows = finish(clock, sequence)[0]

    first_expert = lax.rem(device * per_owner, EXPERTS)
    first = jnp.stack([first_expert, device * per_owner // EXPERTS]).astype(jnp.int32)
    back = lax.rem(plane - jnp.arange(planes, dtype=jnp.int32) + planes, planes)
    sources = jnp.arange(n_ctx, dtype=jnp.int32) ^ ctx
    sources = sources // 2 + (sources % 2) * (n_ctx // 2)
    sources = (back[None, :] * n_ctx + sources[:, None]).reshape(-1)
    ranks, slots, routers = [], [], []

    def small_of(k):
        sides = [side.reshape(-1, amount + EXTRA, width)[:, amount : amount + held] for side in grads[k].result]
        came = jnp.concatenate(sides, axis=0).reshape(n_ctx, EXPERTS + rows, amount)
        ranks.append(came[:, :EXPERTS])
        routers.append(came[:, EXPERTS:])
        mine = lax.dynamic_slice_in_dim(came, first_expert, per_owner, 1).astype(f32)
        offset = (CAP * (jnp.arange(n_ctx) % GROUP)).astype(f32)[:, None, None]
        mine = jnp.where(mine >= 0, mine + offset, -1.0)
        slots.append(mine.transpose(1, 0, 2).reshape(per_owner, n_ctx * amount))

    lane = -(-units // BLOCK) * BLOCK
    s_down = jnp.pad(w_shared_down, ((0, lane - units), (0, 0)))
    early_kept, dhs = [], []

    def grads_stage(transfers, beside=(), work=True):
        nonlocal early_kept
        k, made = len(dhs), []
        if work and k < planes and k < len(grads) and grads[k].done:
            small_of(k)
            early_kept, made = early(
                k, planes, grads[k].result, slots[k], w_expert_down, s_down, early_kept, clock.token
            )
            made = [made]
        arrays = stage(clock, [*transfers, *grads, *grad_blocks], [*beside, *made])
        dhs.extend(arrays[len(beside) :])
        k = len(grads)
        if 2 <= k < planes and grad_blocks[k - 1].done and grads[-1].step is not grads[-1].opening:
            grads.append(Transfer(gather_plane(grad_blocks[k - 1].result, False)))
            grads[-1].opening = grads[-1].step
            if len(grad_blocks) < planes - 1:
                ahead = len(grad_blocks) + 1
                source = own_grads if ahead == 3 else grad_blocks[-1].result
                grad_blocks.append(Transfer(turned(clock.now(source), ahead if ahead == 3 else 1)))
        return arrays[: len(beside)]

    grads[-1].opening = None
    while not ring_w.done:
        grads_stage([ring_w])
    pieces = ring_w.result
    shared_in = Transfer(exchanged(clock.now(shared_in)))
    own_rows = tokens[0].astype(f32)
    plane_id = plane.reshape(1).astype(jnp.int32)
    *attended, normed, query, key, value, mixed, tops, totals = attend(
        plane_id, seq_rows, gain_one[None, :], tables, pieces, heads, clock.token
    )
    saved = [normed, query, key, value, mixed, tops, totals]
    attended = grads_stage([shared_in], attended)
    attended = Transfer(scatter_plane(*attended))
    while not attended.done:
        grads_stage([attended])
    residual = own_rows + attended.result.astype(f32)
    ffn_own = rms_scale(residual, gain_two).astype(bf16)
    shared_in = shared_in.result.reshape(width, 2, units)
    s_in = jnp.pad(shared_in, ((0, 0), (0, 0), (0, lane - units))).reshape(width, 2 * lane)

    ffn, d_parts = [Transfer(gather_plane(ffn_own))], []
    block, d_sum = Transfer(turned(ffn_own)), None
    mid_kept, mids, late_kept, out_parts, out_sum, router_t = [], [], [], [], None, None

    def do_late():
        nonlocal late_kept
        if len(out_parts) == planes:
            return []
        k = (len(out_parts) + 1) % planes
        late_kept, pair = late(
            k, planes, first, mid_kept[1], early_kept[0], slots[k], mids[k][0], mids[k][2],
            w_expert_down, s_down, late_kept, clock.token,
        )
        return list(pair)

    def outs_stage(transfers, beside=(), moving=None):
        nonlocal out_sum
        pair = do_late() if not beside else []
        if out_sum is None and len(out_parts) == planes and out_parts[0].done:
            out_sum = Transfer(staged_sum(out_parts))
        going = [t for t in out_parts if not t.done]
        fresh = [t for t in going if t.step is t.opening]
        going = [t for t in going if t not in fresh]
        if moving is not None:
            going = going[:moving]
        arrays = stage(
            clock, [*transfers, *going, *fresh, *([out_sum] if out_sum else [])], [*beside, *pair]
        )
        if pair:
            out_parts.append(Transfer(scatter_plane(*arrays)))
            out_parts[-1].opening = out_parts[-1].step
            arrays = []
        return arrays

    while d_sum is None or not d_sum.done:
        going = [*ffn, *d_parts, block, *([d_sum] if d_sum else [])]
        k = len(mids)
        if router_t is None and len(routers) == planes:
            router_full = jnp.stack(routers).reshape(devices, rows, amount)
            router_full = jnp.take(router_full, sources, axis=0).reshape(width, amount)[:, :EXPERTS]
            router_t = router_full.T
        if k < planes and ffn[k].done and len(dhs) > k and router_t is not None:
            mid_kept, pair, made = middle(
                k, planes, first, ffn[k].result, router_t, ranks[k], slots[k], w_expert_in, s_in,
                early_kept[1], dhs[k], mid_kept, clock.token,
            )
            mids.append(made)
            pair = grads_stage(going, list(pair), work=False)
            d_parts.append(Transfer(scatter_plane(*pair)))
        elif k == planes:
            outs_stage(going, moving=1 if d_parts[-1].done else 0)
        else:
            grads_stage(going)
        if len(ffn) < planes and block.done:
            ffn.append(Transfer(gather_plane(block.result)))
            if len(ffn) < planes:
                block = Transfer(turned(block.result))
        if d_sum is None and len(d_parts) == planes and d_parts[min(1, planes - 1)].done:
            d_sum = Transfer(staged_sum(d_parts[1:] + d_parts[:1]))
    rows_in, hidden, d_joined = mid_kept
    gates = mids[0][0]

    dgate = d_sum.result[amount:].astype(f32).reshape(4, EXPERTS, amount)
    dgate = jnp.sum(dgate, axis=0)
    gates_own = gates[:, :amount]
    dlogits = gates_own * (dgate - jnp.sum(gates_own * dgate, axis=0, keepdims=True))
    dlogits_b = dlogits.astype(bf16).T
    d_ffn = d_sum.result[:amount].astype(f32) + contract_cols(dlogits_b, router_full)
    second_back = jax.vjp(rms_scale, residual, gain_two)[1](d_ffn)
    d_residual = cotangent[0].astype(f32) + second_back[0]

    d_attn = Transfer(gather_plane(d_residual.astype(bf16)))
    outs_stage([d_attn], moving=0)
    while len(out_parts) < planes:
        outs_stage([], moving=1)
    shared = None
    while not d_attn.done or shared is None:
        if shared is not None:
            outs_stage([d_attn], moving=1)
            continue
        parts = [
            shared_grads(ffn[k].result, grads[k].result, mids[k][2], mids[k][3], clock.token)
            for k in range(planes)
        ]
        into, shared_down_grad = (sum(one) for one in zip(*parts, strict=True))
        into = into.reshape(2, lane, width)[:, :units].reshape(2 * units, width).T
        small = contract_rows(ffn_own, clock.now(dlogits_b))
        shared = jnp.concatenate([into, small, second_back[1][:, None]], axis=1).astype(bf16)
        shared = jnp.pad(shared, ((0, 0), (0, -shared.shape[1] % BLOCK)))
        shared = shared.reshape(devices, rows, -1)
        shared, shared_down_grad = outs_stage([d_attn], [shared, shared_down_grad], moving=1)
    shared = Transfer(exchanged(shared))

    d_normed, ring_grad = attend_back(
        plane_id, d_attn.result, saved, tables, pieces, heads, clock.token
    )
    d_normed = outs_stage([shared], list(d_normed), moving=1)
    ring_grad = Transfer(ring_sum(ring_grad))
    d_normed = Transfer(scatter_plane(*d_normed))

    first_half = -(-per_owner // 2)
    (dy,) = late_kept
    work = [lambda kept: rows_grad(rows_in, d_joined, 0, first_half, kept, clock.token)]
    if first_half < per_owner:
        work.append(
            lambda kept: rows_grad(
                rows_in, d_joined, first_half, per_owner - first_half, kept, clock.token
            )
        )
    work.append(lambda kept: rows_grad(hidden, dy, 0, per_owner, [], clock.token))
    made = []
    while work or not (ring_grad.done and d_normed.done):
        if work:
            one = work.pop(0)(made)
            (one,) = outs_stage([ring_grad, d_normed], [one], moving=1)
            if work:
                made = [one]
            else:
                (expert_in_grad,), expert_down_grad = made, one
        else:
            outs_stage([ring_grad, d_normed], [], moving=1)
    ring_grad = ring_grad.result
    qkv_grad = lax.all_to_all(ring_grad[:, :, : 3 * part], "ctx", split_axis=0, concat_axis=0, tiled=True)
    out_grad = ring_grad[:, :, 3 * part :].transpose(1, 0, 2).reshape(rows, width).astype(f32)
    first_back = jax.vjp(lambda x: rms_scale(x, gain_one), own_rows)[1](d_normed.result.astype(f32))
    tokens_grad = d_residual + first_back[0]
    shared = clock.now(shared.result)
    shared_in_grad = shared[:, :, : 2 * units].reshape(devices, rows, 2, units)
    shared_in_grad = shared_in_grad.transpose(1, 2, 0, 3).reshape(rows, 2 * devices * units).astype(f32)
    small = jnp.sum(shared[:, :, 2 * units :].astype(f32), axis=0)
    router_grad, gain_ffn_grad = small[:, :EXPERTS], small[:, EXPERTS]
    shared_down_grad = shared_down_grad[:units]
    while out_sum is None or not out_sum.done:
        if out_sum is None and out_parts[0].done:
            out_sum = Transfer(staged_sum(out_parts))
        stage(clock, [*out_parts, *([out_sum] if out_sum else [])])
    result = (residual + out_sum.result.astype(f32)).astype(bf16)
    qkv_grad = qkv_grad.reshape(n_ctx, rows, 3, part).transpose(1, 2, 0, 3)
    qkv_grad = qkv_grad.reshape(rows, 3 * width).astype(f32)
    gain_attn_grad = jnp.sum(qkv_grad * w_qkv.astype(f32), axis=1) / gain_attn.astype(f32)
    return (
        result[None],
        tokens_grad[None],
        gain_attn_grad,
        qkv_grad,
        out_grad,
        gain_ffn_grad,
        router_grad,
        shared_in_grad,
        shared_down_grad,
        expert_in_grad,
        expert_down_grad,
    )


def solution(mesh):
    split = P(BOTH)
    matrix = P(BOTH, None)
    cube = P(BOTH, None, None)
    batch = P("fsdp", "ctx", None)
    return jax.shard_map(
        local,
        mesh=mesh,
        in_specs=(
            batch,
            split,
            matrix,
            matrix,
            split,
            matrix,
            matrix,
            matrix,
            cube,
            cube,
            batch,
            P(),
            batch,
        ),
        out_specs=(
            batch,
            batch,
            split,
            matrix,
            matrix,
            split,
            matrix,
            matrix,
            matrix,
            cube,
            cube,
        ),
        check_vma=False,
    )
```

time: 1060 us -> 910 us (0.86)
  Pallas kernels: 217 us -> 447 us
  waiting for transfers between devices: 312 us -> 181 us
  matrix products: 132 us -> 1.63 us
  local copies, waits for them, and re-layouts: 134 us -> 80.3 us
  starting transfers between devices: 172 us -> 135 us
  other arithmetic: 81.6 us -> 52.6 us
    pallas_call x12 -> x43, Pallas kernels: 217 us -> 447 us  [the longest x12 221 us: expert_call(): pl.pallas_call(functools.partial(kernel, carried=len(kept) + 1), grid=(ow...]
    ppermute x27 -> x18, waiting for transfers between devices: 145 us -> 50 us  [turn(): lax.ppermute(values, 'fsdp', [(i, (i + step) % count) for i in range(coun...]
    dot_general x23 -> x1, matrix products: 55.3 us -> 0.86 us  [contract_rows(): lax.dot_general(left, right, (((0,), (0,)), ((), ())), preferred_element_...]
    dot_general x2 -> x0, matrix products: 45 us -> none  [the longest x1 28.1 us: local(): jnp.einsum('jcd,jcf->jdf', rows_in, d_joined, preferred_element_type=f32)]
    ppermute x103 -> x85, starting transfers between devices: 113 us -> 84.3 us  [swap(): return lax.ppermute(values, 'ctx', [(i, i ^ bit) for i in range(count)])]
    unnamed x304 -> x193, local copies, waits for them, and re-layouts: 57.5 us -> 30.2 us
    convert_element_type x41 -> x5, other arithmetic: 32.3 us -> 7.97 us  [add(): (left.astype(jnp.float32) + right.astype(jnp.float32)).astype(left.dtype)]
    all_to_all x6 -> x3, starting transfers between devices: 29 us -> 11.6 us  [to_all(): return lax.all_to_all(values, BOTH, split_axis=0, concat_axis=0, tiled=True)]
  transfers between devices with their start and end apart: 138 -> 108, of which waited for: 47 -> 22; matrix products, arithmetic and copies ran while one was open for 31% -> 11% of each run, Pallas kernels for 21% -> 40%
where the time goes in v2:
time: 910 us; the launch traced here: 901 us
  Pallas kernels  447 us (49%)
  waiting for transfers between devices  181 us (20%)
  starting transfers between devices  135 us (15%)
  local copies, waits for them, and re-layouts  80.3 us (9%)
  other arithmetic  52.6 us (6%)
    pallas_call x12, Pallas kernels, expert_call(): pl.pallas_call(functools.partial(kernel, carried=len(kept) + 1), grid=(ow...  221 us
    ppermute x85, waiting for transfers between devices, swap(): return lax.ppermute(values, 'ctx', [(i, i ^ bit) for i in range(count)])  126 us
    pallas_call x22, Pallas kernels, stage(): pl.pallas_call(kernel, in_specs=[far] * first + [near] * len(taken), out_...  96.8 us
    ppermute x85, starting transfers between devices, swap(): return lax.ppermute(values, 'ctx', [(i, i ^ bit) for i in range(count)])  84.3 us
    pallas_call x2, Pallas kernels, attend_call(): pl.pallas_call(kernel, in_specs=[pl.BlockSpec(memory_space=pltpu.SMEM)] +...  51.3 us
    ppermute x18, waiting for transfers between devices, turn(): lax.ppermute(values, 'fsdp', [(i, (i + step) % count) for i in range(coun...  50 us
    pallas_call x3, Pallas kernels, rows_grad(): pl.pallas_call(rows_kernel, grid=(count,), in_specs=[pl.BlockSpec((1, amo...  50 us
    ppermute x18, starting transfers between devices, turn(): lax.ppermute(values, 'fsdp', [(i, (i + step) % count) for i in range(coun...  32.3 us
  transfers between devices with their start and end apart: 108, of which 22 were waited for; matrix products, arithmetic and copies ran while one was open for 11% of the time, Pallas kernels for 40%

profile of v2, /device:TPU:0, one launch (start us, length us, event | category | flops | bytes accessed | tf_op | source)
XLA Modules:
  0.0 900.7 jit_solution(2455092377686445665)
XLA Ops:
  24.3 22.1 %collective-permute-done.2.refs_4_.refs_11_ = bf16[128,2048]{1,0:T(8,128)(2,1)} collective-permute-done((bf16[128,2048]{1,0:T(8,128)(2,1)S(1)}, bf16[128,2048]{1,0:T(8,128)(2,1)}, u32[]{:S(2)}, u32[]{:S(2)}) %collective-permute-start.2) | collective-permute-done | bytes 524320 | tf_op jit(solution)/shard_map/ppermute | solution.py:57
  46.4 10.1 %collective-permute-done.1.refs_3_.refs_6_ = bf16[144,2048]{1,0:T(8,128)(2,1)S(1)} collective-permute-done((bf16[144,2048]{1,0:T(8,128)(2,1)}, bf16[144,2048]{1,0:T(8,128)(2,1)S(1)}, u32[]{:S(2)}, u32[]{:S(2)}) %collective-permute-start.1) | collective-permute-done | bytes 589856 | tf_op jit(solution)/shard_map/ppermute | solution.py:62
  84.1 5.0 all-to-all-done.1
  90.4 4.8 shard_map.222
  99.2 23.8 %collective-permute-done.11.refs_1_.refs_10_.refs_16_ = bf16[8,64,1024]{2,1,0:T(8,128)(2,1)} collective-permute-done((bf16[8,64,1024]{2,1,0:T(8,128)(2,1)}, bf16[8,64,1024]{2,1,0:T(8,128)(2,1)}, u32[]{:S(2)}, u32[]{:S(2)}) %collective-permute-start.11) | collective-permute-done | bytes 1048608 | tf_op jit(solution)/shard_map/ppermute | solution.py:62
  132.0 12.3 %shard_map.224 = (bf16[4,640,2048]{2,1,0:T(8,128)(2,1)}, f32[4,640,704]{2,1,0:T(8,128)}, f32[1024,128]{1,0:T(8,128)}) custom-call(bf16[576,2048]{1,0:T(8,128)(2,1)} %get-tuple-element.228.refs_0_.ga_ref, bf16[576,2048]{1,0:T(8,128)(2,1)} %copy-done.3, f32[4,1024]{1,0:T(4,128)} %fusion.16.refs_2_.refs_5_.refs_3_, bf16[4,704,2048]{2,1,0:T(8,128)(2,1)} %refs_6_.15, ...), custom_call_target="tpu_custom_call" | custom-call | flops 3724541952 | bytes 20971520 | tf_op jit(solution)/shard_map/pallas_call | solution.py:752
  144.3 5.4 collective-permute-done.16.refs_2_.refs_11_.refs_17_
  170.3 22.5 %shard_map.226 = (bf16[512,2048]{1,0:T(8,128)(2,1)}, bf16[512,2048]{1,0:T(8,128)(2,1)}, bf16[1024,2048]{1,0:T(8,128)(2,1)}, bf16[1024,256]{1,0:T(8,128)(2,1)}, b...) custom-call(s32[1]{0:T(128)} %bitcast.11.refs_0_, ...), custom_call_target="tpu_custom_call" | custom-call | flops 5368709120 | bytes 30000000 | tf_op jit(solution)/shard_map/pallas_call | solution.py:663
  204.2 12.3 %shard_map.228 = (bf16[4,640,2048]{2,1,0:T(8,128)(2,1)}, f32[4,640,704]{2,1,0:T(8,128)}, f32[1024,128]{1,0:T(8,128)}) custom-call(bf16[576,2048]{1,0:T(8,128)(2,1)} %get-tuple-element.241.refs_0_.ga_ref, bf16[576,2048]{1,0:T(8,128)(2,1)} %copy-done.1, f32[4,1024]{1,0:T(4,128)} %fusion.18.refs_2_.refs_5_.refs_3_, ...), custom_call_target="tpu_custom_call", output_to_operand_aliasing={{0}: (5, {}), {1}: (6, {})} | custom-call | flops 3724541952 | bytes 20971520 | tf_op jit(solution)/shard_map/pallas_call | solution.py:752
  216.5 4.6 collective-permute-done.25.refs_5_
  222.0 6.5 shard_map.229
  240.0 22.7 %collective-permute-done.32.refs_6_ = bf16[80,2048]{1,0:T(8,128)(2,1)S(1)} collective-permute-done((bf16[80,2048]{1,0:T(8,128)(2,1)}, bf16[80,2048]{1,0:T(8,128)(2,1)S(1)}, u32[]{:S(2)}, u32[]{:S(2)}) %collective-permute-start.32) | collective-permute-done | bytes 327712 | tf_op jit(solution)/shard_map/ppermute | solution.py:57
  276.9 7.5 collective-permute-start.34
  292.9 12.3 %shard_map.231 = (bf16[4,640,2048]{2,1,0:T(8,128)(2,1)}, f32[4,640,704]{2,1,0:T(8,128)}, f32[1024,128]{1,0:T(8,128)}) custom-call(bf16[576,2048]{1,0:T(8,128)(2,1)} %get-tuple-element.251.refs_0_.ga_ref, bf16[576,2048]{1,0:T(8,128)(2,1)} %copy-done.2, ...), custom_call_target="tpu_custom_call", output_to_operand_aliasing={{0}: (5, {}), {1}: (6, {})} | custom-call | flops 3724541952 | bytes 20971520 | tf_op jit(solution)/shard_map/pallas_call | solution.py:752
  322.1 12.3 %shard_map.233 = (bf16[4,640,2048]{2,1,0:T(8,128)(2,1)}, f32[4,640,704]{2,1,0:T(8,128)}, f32[1024,128]{1,0:T(8,128)}) custom-call(bf16[576,2048]{1,0:T(8,128)(2,1)} %get-tuple-element.263.refs_0_.ga_ref, bf16[576,2048]{1,0:T(8,128)(2,1)} %copy-done, ...), custom_call_target="tpu_custom_call", output_to_operand_aliasing={{0}: (5, {}), {1}: (6, {})} | custom-call | flops 3724541952 | bytes 20971520 | tf_op jit(solution)/shard_map/pallas_call | solution.py:752
  334.4 8.3 collective-permute-done.42.refs_5_
  360.5 28.8 %shard_map.235 = (bf16[4,640,2048]{2,1,0:T(8,128)(2,1)}, bf16[4,640,704]{2,1,0:T(8,128)(2,1)}, bf16[4,640,1408]{2,1,0:T(8,128)(2,1)}, bf16[576,2048]{1,0:T(8,128...) custom-call(s32[2]{0:T(128)} %pad_add_fusion.refs_0_, ...), custom_call_target="tpu_custom_call" | custom-call | flops 12213813248 | bytes 36700160 | tf_op jit(solution)/shard_map/pallas_call | solution.py:752
  398.0 29.3 %shard_map.237 = (bf16[4,640,2048]{2,1,0:T(8,128)(2,1)}, bf16[4,640,704]{2,1,0:T(8,128)(2,1)}, bf16[4,640,1408]{2,1,0:T(8,128)(2,1)}, bf16[576,2048]{1,0:T(8,128...) custom-call(s32[2]{0:T(128)} %pad_add_fusion.refs_0_, ...), custom_call_target="tpu_custom_call", output_to_operand_aliasing={{0}: (10, {}), {1}: (11, {}), {2}: (12, {})} | custom-call | flops 12213813248 | bytes 36700160 | tf_op jit(solution)/shard_map/pallas_call | solution.py:752
  429.2 6.1 shard_map.238
  439.3 29.5 %shard_map.239 = (bf16[4,640,2048]{2,1,0:T(8,128)(2,1)}, bf16[4,640,704]{2,1,0:T(8,128)(2,1)}, bf16[4,640,1408]{2,1,0:T(8,128)(2,1)}, bf16[576,2048]{1,0:T(8,128...) custom-call(s32[2]{0:T(128)} %pad_add_fusion.refs_0_, ...), custom_call_target="tpu_custom_call", output_to_operand_aliasing={{0}: (10, {}), {1}: (11, {}), {2}: (12, {})} | custom-call | flops 12213813248 | bytes 36700160 | tf_op jit(solution)/shard_map/pallas_call | solution.py:752
  470.3 5.7 shard_map.240
  479.6 29.3 %shard_map.241 = (bf16[4,640,2048]{2,1,0:T(8,128)(2,1)}, bf16[4,640,704]{2,1,0:T(8,128)(2,1)}, bf16[4,640,1408]{2,1,0:T(8,128)(2,1)}, bf16[576,2048]{1,0:T(8,128...) custom-call(s32[2]{0:T(128)} %pad_add_fusion.refs_0_, ...), custom_call_target="tpu_custom_call", output_to_operand_aliasing={{0}: (10, {}), {1}: (11, {}), {2}: (12, {})} | custom-call | flops 12213813248 | bytes 36700160 | tf_op jit(solution)/shard_map/pallas_call | solution.py:752
  510.5 5.8 shard_map.242
  520.7 13.8 %shard_map.243 = (bf16[4,640,2048]{2,1,0:T(8,128)(2,1)}, bf16[512,2048]{1,0:T(8,128)(2,1)}, bf16[512,2048]{1,0:T(8,128)(2,1)}) custom-call(s32[2]{0:T(128)} %pad_add_fusion.refs_0_, bf16[4,640,704]{2,1,0:T(8,128)(2,1)} %get-tuple-element.313.refs_1_.left_ref, bf16[4,640,2048]{2,1,0:T(8,128)(2,1)} %get-tuple-element.314.refs_2_, ...), custom_call_target="tpu_custom_call" | custom-call | flops 3724541952 | bytes 20971520 | tf_op jit(solution)/shard_map/pallas_call | solution.py:752
  534.6 12.2 %collective-permute-done.65.refs_5_ = bf16[144,2048]{1,0:T(8,128)(2,1)} collective-permute-done((bf16[144,2048]{1,0:T(8,128)(2,1)}, bf16[144,2048]{1,0:T(8,128)(2,1)}, u32[]{:S(2)}, u32[]{:S(2)}) %collective-permute-start.65) | collective-permute-done | bytes 589856 | tf_op jit(solution)/shard_map/ppermute | solution.py:57
  548.2 5.8 shard_map.244
  561.1 13.5 %shard_map.245 = (bf16[4,640,2048]{2,1,0:T(8,128)(2,1)}, bf16[512,2048]{1,0:T(8,128)(2,1)}, bf16[512,2048]{1,0:T(8,128)(2,1)}) custom-call(s32[2]{0:T(128)} %pad_add_fusion.refs_0_, bf16[4,640,704]{2,1,0:T(8,128)(2,1)} %get-tuple-element.313.refs_1_.left_ref, bf16[4,640,2048]{2,1,0:T(8,128)(2,1)} %get-tuple-element.314.refs_2_, ...), custom_call_target="tpu_custom_call", output_to_operand_aliasing={{0}: (8, {})} | custom-call | flops 3724541952 | bytes 20971520 | tf_op jit(solution)/shard_map/pallas_call | solution.py:752
  574.7 11.7 %collective-permute-done.70.refs_5_ = bf16[144,2048]{1,0:T(8,128)(2,1)} collective-permute-done((bf16[144,2048]{1,0:T(8,128)(2,1)}, bf16[144,2048]{1,0:T(8,128)(2,1)}, u32[]{:S(2)}, u32[]{:S(2)}) %collective-permute-start.70) | collective-permute-done | bytes 589856 | tf_op jit(solution)/shard_map/ppermute | solution.py:57
  587.7 5.5 shard_map.246
  598.7 13.6 %shard_map.247 = (bf16[4,640,2048]{2,1,0:T(8,128)(2,1)}, bf16[512,2048]{1,0:T(8,128)(2,1)}, bf16[512,2048]{1,0:T(8,128)(2,1)}) custom-call(s32[2]{0:T(128)} %pad_add_fusion.refs_0_, bf16[4,640,704]{2,1,0:T(8,128)(2,1)} %get-tuple-element.313.refs_1_.left_ref, bf16[4,640,2048]{2,1,0:T(8,128)(2,1)} %get-tuple-element.314.refs_2_, ...), custom_call_target="tpu_custom_call", output_to_operand_aliasing={{0}: (8, {})} | custom-call | flops 3724541952 | bytes 20971520 | tf_op jit(solution)/shard_map/pallas_call | solution.py:752
  612.5 9.5 %collective-permute-done.75.refs_5_ = bf16[128,2048]{1,0:T(8,128)(2,1)} collective-permute-done((bf16[128,2048]{1,0:T(8,128)(2,1)}, bf16[128,2048]{1,0:T(8,128)(2,1)}, u32[]{:S(2)}, u32[]{:S(2)}) %collective-permute-start.75) | collective-permute-done | bytes 524320 | tf_op jit(solution)/shard_map/ppermute | solution.py:57
  622.0 5.4 shard_map.248
  636.9 14.0 %shard_map.249 = (bf16[4,640,2048]{2,1,0:T(8,128)(2,1)}, bf16[512,2048]{1,0:T(8,128)(2,1)}, bf16[512,2048]{1,0:T(8,128)(2,1)}) custom-call(s32[2]{0:T(128)} %pad_add_fusion.refs_0_, bf16[4,640,704]{2,1,0:T(8,128)(2,1)} %get-tuple-element.313.refs_1_.left_ref, bf16[4,640,2048]{2,1,0:T(8,128)(2,1)} %get-tuple-element.314.refs_2_, ...), custom_call_target="tpu_custom_call", output_to_operand_aliasing={{0}: (8, {})} | custom-call | flops 3724541952 | bytes 20971520 | tf_op jit(solution)/shard_map/pallas_call | solution.py:752
  651.5 6.3 collective-permute-done.79.refs_4_
  658.6 5.8 shard_map.250
  664.9 6.9 shard_map.254
  671.8 7.0 shard_map.253
  678.8 7.0 shard_map.252
  685.8 7.0 shard_map.251
  706.5 10.8 %collective-permute-done.86.refs_7_ = bf16[128,2048]{1,0:T(8,128)(2,1)S(1)} collective-permute-done((bf16[128,2048]{1,0:T(8,128)(2,1)}, bf16[128,2048]{1,0:T(8,128)(2,1)S(1)}, u32[]{:S(2)}, u32[]{:S(2)}) %collective-permute-start.86) | collective-permute-done | bytes 524320 | tf_op jit(solution)/shard_map/ppermute | solution.py:57
  718.1 5.3 shard_map.255
  735.5 28.8 %shard_map.256 = (bf16[512,2048]{1,0:T(8,128)(2,1)}, bf16[512,2048]{1,0:T(8,128)(2,1)}, bf16[8,64,1024]{2,1,0:T(8,128)(2,1)}, bf16[8,64,1024]{2,1,0:T(8,128)(2,1...) custom-call(s32[1]{0:T(128)} %bitcast.11.refs_0_, bf16[512,2048]{1,0:T(8,128)(2,1)} %get-tuple-element.374.refs_1_, ...), custom_call_target="tpu_custom_call" | custom-call | flops 11274289152 | bytes 30000000 | tf_op jit(solution)/shard_map/pallas_call | solution.py:663
  776.5 7.7 collective-permute-done.95.refs_7_
  786.0 16.7 %shard_map.258.refs_1_ = f32[4,2048,1408]{2,1,0:T(8,128)} custom-call(bf16[4,640,2048]{2,1,0:T(8,128)(2,1)} %get-tuple-element.399.left_ref, bf16[4,640,1408]{2,1,0:T(8,128)(2,1)} %get-tuple-element.400.right_ref, f32[8,128]{1,0:T(8,128)} %get-tuple-element.398.refs_0_), custom_call_target="tpu_custom_call" | custom-call | flops 7381975040 | bytes 23068672 | tf_op jit(solution)/shard_map/pallas_call | solution.py:879
  802.7 7.9 collective-permute-done.92.refs_2_
  811.4 6.6 shard_map.259
  822.5 16.7 %shard_map.260.refs_1_ = f32[4,2048,1408]{2,1,0:T(8,128)} custom-call(bf16[4,640,2048]{2,1,0:T(8,128)(2,1)} %get-tuple-element.399.left_ref, bf16[4,640,1408]{2,1,0:T(8,128)(2,1)} %get-tuple-element.400.right_ref, f32[4,2048,1408]{2,1,0:T(8,128)} %get-tuple-element.412.refs_0_, ...), custom_call_target="tpu_custom_call", output_to_operand_aliasing={{}: (2, {})} | custom-call | flops 7381975040 | bytes 23068672 | tf_op jit(solution)/shard_map/pallas_call | solution.py:879
  854.3 16.6 %shard_map.262.refs_1_ = f32[4,704,2048]{2,1,0:T(8,128)} custom-call(bf16[4,640,704]{2,1,0:T(8,128)(2,1)} %get-tuple-element.313.refs_1_.left_ref, bf16[4,640,2048]{2,1,0:T(8,128)(2,1)} %get-tuple-element.421.right_ref, f32[8,128]{1,0:T(8,128)} %get-tuple-element.420.refs_0_), custom_call_target="tpu_custom_call" | custom-call | flops 7381975040 | bytes 23068672 | tf_op jit(solution)/shard_map/pallas_call | solution.py:879
  (527 shorter events, 309.1 us)
Async XLA Ops:
  7.1 49.4 %all-to-all-start = ((bf16[8,64,768]{2,1,0:T(8,128)(2,1)}), bf16[8,64,768]{2,1,0:T(8,128)(2,1)S(1)}, u32[]{:S(2)}, u32[]{:S(2)}) async-start(bf16[8,64,768]{2,1,0:T(8,128)(2,1)} %reshape.379), calls=%async_computation | async-start | bytes 1572864 | tf_op jit(solution)/shard_map/all_to_all | solution.py:955
  11.9 34.5 %collective-permute-start.5 = (bf16[144,2048]{1,0:T(8,128)(2,1)}, bf16[144,2048]{1,0:T(8,128)(2,1)}, u32[]{:S(2)}, u32[]{:S(2)}) collective-permute-start(bf16[144,2048]{1,0:T(8,128)(2,1)} %fusion.7.refs_15_), channel_id=1, source_target_pairs={{0,16},{4,20},{8,24},{12,28},{16,0},{20,4},{24,8},{28,12},{1,17},{... | collective-permute-start | bytes 1769480 | tf_op jit(solution)/shard_map/ppermute | solution.py:57
  13.8 32.6 %collective-permute-start.4 = (bf16[144,2048]{1,0:T(8,128)(2,1)}, bf16[144,2048]{1,0:T(8,128)(2,1)}, u32[]{:S(2)}, u32[]{:S(2)}) collective-permute-start(bf16[144,2048]{1,0:T(8,128)(2,1)} %fusion.7.refs_15_), channel_id=1, source_target_pairs={{0,8},{4,12},{8,0},{12,4},{16,24},{20,28},{24,16},{28,20},{1,9},{5... | collective-permute-start | bytes 1769480 | tf_op jit(solution)/shard_map/ppermute | solution.py:57
  15.3 41.2 %collective-permute-start.1 = (bf16[144,2048]{1,0:T(8,128)(2,1)}, bf16[144,2048]{1,0:T(8,128)(2,1)S(1)}, u32[]{:S(2)}, u32[]{:S(2)}) collective-permute-start(bf16[144,2048]{1,0:T(8,128)(2,1)} %fusion.7.refs_15_), channel_id=1, source_target_pairs={{0,2},{1,3},{2,0},{3,1},{4,6},{5,7},{6,4},{7,5},{8,10},{9,11},{10,... | collective-permute-start | bytes 1769480 | tf_op jit(solution)/shard_map/ppermute | solution.py:62
  17.9 38.6 %collective-permute-start = (bf16[144,2048]{1,0:T(8,128)(2,1)}, bf16[144,2048]{1,0:T(8,128)(2,1)S(1)}, u32[]{:S(2)}, u32[]{:S(2)}) collective-permute-start(bf16[144,2048]{1,0:T(8,128)(2,1)} %fusion.7.refs_15_), channel_id=1, source_target_pairs={{0,1},{1,2},{2,3},{3,0},{4,5},{5,6},{6,7},{7,4},{8,9},{9,10},{10,1... | collective-permute-start | bytes 1769480 | tf_op jit(solution)/shard_map/ppermute | solution.py:62
  153.7 39.8 %collective-permute-start.19 = (bf16[576,2048]{1,0:T(8,128)(2,1)}, bf16[576,2048]{1,0:T(8,128)(2,1)S(1)}, u32[]{:S(2)}, u32[]{:S(2)}) collective-permute-start(bf16[576,2048]{1,0:T(8,128)(2,1)} %get-tuple-element.241.refs_0_.ga_ref), channel_id=1, source_target_pairs={{0,4},{4,0},{8,12},{12,8},{16,20},{20,16},{24,28},{28,24},{1,5},{5... | collective-permute-start | bytes 7077896 | tf_op jit(solution)/shard_map/ppermute | solution.py:57
  157.8 35.7 %all-to-all-start.2 = ((bf16[32,64,176]{2,1,0:T(8,128)(2,1)}), bf16[32,64,176]{2,1,0:T(8,128)(2,1)}, u32[]{:S(2)}, u32[]{:S(2)}) async-start(bf16[32,64,176]{2,1,0:T(8,128)(2,1)} %broadcast_add_fusion.1), calls=%async_computation.2 | async-start | bytes 2097152 | tf_op jit(solution)/shard_map/all_to_all | solution.py:210
  161.4 31.4 %collective-permute-start.22 = (bf16[144,2048]{1,0:T(8,128)(2,1)}, bf16[144,2048]{1,0:T(8,128)(2,1)}, u32[]{:S(2)}, u32[]{:S(2)}) collective-permute-start(bf16[144,2048]{1,0:T(8,128)(2,1)} %copy-done.24), channel_id=1, source_target_pairs={{0,16},{4,20},{8,24},{12,28},{16,0},{20,4},{24,8},{28,12},{1,17},{... | collective-permute-start | bytes 1769480 | tf_op jit(solution)/shard_map/ppermute | solution.py:57
  228.4 34.3 %collective-permute-start.28 = (bf16[576,2048]{1,0:T(8,128)(2,1)}, bf16[576,2048]{1,0:T(8,128)(2,1)S(1)}, u32[]{:S(2)}, u32[]{:S(2)}) collective-permute-start(bf16[576,2048]{1,0:T(8,128)(2,1)} %get-tuple-element.251.refs_0_.ga_ref), channel_id=1, source_target_pairs={{0,4},{4,0},{8,12},{12,8},{16,20},{20,16},{24,28},{28,24},{1,5},{5... | collective-permute-start | bytes 7077896 | tf_op jit(solution)/shard_map/ppermute | solution.py:57
  230.0 32.8 %collective-permute-start.29 = (bf16[128,2048]{1,0:T(8,128)(2,1)}, bf16[128,2048]{1,0:T(8,128)(2,1)S(1)}, u32[]{:S(2)}, u32[]{:S(2)}) collective-permute-start(bf16[128,2048]{1,0:T(8,128)(2,1)} %get-tuple-element.252), channel_id=1, source_target_pairs={{0,8},{4,12},{8,0},{12,4},{16,24},{20,28},{24,16},{28,20},{1,9},{5... | collective-permute-start | bytes 1572872 | tf_op jit(solution)/shard_map/ppermute | solution.py:57
  230.5 32.2 %collective-permute-start.30 = (bf16[128,2048]{1,0:T(8,128)(2,1)}, bf16[128,2048]{1,0:T(8,128)(2,1)S(1)}, u32[]{:S(2)}, u32[]{:S(2)}) collective-permute-start(bf16[128,2048]{1,0:T(8,128)(2,1)} %get-tuple-element.253), channel_id=1, source_target_pairs={{0,16},{4,20},{8,24},{12,28},{16,0},{20,4},{24,8},{28,12},{1,17},{... | collective-permute-start | bytes 1572872 | tf_op jit(solution)/shard_map/ppermute | solution.py:57
  232.0 30.7 %collective-permute-start.31 = (bf16[128,2048]{1,0:T(8,128)(2,1)}, bf16[128,2048]{1,0:T(8,128)(2,1)S(1)}, u32[]{:S(2)}, u32[]{:S(2)}) collective-permute-start(bf16[128,2048]{1,0:T(8,128)(2,1)} %get-tuple-element.254), channel_id=1, source_target_pairs={{0,24},{4,28},{8,16},{12,20},{16,8},{20,12},{24,0},{28,4},{1,25},{... | collective-permute-start | bytes 1572872 | tf_op jit(solution)/shard_map/ppermute | solution.py:57
  273.4 31.8 %collective-permute-start.38 = (bf16[128,2048]{1,0:T(8,128)(2,1)S(1)}, bf16[128,2048]{1,0:T(8,128)(2,1)}, u32[]{:S(2)}, u32[]{:S(2)}) collective-permute-start(bf16[128,2048]{1,0:T(8,128)(2,1)S(1)} %multiply_convert_fusion.refs_7_), channel_id=1, source_target_pairs={{0,24},{4,28},{8,16},{12,20},{16,8},{20,12},{24,0},{28,4},{1,25},{... | collective-permute-start | bytes 1572872 | tf_op jit(solution)/shard_map/ppermute | solution.py:57
  308.4 34.3 %collective-permute-start.39 = (bf16[512,2048]{1,0:T(8,128)(2,1)}, bf16[512,2048]{1,0:T(8,128)(2,1)S(1)}, u32[]{:S(2)}, u32[]{:S(2)}) collective-permute-start(bf16[512,2048]{1,0:T(8,128)(2,1)} %get-tuple-element.268.refs_1_.xa_ref), channel_id=1, source_target_pairs={{0,4},{4,0},{8,12},{12,8},{16,20},{20,16},{24,28},{28,24},{1,5},{5... | collective-permute-start | bytes 6291464 | tf_op jit(solution)/shard_map/ppermute | solution.py:57
  347.3 42.1 %collective-permute-start.44 = (bf16[512,2048]{1,0:T(8,128)(2,1)}, bf16[512,2048]{1,0:T(8,128)(2,1)S(1)}, u32[]{:S(2)}, u32[]{:S(2)}) collective-permute-start(bf16[512,2048]{1,0:T(8,128)(2,1)} %get-tuple-element.274.refs_1_.xa_ref), channel_id=1, source_target_pairs={{0,4},{4,0},{8,12},{12,8},{16,20},{20,16},{24,28},{28,24},{1,5},{5... | collective-permute-start | bytes 6291464 | tf_op jit(solution)/shard_map/ppermute | solution.py:57
  348.0 41.4 %collective-permute-start.48 = (bf16[128,2048]{1,0:T(8,128)(2,1)}, bf16[128,2048]{1,0:T(8,128)(2,1)}, u32[]{:S(2)}, u32[]{:S(2)}) collective-permute-start(bf16[128,2048]{1,0:T(8,128)(2,1)} %copy-done.39), channel_id=1, source_target_pairs={{0,24},{4,28},{8,16},{12,20},{16,8},{20,12},{24,0},{28,4},{1,25},{... | collective-permute-start | bytes 1572872 | tf_op jit(solution)/shard_map/ppermute | solution.py:57
  349.7 39.7 %collective-permute-start.47 = (bf16[128,2048]{1,0:T(8,128)(2,1)}, bf16[128,2048]{1,0:T(8,128)(2,1)}, u32[]{:S(2)}, u32[]{:S(2)}) collective-permute-start(bf16[128,2048]{1,0:T(8,128)(2,1)} %copy-done.39), channel_id=1, source_target_pairs={{0,16},{4,20},{8,24},{12,28},{16,0},{20,4},{24,8},{28,12},{1,17},{... | collective-permute-start | bytes 1572872 | tf_op jit(solution)/shard_map/ppermute | solution.py:57
  351.0 38.5 %collective-permute-start.46 = (bf16[128,2048]{1,0:T(8,128)(2,1)}, bf16[128,2048]{1,0:T(8,128)(2,1)}, u32[]{:S(2)}, u32[]{:S(2)}) collective-permute-start(bf16[128,2048]{1,0:T(8,128)(2,1)} %copy-done.39), channel_id=1, source_target_pairs={{0,8},{4,12},{8,0},{12,4},{16,24},{20,28},{24,16},{28,20},{1,9},{5... | collective-permute-start | bytes 1572872 | tf_op jit(solution)/shard_map/ppermute | solution.py:57
  351.5 37.9 %collective-permute-start.45 = (bf16[128,2048]{1,0:T(8,128)(2,1)}, bf16[128,2048]{1,0:T(8,128)(2,1)S(1)}, u32[]{:S(2)}, u32[]{:S(2)}) collective-permute-start(bf16[128,2048]{1,0:T(8,128)(2,1)} %copy-done.39), channel_id=1, source_target_pairs={{0,1},{1,2},{2,3},{3,0},{4,5},{5,6},{6,7},{7,4},{8,9},{9,10},{10,1... | collective-permute-start | bytes 1572872 | tf_op jit(solution)/shard_map/ppermute | solution.py:62
  394.0 33.4 %collective-permute-start.53 = (bf16[576,2048]{1,0:T(8,128)(2,1)}, bf16[576,2048]{1,0:T(8,128)(2,1)}, u32[]{:S(2)}, u32[]{:S(2)}) collective-permute-start(bf16[576,2048]{1,0:T(8,128)(2,1)} %get-tuple-element.283), channel_id=1, source_target_pairs={{0,4},{4,0},{8,12},{12,8},{16,20},{20,16},{24,28},{28,24},{1,5},{5... | collective-permute-start | bytes 7077896 | tf_op jit(solution)/shard_map/ppermute | solution.py:57
  394.0 33.4 %collective-permute-start.49 = (bf16[512,2048]{1,0:T(8,128)(2,1)}, bf16[512,2048]{1,0:T(8,128)(2,1)S(1)}, u32[]{:S(2)}, u32[]{:S(2)}) collective-permute-start(bf16[512,2048]{1,0:T(8,128)(2,1)} %get-tuple-element.282.refs_1_.xa_ref), channel_id=1, source_target_pairs={{0,4},{4,0},{8,12},{12,8},{16,20},{20,16},{24,28},{28,24},{1,5},{5... | collective-permute-start | bytes 6291464 | tf_op jit(solution)/shard_map/ppermute | solution.py:57
  394.5 32.8 %collective-permute-start.52 = (bf16[128,2048]{1,0:T(8,128)(2,1)}, bf16[128,2048]{1,0:T(8,128)(2,1)S(1)}, u32[]{:S(2)}, u32[]{:S(2)}) collective-permute-start(bf16[128,2048]{1,0:T(8,128)(2,1)} %copy-done.38), channel_id=1, source_target_pairs={{0,24},{4,28},{8,16},{12,20},{16,8},{20,12},{24,0},{28,4},{1,25},{... | collective-permute-start | bytes 1572872 | tf_op jit(solution)/shard_map/ppermute | solution.py:57
  396.2 31.2 %collective-permute-start.51 = (bf16[128,2048]{1,0:T(8,128)(2,1)}, bf16[128,2048]{1,0:T(8,128)(2,1)S(1)}, u32[]{:S(2)}, u32[]{:S(2)}) collective-permute-start(bf16[128,2048]{1,0:T(8,128)(2,1)} %copy-done.38), channel_id=1, source_target_pairs={{0,16},{4,20},{8,24},{12,28},{16,0},{20,4},{24,8},{28,12},{1,17},{... | collective-permute-start | bytes 1572872 | tf_op jit(solution)/shard_map/ppermute | solution.py:57
  435.3 33.6 %collective-permute-start.58 = (bf16[576,2048]{1,0:T(8,128)(2,1)}, bf16[576,2048]{1,0:T(8,128)(2,1)}, u32[]{:S(2)}, u32[]{:S(2)}) collective-permute-start(bf16[576,2048]{1,0:T(8,128)(2,1)} %get-tuple-element.297), channel_id=1, source_target_pairs={{0,4},{4,0},{8,12},{12,8},{16,20},{20,16},{24,28},{28,24},{1,5},{5... | collective-permute-start | bytes 7077896 | tf_op jit(solution)/shard_map/ppermute | solution.py:57
  435.3 33.5 %collective-permute-start.54 = (bf16[512,2048]{1,0:T(8,128)(2,1)}, bf16[512,2048]{1,0:T(8,128)(2,1)S(1)}, u32[]{:S(2)}, u32[]{:S(2)}) collective-permute-start(bf16[512,2048]{1,0:T(8,128)(2,1)} %get-tuple-element.292.refs_1_.xa_ref), channel_id=1, source_target_pairs={{0,4},{4,0},{8,12},{12,8},{16,20},{20,16},{24,28},{28,24},{1,5},{5... | collective-permute-start | bytes 6291464 | tf_op jit(solution)/shard_map/ppermute | solution.py:57
  435.8 33.0 %collective-permute-start.55 = (bf16[144,2048]{1,0:T(8,128)(2,1)}, bf16[144,2048]{1,0:T(8,128)(2,1)S(1)}, u32[]{:S(2)}, u32[]{:S(2)}) collective-permute-start(bf16[144,2048]{1,0:T(8,128)(2,1)} %get-tuple-element.293), channel_id=1, source_target_pairs={{0,8},{4,12},{8,0},{12,4},{16,24},{20,28},{24,16},{28,20},{1,9},{5... | collective-permute-start | bytes 1769480 | tf_op jit(solution)/shard_map/ppermute | solution.py:57
  437.3 31.5 %collective-permute-start.56 = (bf16[144,2048]{1,0:T(8,128)(2,1)}, bf16[144,2048]{1,0:T(8,128)(2,1)}, u32[]{:S(2)}, u32[]{:S(2)}) collective-permute-start(bf16[144,2048]{1,0:T(8,128)(2,1)} %get-tuple-element.294), channel_id=1, source_target_pairs={{0,16},{4,20},{8,24},{12,28},{16,0},{20,4},{24,8},{28,12},{1,17},{... | collective-permute-start | bytes 1769480 | tf_op jit(solution)/shard_map/ppermute | solution.py:57
  438.0 30.8 %collective-permute-start.57 = (bf16[144,2048]{1,0:T(8,128)(2,1)}, bf16[144,2048]{1,0:T(8,128)(2,1)}, u32[]{:S(2)}, u32[]{:S(2)}) collective-permute-start(bf16[144,2048]{1,0:T(8,128)(2,1)} %get-tuple-element.295), channel_id=1, source_target_pairs={{0,24},{4,28},{8,16},{12,20},{16,8},{20,12},{24,0},{28,4},{1,25},{... | collective-permute-start | bytes 1769480 | tf_op jit(solution)/shard_map/ppermute | solution.py:57
  476.1 32.8 %collective-permute-start.62 = (bf16[576,2048]{1,0:T(8,128)(2,1)}, bf16[576,2048]{1,0:T(8,128)(2,1)S(1)}, u32[]{:S(2)}, u32[]{:S(2)}) collective-permute-start(bf16[576,2048]{1,0:T(8,128)(2,1)} %get-tuple-element.310), channel_id=1, source_target_pairs={{0,4},{4,0},{8,12},{12,8},{16,20},{20,16},{24,28},{28,24},{1,5},{5... | collective-permute-start | bytes 7077896 | tf_op jit(solution)/shard_map/ppermute | solution.py:57
  476.1 32.8 %collective-permute-start.59 = (bf16[144,2048]{1,0:T(8,128)(2,1)}, bf16[144,2048]{1,0:T(8,128)(2,1)S(1)}, u32[]{:S(2)}, u32[]{:S(2)}) collective-permute-start(bf16[144,2048]{1,0:T(8,128)(2,1)} %get-tuple-element.306), channel_id=1, source_target_pairs={{0,8},{4,12},{8,0},{12,4},{16,24},{20,28},{24,16},{28,20},{1,9},{5... | collective-permute-start | bytes 1769480 | tf_op jit(solution)/shard_map/ppermute | solution.py:57
  477.6 31.3 %collective-permute-start.60 = (bf16[144,2048]{1,0:T(8,128)(2,1)}, bf16[144,2048]{1,0:T(8,128)(2,1)}, u32[]{:S(2)}, u32[]{:S(2)}) collective-permute-start(bf16[144,2048]{1,0:T(8,128)(2,1)} %get-tuple-element.307), channel_id=1, source_target_pairs={{0,16},{4,20},{8,24},{12,28},{16,0},{20,4},{24,8},{28,12},{1,17},{... | collective-permute-start | bytes 1769480 | tf_op jit(solution)/shard_map/ppermute | solution.py:57
  478.3 30.6 %collective-permute-start.61 = (bf16[144,2048]{1,0:T(8,128)(2,1)}, bf16[144,2048]{1,0:T(8,128)(2,1)}, u32[]{:S(2)}, u32[]{:S(2)}) collective-permute-start(bf16[144,2048]{1,0:T(8,128)(2,1)} %get-tuple-element.308), channel_id=1, source_target_pairs={{0,24},{4,28},{8,16},{12,20},{16,8},{20,12},{24,0},{28,4},{1,25},{... | collective-permute-start | bytes 1769480 | tf_op jit(solution)/shard_map/ppermute | solution.py:57
  516.2 30.6 %collective-permute-start.67 = (bf16[576,2048]{1,0:T(8,128)(2,1)}, bf16[576,2048]{1,0:T(8,128)(2,1)S(1)}, u32[]{:S(2)}, u32[]{:S(2)}) collective-permute-start(bf16[576,2048]{1,0:T(8,128)(2,1)} %get-tuple-element.324), channel_id=1, source_target_pairs={{0,4},{4,0},{8,12},{12,8},{16,20},{20,16},{24,28},{28,24},{1,5},{5... | collective-permute-start | bytes 7077896 | tf_op jit(solution)/shard_map/ppermute | solution.py:57
  554.0 32.4 %collective-permute-start.72 = (bf16[512,2048]{1,0:T(8,128)(2,1)}, bf16[512,2048]{1,0:T(8,128)(2,1)S(1)}, u32[]{:S(2)}, u32[]{:S(2)}) collective-permute-start(bf16[512,2048]{1,0:T(8,128)(2,1)} %get-tuple-element.337), channel_id=1, source_target_pairs={{0,4},{4,0},{8,12},{12,8},{16,20},{20,16},{24,28},{28,24},{1,5},{5... | collective-permute-start | bytes 6291464 | tf_op jit(solution)/shard_map/ppermute | solution.py:57
  627.4 31.2 %collective-permute-start.81 = (bf16[512,2048]{1,0:T(8,128)(2,1)}, bf16[512,2048]{1,0:T(8,128)(2,1)}, u32[]{:S(2)}, u32[]{:S(2)}) collective-permute-start(bf16[512,2048]{1,0:T(8,128)(2,1)} %get-tuple-element.359), channel_id=1, source_target_pairs={{0,4},{4,0},{8,12},{12,8},{16,20},{20,16},{24,28},{28,24},{1,5},{5... | collective-permute-start | bytes 6291464 | tf_op jit(solution)/shard_map/ppermute | solution.py:57
  634.9 67.3 %collective-permute-start.83 = (bf16[128,2048]{1,0:T(8,128)(2,1)}, bf16[128,2048]{1,0:T(8,128)(2,1)}, u32[]{:S(2)}, u32[]{:S(2)}) collective-permute-start(bf16[128,2048]{1,0:T(8,128)(2,1)} %get-tuple-element.375), channel_id=1, source_target_pairs={{0,1},{1,2},{2,3},{3,0},{4,5},{5,6},{6,7},{7,4},{8,9},{9,10},{10,1... | collective-permute-start | bytes 1572872 | tf_op jit(solution)/shard_map/ppermute | solution.py:62
  650.9 55.6 %collective-permute-start.84 = (bf16[128,2048]{1,0:T(8,128)(2,1)}, bf16[128,2048]{1,0:T(8,128)(2,1)}, u32[]{:S(2)}, u32[]{:S(2)}) collective-permute-start(bf16[128,2048]{1,0:T(8,128)(2,1)} %get-tuple-element.376), channel_id=1, source_target_pairs={{0,8},{4,12},{8,0},{12,4},{16,24},{20,28},{24,16},{28,20},{1,9},{5... | collective-permute-start | bytes 1572872 | tf_op jit(solution)/shard_map/ppermute | solution.py:57
  657.8 48.7 %collective-permute-start.85 = (bf16[128,2048]{1,0:T(8,128)(2,1)}, bf16[128,2048]{1,0:T(8,128)(2,1)}, u32[]{:S(2)}, u32[]{:S(2)}) collective-permute-start(bf16[128,2048]{1,0:T(8,128)(2,1)} %get-tuple-element.377), channel_id=1, source_target_pairs={{0,16},{4,20},{8,24},{12,28},{16,0},{20,4},{24,8},{28,12},{1,17},{... | collective-permute-start | bytes 1572872 | tf_op jit(solution)/shard_map/ppermute | solution.py:57
  664.4 52.9 %collective-permute-start.87 = (bf16[512,2048]{1,0:T(8,128)(2,1)}, bf16[512,2048]{1,0:T(8,128)(2,1)}, u32[]{:S(2)}, u32[]{:S(2)}) collective-permute-start(bf16[512,2048]{1,0:T(8,128)(2,1)} %get-tuple-element.380), channel_id=1, source_target_pairs={{0,4},{4,0},{8,12},{12,8},{16,20},{20,16},{24,28},{28,24},{1,5},{5... | collective-permute-start | bytes 6291464 | tf_op jit(solution)/shard_map/ppermute | solution.py:57
  664.5 52.8 %collective-permute-start.82 = (bf16[512,2048]{1,0:T(8,128)(2,1)}, bf16[512,2048]{1,0:T(8,128)(2,1)}, u32[]{:S(2)}, u32[]{:S(2)}) collective-permute-start(bf16[512,2048]{1,0:T(8,128)(2,1)} %get-tuple-element.374.refs_1_), channel_id=1, source_target_pairs={{0,4},{4,0},{8,12},{12,8},{16,20},{20,16},{24,28},{28,24},{1,5},{5... | collective-permute-start | bytes 6291464 | tf_op jit(solution)/shard_map/ppermute | solution.py:57
  723.4 42.0 %all-to-all-start.3 = ((bf16[32,64,256]{2,1,0:T(8,128)(2,1)}), bf16[32,64,256]{2,1,0:T(8,128)(2,1)S(1)}, u32[]{:S(2)}, u32[]{:S(2)}) async-start(bf16[32,64,256]{2,1,0:T(8,128)(2,1)} %get-tuple-element.392), calls=%async_computation.3 | async-start | bytes 2097152 | tf_op jit(solution)/shard_map/all_to_all | solution.py:210
  727.9 36.4 %collective-permute-start.89 = (bf16[128,2048]{1,0:T(8,128)(2,1)}, bf16[128,2048]{1,0:T(8,128)(2,1)S(1)}, u32[]{:S(2)}, u32[]{:S(2)}) collective-permute-start(bf16[128,2048]{1,0:T(8,128)(2,1)} %get-tuple-element.394), channel_id=1, source_target_pairs={{0,8},{4,12},{8,0},{12,4},{16,24},{20,28},{24,16},{28,20},{1,9},{5... | collective-permute-start | bytes 1572872 | tf_op jit(solution)/shard_map/ppermute | solution.py:57
  729.7 34.6 %collective-permute-start.90 = (bf16[128,2048]{1,0:T(8,128)(2,1)}, bf16[128,2048]{1,0:T(8,128)(2,1)}, u32[]{:S(2)}, u32[]{:S(2)}) collective-permute-start(bf16[128,2048]{1,0:T(8,128)(2,1)} %get-tuple-element.395), channel_id=1, source_target_pairs={{0,16},{4,20},{8,24},{12,28},{16,0},{20,4},{24,8},{28,12},{1,17},{... | collective-permute-start | bytes 1572872 | tf_op jit(solution)/shard_map/ppermute | solution.py:57
  731.2 34.3 %collective-permute-start.91 = (bf16[128,2048]{1,0:T(8,128)(2,1)}, bf16[128,2048]{1,0:T(8,128)(2,1)}, u32[]{:S(2)}, u32[]{:S(2)}) collective-permute-start(bf16[128,2048]{1,0:T(8,128)(2,1)} %get-tuple-element.396), channel_id=1, source_target_pairs={{0,24},{4,28},{8,16},{12,20},{16,8},{20,12},{24,0},{28,4},{1,25},{... | collective-permute-start | bytes 1572872 | tf_op jit(solution)/shard_map/ppermute | solution.py:57
  733.6 31.9 %collective-permute-start.88 = (bf16[128,2048]{1,0:T(8,128)(2,1)}, bf16[128,2048]{1,0:T(8,128)(2,1)}, u32[]{:S(2)}, u32[]{:S(2)}) collective-permute-start(bf16[128,2048]{1,0:T(8,128)(2,1)} %add_convert_fusion.7), channel_id=1, source_target_pairs={{0,1},{1,2},{2,3},{3,0},{4,5},{5,6},{6,7},{7,4},{8,9},{9,10},{10,1... | collective-permute-start | bytes 1572872 | tf_op jit(solution)/shard_map/ppermute | solution.py:62
  769.1 41.5 %collective-permute-start.94 = (bf16[512,2048]{1,0:T(8,128)(2,1)}, bf16[512,2048]{1,0:T(8,128)(2,1)}, u32[]{:S(2)}, u32[]{:S(2)}) collective-permute-start(bf16[512,2048]{1,0:T(8,128)(2,1)} %get-tuple-element.404), channel_id=1, source_target_pairs={{0,4},{4,0},{8,12},{12,8},{16,20},{20,16},{24,28},{28,24},{1,5},{5... | collective-permute-start | bytes 6291464 | tf_op jit(solution)/shard_map/ppermute | solution.py:57
  770.9 31.8 %collective-permute-start.96 = (bf16[128,2048]{1,0:T(8,128)(2,1)}, bf16[128,2048]{1,0:T(8,128)(2,1)}, u32[]{:S(2)}, u32[]{:S(2)}) collective-permute-start(bf16[128,2048]{1,0:T(8,128)(2,1)} %get-tuple-element.407), channel_id=1, source_target_pairs={{0,16},{4,20},{8,24},{12,28},{16,0},{20,4},{24,8},{28,12},{1,17},{... | collective-permute-start | bytes 1572872 | tf_op jit(solution)/shard_map/ppermute | solution.py:57
  771.7 31.0 %collective-permute-start.97 = (bf16[128,2048]{1,0:T(8,128)(2,1)}, bf16[128,2048]{1,0:T(8,128)(2,1)}, u32[]{:S(2)}, u32[]{:S(2)}) collective-permute-start(bf16[128,2048]{1,0:T(8,128)(2,1)} %get-tuple-element.408), channel_id=1, source_target_pairs={{0,24},{4,28},{8,16},{12,20},{16,8},{20,12},{24,0},{28,4},{1,25},{... | collective-permute-start | bytes 1572872 | tf_op jit(solution)/shard_map/ppermute | solution.py:57
  (153 other events, 1948.2 us)

commit v3 on v2

--- a/solution.py
+++ b/solution.py
@@ -67,8 +67,8 @@
 
 
 class Step:
-    def __init__(self, sent, make=None, beside=(), outs=()):
-        self.sent, self.make, self.beside, self.outs = sent, make, list(beside), list(outs)
+    def __init__(self, sent, outs=(), beside=()):
+        self.sent, self.outs, self.beside = list(sent), list(outs), list(beside)
 
 
 class Transfer:
@@ -91,39 +91,96 @@
         return values + self.token[0, 0].astype(values.dtype)
 
 
+CHUNK = 16
+
+
+def add_rows(target, at, sources, rows):
+    @pl.loop(0, rows // CHUNK)
+    def _(i):
+        row = pl.multiple_of(i * CHUNK, CHUNK)
+        total = sum(ref[pl.ds(row, CHUNK), :].astype(jnp.float32) for ref in sources)
+        target[pl.ds(at + row, CHUNK), :] = total.astype(target.dtype)
+
+
+def make_outs(inputs, outs, plans, scratch):
+    held, terms, (in_sems, out_sems) = scratch[: len(outs)], scratch[len(outs) : -2], scratch[-2:]
+    parts, copies, used = [], 0, 0
+    for buffer, out, plan in zip(held, outs, plans, strict=True):
+        at = 0
+        for rows, sources in plan:
+            place = buffer.at[pl.ds(at, rows)]
+            into = [place] if len(sources) == 1 else list(terms[used : used + len(sources)])
+            used += 0 if len(sources) == 1 else len(sources)
+            arriving = []
+            for (i, start), target in zip(sources, into, strict=True):
+                source = inputs[i].at[pl.ds(start, rows)]
+                arriving.append(pltpu.make_async_copy(source, target, in_sems.at[copies]))
+                arriving[-1].start()
+                copies += 1
+            leaving = pltpu.make_async_copy(place, out.at[pl.ds(at, rows)], out_sems.at[len(parts)])
+            parts.append((arriving, buffer, at, into, rows, leaving))
+            at += rows
+    for arriving, buffer, at, into, rows, leaving in parts:
+        for copy in arriving:
+            copy.wait()
+        if len(arriving) > 1:
+            add_rows(buffer, at, into, rows)
+        leaving.start()
+    for *_, leaving in parts:
+        leaving.wait()
+
+
 def stage(clock, transfers, beside=()):
     active = [t for t in transfers if not t.done]
-    making = [t.step for t in active if t.step.make is not None]
+    making = [t for t in active if t.step.outs]
+    waited = [a for t in active if not t.step.outs for a in t.step.sent]
     passed = [clock.token, *beside]
-    waited = [a for t in active if t.step.make is None for a in t.step.sent]
-    taken = [a for step in making for a in step.sent + step.beside]
-    outs = [jax.ShapeDtypeStruct(o, step.sent[0].dtype) for step in making for o in step.outs]
+    taken, plans, kinds = [], [], []
+    for t in making:
+        base = len(taken)
+        taken += t.step.sent + t.step.beside
+        for plan in t.step.outs:
+            plans.append([(rows, [(base + i, start) for i, start in terms]) for rows, terms in plan])
+            like = t.step.sent[0]
+            kinds.append((sum(rows for rows, _ in plan), like.shape[1], like.dtype))
+    scratch = [pltpu.VMEM((rows, width), kind) for rows, width, kind in kinds]
+    count = 0
+    for (_, width, kind), plan in zip(kinds, plans, strict=True):
+        for rows, terms in plan:
+            count += len(terms)
+            if len(terms) > 1:
+                scratch += [pltpu.VMEM((rows, width), kind)] * len(terms)
+    if making:
+        scratch += [pltpu.SemaphoreType.DMA((count,)), pltpu.SemaphoreType.DMA((sum(map(len, plans)),))]
     first = len(passed) + len(waited)
 
     def kernel(*refs):
-        inputs, made = refs[first : first + len(taken)], refs[first + len(taken) + len(passed) :]
-        for step in making:
-            count = len(step.sent) + len(step.beside)
-            step.make(inputs[:count], made[: len(step.outs)])
-            inputs, made = inputs[count:], made[len(step.outs) :]
-
-    far, near = pl.BlockSpec(memory_space=pltpu.HBM), pl.BlockSpec(memory_space=pltpu.VMEM)
+        outs = first + len(taken) + len(passed)
+        if making:
+            make_outs(
+                refs[first : first + len(taken)],
+                refs[outs : outs + len(kinds)],
+                plans,
+                refs[outs + len(kinds) :],
+            )
+
+    far = pl.BlockSpec(memory_space=pl.ANY)
     arrays = pl.pallas_call(
         kernel,
-        in_specs=[far] * first + [near] * len(taken),
-        out_specs=[far] * len(passed) + [near] * len(outs),
-        out_shape=[jax.ShapeDtypeStruct(a.shape, a.dtype) for a in passed] + outs,
+        in_specs=[far] * (first + len(taken)),
+        out_specs=[far] * (len(passed) + len(kinds)),
+        out_shape=[jax.ShapeDtypeStruct(a.shape, a.dtype) for a in passed]
+        + [jax.ShapeDtypeStruct((rows, width), kind) for rows, width, kind in kinds],
+        scratch_shapes=scratch,
         input_output_aliases={i: i for i in range(len(passed))},
         compiler_params=pltpu.CompilerParams(vmem_limit_bytes=VMEM),
     )(*passed, *waited, *taken)
     clock.token, given, arrays = arrays[0], arrays[1 : len(passed)], arrays[len(passed) :]
+    results = {}
+    for t in making:
+        results[id(t)], arrays = arrays[: len(t.step.outs)], arrays[len(t.step.outs) :]
     for t in active:
-        if t.step.make is None:
-            t.advance(t.step.sent)
-        else:
-            count = len(t.step.outs)
-            made, arrays = arrays[:count], arrays[count:]
-            t.advance(made)
+        t.advance(results[id(t)] if id(t) in results else t.step.sent)
     return given
 
 
@@ -131,49 +188,6 @@
     while not all(t.done for t in transfers):
         stage(clock, transfers)
     return [t.result for t in transfers]
-
-
-CHUNK = 16
-
-
-def chunks(amount, body):
-    @pl.loop(0, amount // CHUNK)
-    def _(i):
-        body(pl.multiple_of(i * CHUNK, CHUNK))
-
-
-def put(source, target, at=0, start=0, amount=None):
-    def body(row):
-        target[pl.ds(at + row, CHUNK), :] = source[pl.ds(start + row, CHUNK), :]
-
-    chunks(amount or target.shape[0] - at, body)
-
-
-def put_sum(target, sources, starts=None, at=0, amount=None):
-    starts = starts or [0] * len(sources)
-
-    def body(row):
-        total = 0.0
-        for source, start in zip(sources, starts, strict=True):
-            total = total + source[pl.ds(start + row, CHUNK), :].astype(jnp.float32)
-        target[pl.ds(at + row, CHUNK), :] = total.astype(target.dtype)
-
-    chunks(amount or target.shape[0] - at, body)
-
-
-def put_blocks_sum(taken, made):
-    for i in range(made[0].shape[0]):
-        put_sum(made[0].at[i], [ref.at[i] for ref in taken])
-
-
-def put_joined(order):
-    def make(taken, made):
-        at = 0
-        for i in order:
-            put(taken[i], made[0], at, 0, taken[i].shape[0])
-            at += taken[i].shape[0]
-
-    return make
 
 
 def turned(block, step=1):
@@ -192,7 +206,8 @@
 def ring_sum(pieces):
     total = pieces[min(1, len(pieces) - 1)]
     for piece in pieces[2:] + (pieces[:1] if len(pieces) > 1 else []):
-        (total,) = yield Step([turn(total)], put_blocks_sum, [piece], [piece.shape])
+        rows = total.shape[0]
+        (total,) = yield Step([turn(total)], [[(rows, [(0, 0), (1, 0)])]], [piece])
     return total
 
 
@@ -217,82 +232,43 @@
 
 def gather_plane(block, direct=True):
     bits = ctx_bits()
-    amount, width = block.shape
+    amount = block.shape[0]
     half = -(-amount // 2 // CHUNK) * CHUNK
+    rest = amount - half
     if len(bits) == 2 and direct:
         others = [swap(block, place) for place in (bits[0], bits[1], bits[0] | bits[1])]
-        (near,) = yield Step(others, put_joined([3, 0, 1, 2]), [block], [(4 * amount, width)])
+        (near,) = yield Step(others, [[(amount, [(i, 0)]) for i in (3, 0, 1, 2)]], [block])
     elif len(bits) == 2:
         x_bit, y_bit = bits
-        over_x, over_y = swap(block, x_bit), swap(block, y_bit)
-
-        def halves(taken, made):
-            put(taken[0], made[0], 0, 0, half)
-            put(taken[1], made[1], 0, half, amount - half)
-
-        parts = [(half, width), (amount - half, width)]
-        first, second = yield Step([over_x, over_y], halves, [], parts)
+        over = [swap(block, x_bit), swap(block, y_bit)]
+        first, second = yield Step(over, [[(half, [(0, 0)])], [(rest, [(1, half)])]])
         corner = [swap(first, y_bit), swap(second, x_bit)]
-        (near,) = yield Step(
-            corner, put_joined([2, 3, 4, 0, 1]), [block, over_x, over_y], [(4 * amount, width)]
-        )
+        parts = [(amount, [(i, 0)]) for i in (2, 3, 4)] + [(half, [(0, 0)]), (rest, [(1, 0)])]
+        (near,) = yield Step(corner, [parts], [block, *over])
     else:
         near = block
         for bit in bits:
-            shape = (2 * near.shape[0], width)
-            (near,) = yield Step([swap(near, bit)], put_joined([1, 0]), [near], [shape])
+            rows = near.shape[0]
+            (near,) = yield Step([swap(near, bit)], [[(rows, [(1, 0)]), (rows, [(0, 0)])]], [near])
     (far,) = yield Step([swap(near, 1)])
     return near, far
 
 
-def scatter_plane(near, far, direct=True):
+def scatter_plane(near, far):
     bits = ctx_bits()
-    size, width = near.shape[0] >> len(bits), near.shape[1]
-    half = size // 2
-    whole, part = (size, width), (half, width)
-    if len(bits) != 2:
-        (held,) = yield Step([swap(far, 1)], lambda t, m: put_sum(m[0], t), [near], [near.shape])
-        for bit in reversed(bits):
-            middle = held.shape[0] // 2
-
-            def fold(taken, made, middle=middle):
-                put_sum(made[0], taken)
-
-            (held,) = yield Step([swap(held[middle:], bit)], fold, [held[:middle]], [(middle, width)])
-        return held
-    x_bit, y_bit = bits
-    if direct:
-
-        def spread(taken, made):
-            for i in range(4):
-                put_sum(made[i], taken, [i * size, i * size])
-
-        own, part_x, part_y, corner = yield Step([swap(far, 1)], spread, [near], [whole] * 4)
-        back = [swap(part_x, x_bit), swap(part_y, y_bit), swap(corner, x_bit | y_bit)]
-        (total,) = yield Step(back, lambda t, m: put_sum(m[0], t), [own], [whole])
+    size = near.shape[0] >> len(bits)
+    if len(bits) == 2:
+        parts = [[(size, [(0, i * size), (1, i * size)])] for i in range(4)]
+        own, part_x, part_y, corner = yield Step([swap(far, 1)], parts, [near])
+        back = [swap(part_x, bits[0]), swap(part_y, bits[1]), swap(corner, bits[0] | bits[1])]
+        (total,) = yield Step(back, [[(size, [(i, 0) for i in range(4)])]], [own])
         return total
-
-    def split(taken, made):
-        for i, at in enumerate((0, size, 2 * size, 3 * size, 3 * size + half)):
-            put_sum(made[i], taken, [at, at])
-
-    def join(taken, made):
-        for_y, for_x, part_x, part_y = taken
-        put(part_x, made[0], 0, 0, half)
-        put_sum(made[0], [part_x, for_x], [half, 0], half, half)
-        put_sum(made[1], [part_y, for_y], [0, 0], 0, half)
-        put(part_y, made[1], half, half, half)
-
-    own, part_x, part_y, corner_a, corner_b = yield Step(
-        [swap(far, 1)], split, [near], [whole] * 3 + [part] * 2
-    )
-    part_x, part_y = yield Step(
-        [swap(corner_a, x_bit), swap(corner_b, y_bit)], join, [part_x, part_y], [whole] * 2
-    )
-    (total,) = yield Step(
-        [swap(part_x, x_bit), swap(part_y, y_bit)], lambda t, m: put_sum(m[0], t), [own], [whole]
-    )
-    return total
+    rows = near.shape[0]
+    (held,) = yield Step([swap(far, 1)], [[(rows, [(0, 0), (1, 0)])]], [near])
+    for bit in reversed(bits):
+        rows //= 2
+        (held,) = yield Step([swap(held[rows:], bit)], [[(rows, [(0, 0), (1, 0)])]], [held])
+    return held
 
 
 def gate_parts(first, second):
@@ -345,24 +321,66 @@
     return slice(span * GROUP * BLOCK, (span + 1) * GROUP * BLOCK)
 
 
+def streamed(source, buffers, sems, step, count):
+    def copy(owner):
+        return pltpu.make_async_copy(source.at[owner], buffers.at[owner % 2], sems.at[owner % 2])
+
+    @pl.when(step == 0)
+    def _():
+        copy(0).start()
+
+    @pl.when(step + 1 < count)
+    def _():
+        copy(step + 1).start()
+
+    def arrived():
+        copy(step).wait()
+        return buffers[step % 2]
+
+    return arrived
+
+
 def early_kernel(*refs, carried):
-    ga_ref, gb_ref, slot_ref, down_ref, s_down_ref = refs[:5]
-    rows_ref, dh_ref, dhs_ref, kept_ref = refs[5 + carried :]
+    first_ref, ga_ref, gb_ref, down_ref, s_down_ref = refs[:5]
+    (rows_ref, dh_ref, router_out, dhs_ref, ranks_ref, slot_ref, kept_ref, router_ref, w_ref, w_sems, sem) = refs[
+        5 + carried :
+    ]
     owners = slot_ref.shape[0]
     step = pl.program_id(0)
+    weights = streamed(down_ref, w_ref, w_sems, step, owners)
 
     @pl.when(step == 0)
     def _():
-        for span, place in enumerate(spans_of(ga_ref, gb_ref, BLOCK + EXTRA)):
+        places = spans_of(ga_ref, gb_ref, BLOCK + EXTRA)
+        blocks, count = router_ref.shape[:2]
+        for block, (ref, at) in enumerate((ref, at) for ref, starts in places for at in starts):
+            place = 2 * block if 2 * block < blocks else 2 * block - blocks + 1
+            came = ref[at + BLOCK : at + BLOCK + EXTRA, :]
+            lanes = slice(block * BLOCK, (block + 1) * BLOCK)
+            for i in range((EXPERTS + count) // EXTRA):
+                tile, row = came[:, i * BLOCK : (i + 1) * BLOCK], i * EXTRA
+                if row < EXPERTS:
+                    ranks_ref[row : row + EXTRA, lanes] = tile.astype(jnp.float32)
+                else:
+                    router_ref[first_ref[2] ^ place, row - EXPERTS : row - EXPERTS + EXTRA, :] = tile
+        router_copy = pltpu.make_async_copy(router_ref, router_out.at[:, first_ref[3]], sem)
+        router_copy.start()
+        lane = lax.broadcasted_iota(jnp.int32, (1, slot_ref.shape[1]), 1)
+        offset = (CAP * (lane // BLOCK % GROUP)).astype(jnp.float32)
+        for owner in range(owners):
+            ranks = ranks_ref[pl.ds(first_ref[0] + owner, 1), :]
+            slot_ref[owner : owner + 1, :] = jnp.where(ranks >= 0, ranks + offset, -1.0)
+        for span, place in enumerate(places):
             values = read_span(*place)
             taken = dot(pick_all(slot_ref, span), values).astype(jnp.bfloat16)
             for owner in range(owners):
                 kept_ref[owner, slots_at(span), :] = taken[slots_at(owner)]
             dhs_ref[tokens_at(span), :] = contract_cols(values, s_down_ref[...])
+        router_copy.wait()
 
     rows = kept_ref[step]
     rows_ref[0] = rows
-    dh_ref[0] = contract_cols(rows, down_ref[0])
+    dh_ref[0] = contract_cols(rows, weights())
 
 
 def gate_rows(first_ref, values, width):
@@ -383,21 +401,19 @@
 
 def middle_kernel(*refs, carried):
     (first_ref, xa_ref, xb_ref, router_ref, mask_ref, slot_ref, in_ref, s_in_ref, dh_ref, dhs_ref) = refs[:10]
-    (rows_ref, hidden_ref, dj_ref, da_ref, db_ref, gates_ref, dgate_ref, sh_ref, ds_ref, r_ref, z_ref, gate_ref) = refs[10 + carried :]
+    (rows_ref, hidden_ref, dj_ref, da_ref, db_ref, gates_ref, dgate_ref, sh_ref, ds_ref, r_ref, z_ref, gate_ref, w_ref, w_sems) = refs[10 + carried :]
     bf16 = jnp.bfloat16
     owners = slot_ref.shape[0]
     step = pl.program_id(0)
     spans = spans_of(xa_ref, xb_ref)
+    weights = streamed(in_ref, w_ref, w_sems, step, owners)
 
     @pl.when(step == 0)
     def _():
         for span, place in enumerate(spans):
             x = read_span(*place)
             lanes = tokens_at(span)
-            mask = jnp.concatenate(
-                [mask_ref[span * GROUP + i].astype(jnp.float32) for i in range(GROUP)], axis=1
-            )
-            mask = mask >= 0
+            mask = mask_ref[:, lanes] >= 0
             logits = jnp.where(mask, contract_cols(router_ref[...], x), NEGATIVE)
             gates = jnp.where(mask, jnp.exp(logits - jnp.max(logits, axis=0, keepdims=True)), 0.0)
             gates = gates / jnp.sum(gates, axis=0, keepdims=True)
@@ -420,7 +436,8 @@
             ds_ref[lanes, :] = jnp.concatenate(back, axis=1).astype(bf16)
 
     rows = r_ref[step]
-    joined = dot(rows, in_ref[0])
+    weights_in = weights()
+    joined = dot(rows, weights_in)
     units = joined.shape[1] // 2
     first, second = joined[:, :units], joined[:, units:]
     sigmoid, hidden = gate_parts(first, second)
@@ -430,7 +447,7 @@
         spread = jnp.where(pick(slot_ref, step, span), d_gate[slots_at(span)], 0.0)
         dgate_ref[pl.ds(step, 1), tokens_at(span)] = jnp.sum(spread, axis=0, keepdims=True)
     d_joined = jnp.concatenate(back, axis=1).astype(bf16)
-    z_ref[step] = contract_cols(d_joined, in_ref[0]).astype(bf16)
+    z_ref[step] = contract_cols(d_joined, weights_in).astype(bf16)
     rows_ref[0] = rows
     hidden_ref[0] = hidden.astype(bf16)
     dj_ref[0] = d_joined
@@ -501,30 +518,39 @@
 
 
 def attend_kernel(*refs, planes, heads):
-    (plane_ref, near_ref, far_ref, gain_ref, cos_ref, sin_ref, column_ref, row_ref) = refs[:8]
-    w_pieces = refs[8 : 8 + planes]
-    (oa_ref, ob_ref, normed_ref, q_ref, k_ref, v_ref, mixed_ref, top_ref, total_ref) = refs[
-        9 + planes : 18 + planes
-    ]
-    w_ref, sems = refs[18 + planes :]
+    (plane_ref, gain_ref, cos_ref, sin_ref, column_ref, row_ref) = refs[:6]
+    near_out, far_out, w_pieces = refs[6], refs[7], refs[8 : 8 + planes]
+    outs = refs[9 + planes : 18 + planes]
+    (w_ref, x_ref, o_ref, *kept, sems) = refs[18 + planes :]
+    (normed_ref, q_ref, k_ref, v_ref, mixed_ref, top_ref, total_ref) = kept
     bf16, f32 = jnp.bfloat16, jnp.float32
     plane = plane_ref[0]
-    width = near_ref.shape[1]
+    width = near_out.shape[1]
     blocks, part = w_ref.shape[0], w_ref.shape[3] // 4
     size = part // heads
-    half = near_ref.shape[0]
+    half = near_out.shape[0]
     amount = 2 * half
     copies = plane_copies(plane, w_pieces, lambda at: w_ref.at[:, at], sems.at[0])
-    for copy in copies:
+    sides = [
+        pltpu.make_async_copy(ref, x_ref.at[side], sems.at[1, side])
+        for side, ref in enumerate((near_out, far_out))
+    ]
+    leaving = [pltpu.make_async_copy(o_ref.at[side], outs[side], sems.at[2, side]) for side in range(2)]
+    leaving += [
+        pltpu.make_async_copy(ref, out, sems.at[3, i])
+        for i, (ref, out) in enumerate(zip(kept, outs[2:], strict=True))
+    ]
+    for copy in copies + sides:
         copy.start()
     for copy in copies:
         copy.wait()
 
-    for base, ref in ((0, near_ref), (half, far_ref)):
-
-        def project(row, base=base, ref=ref):
+    for side, base in enumerate((0, half)):
+        sides[side].wait()
+
+        def project(row, base=base, side=side):
             at = pl.ds(base + row, ROWS)
-            x = ref[pl.ds(row, ROWS), :].astype(f32)
+            x = x_ref[side, pl.ds(row, ROWS), :].astype(f32)
             normed = rms_scale(x, gain_ref[...]).astype(bf16)
             normed_ref[at, :] = normed
             projected = dot(normed, w_ref[:, :, :, : 3 * part].reshape(width, 3 * part))
@@ -537,6 +563,8 @@
             v_ref[at, :] = projected[:, 2 * part :].astype(bf16)
 
         row_chunks(half, project)
+    for copy in leaving[2:6]:
+        copy.start()
 
     for head in range(heads):
         mine = slice(head * size, (head + 1) * size)
@@ -554,26 +582,31 @@
             mixed_ref[at, mine] = dot(expo.astype(bf16), v_ref[:, mine]) / total
 
         row_chunks(amount, attend)
-
-    for base, ref in ((0, oa_ref), (half, ob_ref)):
-
-        def project_out(row, base=base, ref=ref):
+    for copy in leaving[6:]:
+        copy.start()
+
+    for side, base in enumerate((0, half)):
+
+        def project_out(row, base=base, side=side):
             mixed = mixed_ref[pl.ds(base + row, ROWS), :].astype(bf16)
             for i in range(blocks):
                 weights = w_ref[i, :, :, 3 * part :].reshape(part, width // blocks)
                 into = slice(i * width // blocks, (i + 1) * width // blocks)
-                ref[pl.ds(row, ROWS), into] = dot(mixed, weights).astype(bf16)
+                o_ref[side, pl.ds(row, ROWS), into] = dot(mixed, weights).astype(bf16)
 
         row_chunks(half, project_out)
+        leaving[side].start()
+    for copy in leaving:
+        copy.wait()
 
 
 def attend_back_kernel(*refs, planes, heads):
-    (plane_ref, near_ref, far_ref, normed_ref, q_ref, k_ref, v_ref, mixed_ref, top_ref, total_ref) = refs[:10]
-    (cos_ref, sin_ref, column_ref, row_ref) = refs[10:14]
-    w_pieces = refs[14 : 14 + planes]
+    (plane_ref, cos_ref, sin_ref, column_ref, row_ref) = refs[:5]
+    arriving, w_pieces = refs[5:14], refs[14 : 14 + planes]
     rest = refs[15 + planes :]
-    (da_ref, db_ref), w_grads = rest[:2], rest[2 : 2 + planes]
-    (w_ref, gw_ref, dm_ref, dp_ref, dk_ref, dv_ref, sems) = rest[2 + planes :]
+    d_outs, w_grads = rest[:2], rest[2 : 2 + planes]
+    (w_ref, gw_ref, dm_ref, dp_ref, dk_ref, dv_ref, o_ref, *came, sems) = rest[2 + planes :]
+    (near_ref, far_ref, normed_ref, q_ref, k_ref, v_ref, mixed_ref, top_ref, total_ref) = came
     bf16, f32 = jnp.bfloat16, jnp.float32
     plane = plane_ref[0]
     width = near_ref.shape[1]
@@ -582,12 +615,18 @@
     half = near_ref.shape[0]
     amount = 2 * half
     w_copies = plane_copies(plane, w_pieces, lambda at: w_ref.at[:, at], sems.at[0])
-    for copy in w_copies:
+    copies = [
+        pltpu.make_async_copy(source, ref, sems.at[2, i])
+        for i, (source, ref) in enumerate(zip(arriving, came, strict=True))
+    ]
+    d_copies = [pltpu.make_async_copy(o_ref.at[side], d_outs[side], sems.at[3, side]) for side in range(2)]
+    for copy in w_copies + copies[:2] + copies[3:] + copies[2:3]:
         copy.start()
     for copy in w_copies:
         copy.wait()
 
-    for base, ref in ((0, near_ref), (half, far_ref)):
+    for side, (base, ref) in enumerate(((0, near_ref), (half, far_ref))):
+        copies[side].wait()
 
         def back_out(row, base=base, ref=ref):
             values = 0.0
@@ -598,6 +637,8 @@
             dm_ref[pl.ds(base + row, ROWS), :] = values.astype(bf16).astype(f32)
 
         row_chunks(half, back_out)
+    for copy in copies[3:]:
+        copy.wait()
     sides = [(mixed_ref[:half, :].astype(bf16), near_ref), (mixed_ref[half:, :].astype(bf16), far_ref)]
     for i in range(blocks):
         into = slice(i * width // blocks, (i + 1) * width // blocks)
@@ -631,6 +672,7 @@
         dp_ref[:, part + head * size : part + (head + 1) * size] = d_key.astype(bf16)
         dp_ref[:, 2 * part + head * size : 2 * part + (head + 1) * size] = dv_ref[...].astype(bf16)
 
+    copies[2].wait()
     pieces = 4
     step, count = width // pieces, blocks // pieces
     for i in range(pieces):
@@ -645,32 +687,33 @@
     ]
     for copy in w_back:
         copy.start()
-    for base, ref in ((0, da_ref), (half, db_ref)):
-
-        def back_project(row, base=base, ref=ref):
+    for side, base in enumerate((0, half)):
+
+        def back_project(row, base=base, side=side):
             values = contract_cols(
                 dp_ref[pl.ds(base + row, ROWS), :], w_ref[:, :, :, : 3 * part].reshape(width, 3 * part)
             )
-            ref[pl.ds(row, ROWS), :] = values.astype(bf16)
+            o_ref[side, pl.ds(row, ROWS), :] = values.astype(bf16)
 
         row_chunks(half, back_project)
-    for copy in w_back:
+        d_copies[side].start()
+    for copy in w_back + d_copies:
         copy.wait()
 
 
-def attend_call(kernel, small, blocks, pieces, outs, piece_outs, scratch, after, flops):
+def attend_call(kernel, small, blocks, arrays, outs, scratch, after, flops):
     far, near = pl.BlockSpec(memory_space=pltpu.HBM), pl.BlockSpec(memory_space=pltpu.VMEM)
     return pl.pallas_call(
         kernel,
         in_specs=[pl.BlockSpec(memory_space=pltpu.SMEM)]
         + [near] * len(blocks)
-        + [far] * (len(pieces) + 1),
-        out_specs=[near] * len(outs) + [far] * len(piece_outs),
-        out_shape=[jax.ShapeDtypeStruct(shape, kind) for shape, kind in outs + piece_outs],
+        + [far] * (len(arrays) + 1),
+        out_specs=[far] * len(outs),
+        out_shape=[jax.ShapeDtypeStruct(shape, kind) for shape, kind in outs],
         scratch_shapes=scratch,
         compiler_params=pltpu.CompilerParams(vmem_limit_bytes=VMEM),
         cost_estimate=pl.CostEstimate(flops=flops, bytes_accessed=30_000_000, transcendentals=0),
-    )(small, *blocks, *pieces, after)
+    )(small, *blocks, *arrays, after)
 
 
 def attend(plane, rows, gain, tables, pieces, heads, after):
@@ -679,20 +722,18 @@
     planes = len(pieces)
     n_ctx, depth, four = pieces[0].shape
     part = four // 4
-    outs = [((half, width), bf16)] * 2 + [((2 * half, width), bf16)]
-    outs += [((2 * half, part), bf16)] * 3 + [((2 * half, part), f32)]
-    outs += [((heads, 2 * half, 1), f32)] * 2
+    kept = [((2 * half, width), bf16)] + [((2 * half, part), bf16)] * 3
+    kept += [((2 * half, part), f32)] + [((heads, 2 * half, 1), f32)] * 2
     return attend_call(
         functools.partial(attend_kernel, planes=planes, heads=heads),
         plane,
-        [*rows, gain, *tables],
-        pieces,
-        outs,
-        [],
-        [
-            pltpu.VMEM((n_ctx, planes, depth, four), bf16),
-            pltpu.SemaphoreType.DMA((1, planes)),
-        ],
+        [gain, *tables],
+        [*rows, *pieces],
+        [((half, width), bf16)] * 2 + kept,
+        [pltpu.VMEM((n_ctx, planes, depth, four), bf16)]
+        + [pltpu.VMEM((2, half, width), bf16)] * 2
+        + [pltpu.VMEM(shape, kind) for shape, kind in kept]
+        + [pltpu.SemaphoreType.DMA((4, max(planes, 7)))],
         after,
         4 * half * width * 4 * part + 16 * half * half * part,
     )
@@ -707,10 +748,9 @@
     made = attend_call(
         functools.partial(attend_back_kernel, planes=planes, heads=heads),
         plane,
-        [*rows, *saved, *tables],
-        pieces,
-        [((half, width), bf16)] * 2,
-        [(pieces[0].shape, bf16)] * planes,
+        tables,
+        [*rows, *saved, *pieces],
+        [((half, width), bf16)] * 2 + [(pieces[0].shape, bf16)] * planes,
         [
             pltpu.VMEM((n_ctx, planes, depth, four), bf16),
             pltpu.VMEM((n_ctx, planes, depth, four), bf16),
@@ -718,7 +758,9 @@
             pltpu.VMEM((2 * half, 3 * part), bf16),
             pltpu.VMEM((2 * half, part // heads), f32),
             pltpu.VMEM((2 * half, part // heads), f32),
-            pltpu.SemaphoreType.DMA((2, planes)),
+            pltpu.VMEM((2, half, width), bf16),
+            *(pltpu.VMEM(a.shape, a.dtype) for a in (*rows, *saved)),
+            pltpu.SemaphoreType.DMA((4, max(planes, 9))),
         ],
         after,
         4 * half * width * 8 * part + 40 * half * half * part,
@@ -730,16 +772,39 @@
     refs[-1][0] = contract_rows(left_ref[0], right_ref[0])
 
 
-def shared_kernel(xa_ref, xb_ref, ga_ref, gb_ref, hidden_ref, joined_ref, *refs):
-    into_ref, down_ref = refs[-2:]
+def shared_kernel(*refs, count):
+    xs, gs = refs[:count], refs[count : 2 * count]
+    hidden_ref, joined_ref, _, into_ref, down_ref, x_ref, g_ref, sum_ref, sems = refs[2 * count :]
     size = GROUP * BLOCK
-    places = spans_of(ga_ref, gb_ref, BLOCK + EXTRA)
-    for i, (x_place, g_place) in enumerate(zip(spans_of(xa_ref, xb_ref), places, strict=True)):
+    places = []
+    for x, g in zip(xs, gs, strict=True):
+        for at, (_, starts) in enumerate(spans_of(g, g, BLOCK + EXTRA)[: x.shape[0] // size]):
+            places.append((x, at * size, g, starts))
+
+    def copies(i):
+        x, at, g, starts = places[i]
+        slot = i % 2
+        made = [pltpu.make_async_copy(x.at[pl.ds(at, size)], x_ref.at[slot], sems.at[slot, 0])]
+        for n, start in enumerate(starts):
+            source, target = g.at[pl.ds(start, BLOCK)], g_ref.at[slot, pl.ds(n * BLOCK, BLOCK)]
+            made.append(pltpu.make_async_copy(source, target, sems.at[slot, 1 + n]))
+        return made
+
+    for copy in copies(0):
+        copy.start()
+    for i in range(len(places)):
+        if i + 1 < len(places):
+            for copy in copies(i + 1):
+                copy.start()
+        for copy in copies(i):
+            copy.wait()
         at = slice(i * size, (i + 1) * size)
-        into = contract_rows(joined_ref[at, :], read_span(*x_place))
-        down = contract_rows(hidden_ref[at, :], read_span(*g_place))
-        into_ref[...] = into if i == 0 else into_ref[...] + into
+        into = contract_rows(joined_ref[at, :], x_ref[i % 2])
+        down = contract_rows(hidden_ref[at, :], g_ref[i % 2])
+        sum_ref[...] = into if i == 0 else sum_ref[...] + into
         down_ref[...] = down if i == 0 else down_ref[...] + down
+    for at in range(0, into_ref.shape[0], size):
+        into_ref[at : at + size, :] = sum_ref[:, at : at + size].T.astype(into_ref.dtype)
 
 
 def held_whole(*shape):
@@ -766,14 +831,12 @@
     return pl.BlockSpec((1, rows, columns), lambda j: (j, k, 0))
 
 
-def weights_of(array):
-    depth = 2 if array.shape[0] > 1 else 1
-    return pl.BlockSpec(
-        (1,) + array.shape[1:], lambda j: (j, 0, 0), pipeline_mode=pl.Buffered(depth)
-    )
-
-
-def early(k, planes, grads, slots, w_down, s_down, kept, after):
+def weight_buffers(array):
+    depth = min(2, array.shape[0])
+    return [pltpu.VMEM((depth,) + array.shape[1:], array.dtype), pltpu.SemaphoreType.DMA((depth,))]
+
+
+def early(k, planes, first, grads, count, w_down, s_down, kept, after):
     bf16, f32 = jnp.bfloat16, jnp.float32
     owners, units, width = w_down.shape
     half = grads[0].shape[0] * BLOCK // (BLOCK + EXTRA)
@@ -781,23 +844,33 @@
     outs = [
         ((owners, planes * rows, width), bf16),
         ((owners, planes * rows, units), f32),
+        ((2 * half // BLOCK, planes, count, BLOCK), bf16),
         ((2 * half, lane), f32),
+        ((EXPERTS, 2 * half), f32),
+        ((owners, 2 * half), f32),
     ]
-    taken, dh, dhs = expert_call(
+    made = expert_call(
         early_kernel,
         owners,
-        [*grads, slots, w_down, s_down],
-        [held_whole(*grads[0].shape)] * 2
-        + [held_whole(*slots.shape), weights_of(w_down), held_whole(*s_down.shape)],
+        [first, *grads, w_down, s_down],
+        [pl.BlockSpec(memory_space=pltpu.SMEM)]
+        + [held_whole(*grads[0].shape)] * 2
+        + [pl.BlockSpec(memory_space=pltpu.HBM), held_whole(*s_down.shape)],
         outs,
-        [growing(k, rows, width), growing(k, rows, units), held_whole(2 * half, lane)],
+        [growing(k, rows, width), growing(k, rows, units), pl.BlockSpec(memory_space=pltpu.HBM)]
+        + [held_whole(*shape) for shape, _ in outs[3:]],
         kept,
         after,
-        [pltpu.VMEM((owners, rows, width), bf16)],
+        [
+            pltpu.VMEM((owners, rows, width), bf16),
+            pltpu.VMEM((2 * half // BLOCK, count, BLOCK), bf16),
+            *weight_buffers(w_down),
+            pltpu.SemaphoreType.DMA(()),
+        ],
         2 * owners * rows * width * (units + GROUP * BLOCK) + 4 * half * width * lane,
         2 * owners * width * (units + 2 * rows) + 4 * half * width,
     )
-    return [taken, dh], dhs
+    return list(made[:3]), made[3:]
 
 
 def middle(
@@ -825,7 +898,7 @@
         [pl.BlockSpec(memory_space=pltpu.SMEM)]
         + [held_whole(half, width)] * 2
         + [held_whole(*a.shape) for a in (router_t, mask, slots)]
-        + [weights_of(w_in), held_whole(*s_in.shape), growing(k, rows, joined // 2)]
+        + [pl.BlockSpec(memory_space=pltpu.HBM), held_whole(*s_in.shape), growing(k, rows, joined // 2)]
         + [held_whole(*dhs.shape)],
         outs,
         [growing(k, rows, width), growing(k, rows, joined // 2), growing(k, rows, joined)]
@@ -836,6 +909,7 @@
             pltpu.VMEM((owners, rows, width), bf16),
             pltpu.VMEM((owners, rows, width), bf16),
             pltpu.VMEM((owners, rows, 1), f32),
+            *weight_buffers(w_in),
         ],
         4 * owners * rows * width * (joined + GROUP * BLOCK) + 16 * half * width * lane,
         2 * owners * width * (joined + 2 * rows) + 8 * half * width,
@@ -859,7 +933,10 @@
         [first, hidden, taken, slots, gates, shared, w_down, s_down],
         [pl.BlockSpec(memory_space=pltpu.SMEM), growing(k, rows, units), growing(k, rows, width)]
         + [held_whole(*a.shape) for a in (slots, gates, shared)]
-        + [weights_of(w_down), held_whole(*s_down.shape)],
+        + [
+            pl.BlockSpec((1, units, width), lambda j: (j, 0, 0)),
+            held_whole(*s_down.shape),
+        ],
         outs,
         [growing(k, rows, width)] + [held_whole(*shape) for shape, _ in outs[1:]],
         kept,
@@ -896,19 +973,54 @@
     )(left, right, *kept, after)
 
 
+def rows_of_columns_kernel(came_ref, weights_ref, rows_ref, sum_ref):
+    blocks, _, three = came_ref.shape
+    part, width = three // 3, rows_ref.shape[1] // 3
+    total = 0.0
+    for block in range(blocks):
+        for i in range(3):
+            into = slice(i * width + block * part, i * width + (block + 1) * part)
+            values = came_ref[block, :, i * part : (i + 1) * part].astype(jnp.float32)
+            rows_ref[:, into] = values
+            weighted = values * weights_ref[:, into].astype(jnp.float32)
+            total = total + jnp.sum(weighted, axis=1, keepdims=True)
+    sum_ref[...] = total
+
+
+def rows_of_columns(came, weights):
+    return pl.pallas_call(
+        rows_of_columns_kernel,
+        out_shape=[
+            jax.ShapeDtypeStruct(weights.shape, jnp.float32),
+            jax.ShapeDtypeStruct((weights.shape[0], 1), jnp.float32),
+        ],
+        compiler_params=pltpu.CompilerParams(vmem_limit_bytes=VMEM),
+    )(came, weights)
+
+
 def shared_grads(rows_x, rows_g, hidden, joined, after):
-    half, width = rows_x[0].shape
-    near = pl.BlockSpec(memory_space=pltpu.VMEM)
-    outs = [(joined.shape[1], width), (hidden.shape[1], width)]
+    count, width = len(rows_x), rows_x[0].shape[1]
+    bf16, f32 = jnp.bfloat16, jnp.float32
+    far, near = pl.BlockSpec(memory_space=pltpu.HBM), pl.BlockSpec(memory_space=pltpu.VMEM)
+    wide, size = joined.shape[1], GROUP * BLOCK
     return pl.pallas_call(
-        shared_kernel,
-        in_specs=[near] * 6 + [pl.BlockSpec(memory_space=pltpu.HBM)],
+        functools.partial(shared_kernel, count=count),
+        in_specs=[far] * (2 * count) + [near] * 2 + [far],
         out_specs=[near] * 2,
-        out_shape=[jax.ShapeDtypeStruct(shape, jnp.float32) for shape in outs],
+        out_shape=[
+            jax.ShapeDtypeStruct((width, wide), bf16),
+            jax.ShapeDtypeStruct((hidden.shape[1], width), f32),
+        ],
+        scratch_shapes=[
+            pltpu.VMEM((2, size, width), bf16),
+            pltpu.VMEM((2, size, width), bf16),
+            pltpu.VMEM((wide, width), f32),
+            pltpu.SemaphoreType.DMA((2, 1 + GROUP)),
+        ],
         compiler_params=pltpu.CompilerParams(vmem_limit_bytes=VMEM),
         cost_estimate=pl.CostEstimate(
-            flops=4 * half * width * (joined.shape[1] + hidden.shape[1]),
-            bytes_accessed=8 * half * width,
+            flops=2 * hidden.shape[0] * width * (wide + hidden.shape[1]),
+            bytes_accessed=4 * hidden.shape[0] * width,
             transcendentals=0,
         ),
     )(*rows_x, *rows_g, hidden, joined, after)
@@ -955,9 +1067,8 @@
     qkv_part = lax.all_to_all(qkv_part, "ctx", split_axis=0, concat_axis=0, tiled=True)
     sequence = Transfer(gather_plane(tokens[0], False))
     small = jnp.concatenate([ranking.astype(bf16), jnp.pad(w_router, ((0, 0), (0, amount - EXPERTS)))])
-    small = small.reshape(-1, width)
-    held = small.shape[0]
-    small = jnp.pad(small, ((0, EXTRA - held), (0, 0)))
+    small = small.reshape(-1, EXTRA, amount).transpose(1, 0, 2).reshape(EXTRA, -1)
+    small = jnp.pad(small, ((0, 0), (0, width - small.shape[1])))
     own_grads = jnp.concatenate([cotangent[0], small], axis=0)
     grads = [Transfer(gather_plane(own_grads, False))]
     grad_blocks = [Transfer(turned(own_grads, k)) for k in range(1, min(3, planes))]
@@ -995,22 +1106,10 @@
     seq_rows = finish(clock, sequence)[0]
 
     first_expert = lax.rem(device * per_owner, EXPERTS)
-    first = jnp.stack([first_expert, device * per_owner // EXPERTS]).astype(jnp.int32)
+    first = [first_expert, device * per_owner // EXPERTS, ctx]
     back = lax.rem(plane - jnp.arange(planes, dtype=jnp.int32) + planes, planes)
-    sources = jnp.arange(n_ctx, dtype=jnp.int32) ^ ctx
-    sources = sources // 2 + (sources % 2) * (n_ctx // 2)
-    sources = (back[None, :] * n_ctx + sources[:, None]).reshape(-1)
-    ranks, slots, routers = [], [], []
-
-    def small_of(k):
-        sides = [side.reshape(-1, amount + EXTRA, width)[:, amount : amount + held] for side in grads[k].result]
-        came = jnp.concatenate(sides, axis=0).reshape(n_ctx, EXPERTS + rows, amount)
-        ranks.append(came[:, :EXPERTS])
-        routers.append(came[:, EXPERTS:])
-        mine = lax.dynamic_slice_in_dim(came, first_expert, per_owner, 1).astype(f32)
-        offset = (CAP * (jnp.arange(n_ctx) % GROUP)).astype(f32)[:, None, None]
-        mine = jnp.where(mine >= 0, mine + offset, -1.0)
-        slots.append(mine.transpose(1, 0, 2).reshape(per_owner, n_ctx * amount))
+    first = [jnp.stack([*first, back[k]]).astype(jnp.int32) for k in range(planes)]
+    ranks, slots = [], []
 
     lane = -(-units // BLOCK) * BLOCK
     s_down = jnp.pad(w_shared_down, ((0, lane - units), (0, 0)))
@@ -1020,12 +1119,12 @@
         nonlocal early_kept
         k, made = len(dhs), []
         if work and k < planes and k < len(grads) and grads[k].done:
-            small_of(k)
             early_kept, made = early(
-                k, planes, grads[k].result, slots[k], w_expert_down, s_down, early_kept, clock.token
+                k, planes, first[k], grads[k].result, rows, w_expert_down, s_down, early_kept, clock.token
             )
-            made = [made]
-        arrays = stage(clock, [*transfers, *grads, *grad_blocks], [*beside, *made])
+            for some, one in zip((ranks, slots), made[1:], strict=True):
+                some.append(one)
+        arrays = stage(clock, [*transfers, *grads, *grad_blocks], [*beside, *made[:1]])
         dhs.extend(arrays[len(beside) :])
         k = len(grads)
         if 2 <= k < planes and grad_blocks[k - 1].done and grads[-1].step is not grads[-1].opening:
@@ -1034,14 +1133,14 @@
             if len(grad_blocks) < planes - 1:
                 ahead = len(grad_blocks) + 1
                 source = own_grads if ahead == 3 else grad_blocks[-1].result
-                grad_blocks.append(Transfer(turned(clock.now(source), ahead if ahead == 3 else 1)))
+                grad_blocks.append(Transfer(turned(source, ahead if ahead == 3 else 1)))
         return arrays[: len(beside)]
 
     grads[-1].opening = None
     while not ring_w.done:
-        grads_stage([ring_w])
+        shared_in, own_grads = grads_stage([ring_w], [shared_in, own_grads])
     pieces = ring_w.result
-    shared_in = Transfer(exchanged(clock.now(shared_in)))
+    shared_in = Transfer(exchanged(shared_in))
     own_rows = tokens[0].astype(f32)
     plane_id = plane.reshape(1).astype(jnp.int32)
     *attended, normed, query, key, value, mixed, tops, totals = attend(
@@ -1050,12 +1149,13 @@
     saved = [normed, query, key, value, mixed, tops, totals]
     attended = grads_stage([shared_in], attended)
     attended = Transfer(scatter_plane(*attended))
+    shared_in = shared_in.result.reshape(width, 2, units)
+    s_in = jnp.pad(shared_in, ((0, 0), (0, 0), (0, lane - units))).reshape(width, 2 * lane)
+    (s_in,) = grads_stage([attended], [s_in])
     while not attended.done:
         grads_stage([attended])
     residual = own_rows + attended.result.astype(f32)
     ffn_own = rms_scale(residual, gain_two).astype(bf16)
-    shared_in = shared_in.result.reshape(width, 2, units)
-    s_in = jnp.pad(shared_in, ((0, 0), (0, 0), (0, lane - units))).reshape(width, 2 * lane)
 
     ffn, d_parts = [Transfer(gather_plane(ffn_own))], []
     block, d_sum = Transfer(turned(ffn_own)), None
@@ -1067,12 +1167,12 @@
             return []
         k = (len(out_parts) + 1) % planes
         late_kept, pair = late(
-            k, planes, first, mid_kept[1], early_kept[0], slots[k], mids[k][0], mids[k][2],
+            k, planes, first[k], mid_kept[1], early_kept[0], slots[k], mids[k][0], mids[k][2],
             w_expert_down, s_down, late_kept, clock.token,
         )
         return list(pair)
 
-    def outs_stage(transfers, beside=(), moving=None):
+    def outs_stage(transfers, beside=(), moving=None, adding=True, opening=True):
         nonlocal out_sum
         pair = do_late() if not beside else []
         if out_sum is None and len(out_parts) == planes and out_parts[0].done:
@@ -1080,11 +1180,11 @@
         going = [t for t in out_parts if not t.done]
         fresh = [t for t in going if t.step is t.opening]
         going = [t for t in going if t not in fresh]
+        fresh = fresh if opening else []
         if moving is not None:
             going = going[:moving]
-        arrays = stage(
-            clock, [*transfers, *going, *fresh, *([out_sum] if out_sum else [])], [*beside, *pair]
-        )
+        sums = [out_sum] if out_sum and adding else []
+        arrays = stage(clock, [*transfers, *going, *fresh, *sums], [*beside, *pair])
         if pair:
             out_parts.append(Transfer(scatter_plane(*arrays)))
             out_parts[-1].opening = out_parts[-1].step
@@ -1094,13 +1194,12 @@
     while d_sum is None or not d_sum.done:
         going = [*ffn, *d_parts, block, *([d_sum] if d_sum else [])]
         k = len(mids)
-        if router_t is None and len(routers) == planes:
-            router_full = jnp.stack(routers).reshape(devices, rows, amount)
-            router_full = jnp.take(router_full, sources, axis=0).reshape(width, amount)[:, :EXPERTS]
+        if router_t is None and len(ranks) == planes:
+            router_full = early_kept[2].reshape(width, amount)[:, :EXPERTS]
             router_t = router_full.T
         if k < planes and ffn[k].done and len(dhs) > k and router_t is not None:
             mid_kept, pair, made = middle(
-                k, planes, first, ffn[k].result, router_t, ranks[k], slots[k], w_expert_in, s_in,
+                k, planes, first[k], ffn[k].result, router_t, ranks[k], slots[k], w_expert_in, s_in,
                 early_kept[1], dhs[k], mid_kept, clock.token,
             )
             mids.append(made)
@@ -1137,24 +1236,28 @@
         if shared is not None:
             outs_stage([d_attn], moving=1)
             continue
-        parts = [
-            shared_grads(ffn[k].result, grads[k].result, mids[k][2], mids[k][3], clock.token)
-            for k in range(planes)
-        ]
-        into, shared_down_grad = (sum(one) for one in zip(*parts, strict=True))
-        into = into.reshape(2, lane, width)[:, :units].reshape(2 * units, width).T
-        small = contract_rows(ffn_own, clock.now(dlogits_b))
-        shared = jnp.concatenate([into, small, second_back[1][:, None]], axis=1).astype(bf16)
+        into, shared_down_grad = shared_grads(
+            [side for t in ffn for side in t.result],
+            [side for t in grads for side in t.result],
+            jnp.concatenate([made[2] for made in mids]),
+            jnp.concatenate([made[3] for made in mids]),
+            clock.token,
+        )
+        small = contract_rows(ffn_own, clock.now(dlogits_b)).astype(bf16)
+        gain = second_back[1][:, None].astype(bf16)
+        shared = jnp.concatenate([into[:, :units], into[:, lane : lane + units], small, gain], axis=1)
         shared = jnp.pad(shared, ((0, 0), (0, -shared.shape[1] % BLOCK)))
         shared = shared.reshape(devices, rows, -1)
-        shared, shared_down_grad = outs_stage([d_attn], [shared, shared_down_grad], moving=1)
+        shared, shared_down_grad = outs_stage(
+            [d_attn], [shared, shared_down_grad], moving=1, opening=False
+        )
     shared = Transfer(exchanged(shared))
 
     d_normed, ring_grad = attend_back(
         plane_id, d_attn.result, saved, tables, pieces, heads, clock.token
     )
     d_normed = outs_stage([shared], list(d_normed), moving=1)
-    ring_grad = Transfer(ring_sum(ring_grad))
+    ring_grad = Transfer(ring_sum([piece.reshape(-1, 4 * part) for piece in ring_grad]))
     d_normed = Transfer(scatter_plane(*d_normed))
 
     first_half = -(-per_owner // 2)
@@ -1171,14 +1274,14 @@
     while work or not (ring_grad.done and d_normed.done):
         if work:
             one = work.pop(0)(made)
-            (one,) = outs_stage([ring_grad, d_normed], [one], moving=1)
+            (one,) = outs_stage([ring_grad, d_normed], [one], 1, False)
             if work:
                 made = [one]
             else:
                 (expert_in_grad,), expert_down_grad = made, one
         else:
-            outs_stage([ring_grad, d_normed], [], moving=1)
-    ring_grad = ring_grad.result
+            outs_stage([ring_grad, d_normed], [], 1, False)
+    ring_grad = ring_grad.result.reshape(n_ctx, rows, 4 * part)
     qkv_grad = lax.all_to_all(ring_grad[:, :, : 3 * part], "ctx", split_axis=0, concat_axis=0, tiled=True)
     out_grad = ring_grad[:, :, 3 * part :].transpose(1, 0, 2).reshape(rows, width).astype(f32)
     first_back = jax.vjp(lambda x: rms_scale(x, gain_one), own_rows)[1](d_normed.result.astype(f32))
@@ -1194,9 +1297,8 @@
             out_sum = Transfer(staged_sum(out_parts))
         stage(clock, [*out_parts, *([out_sum] if out_sum else [])])
     result = (residual + out_sum.result.astype(f32)).astype(bf16)
-    qkv_grad = qkv_grad.reshape(n_ctx, rows, 3, part).transpose(1, 2, 0, 3)
-    qkv_grad = qkv_grad.reshape(rows, 3 * width).astype(f32)
-    gain_attn_grad = jnp.sum(qkv_grad * w_qkv.astype(f32), axis=1) / gain_attn.astype(f32)
+    qkv_grad, weighted = rows_of_columns(qkv_grad, w_qkv)
+    gain_attn_grad = weighted[:, 0] / gain_attn.astype(f32)
     return (
         result[None],
         tokens_grad[None],

time: 910 us -> 839 us (0.922)
  Pallas kernels: 447 us -> 407 us
  local copies, waits for them, and re-layouts: 80.3 us -> 65.7 us
  other arithmetic: 52.6 us -> 39.2 us
    pallas_call x26 -> x24, Pallas kernels: 125 us -> 97.5 us  [the longest x22 78.7 us: stage(): pl.pallas_call(kernel, in_specs=[far] * (first + len(taken)), out_specs=[...]
    unnamed x193 -> x180, local copies, waits for them, and re-layouts: 30.2 us -> 28.8 us
  transfers between devices with their start and end apart: 108 -> 108, of which waited for: 22 -> 23; matrix products, arithmetic and copies ran while one was open for 11% -> 9% of each run, Pallas kernels for 40% -> 40%
where the time goes in v3:
time: 839 us; the launch traced here: 830 us
  Pallas kernels  407 us (49%)
  waiting for transfers between devices  182 us (22%)
  starting transfers between devices  132 us (16%)
  local copies, waits for them, and re-layouts  65.7 us (8%)
  other arithmetic  39.2 us (5%)
    pallas_call x12, Pallas kernels, expert_call(): pl.pallas_call(functools.partial(kernel, carried=len(kept) + 1), grid=(ow...  215 us
    ppermute x85, waiting for transfers between devices, swap(): return lax.ppermute(values, 'ctx', [(i, i ^ bit) for i in range(count)])  132 us
    ppermute x85, starting transfers between devices, swap(): return lax.ppermute(values, 'ctx', [(i, i ^ bit) for i in range(count)])  85.8 us
    pallas_call x22, Pallas kernels, stage(): pl.pallas_call(kernel, in_specs=[far] * (first + len(taken)), out_specs=[...  78.7 us
    pallas_call x3, Pallas kernels, rows_grad(): pl.pallas_call(rows_kernel, grid=(count,), in_specs=[pl.BlockSpec((1, amo...  50 us
    ppermute x18, waiting for transfers between devices, turn(): lax.ppermute(values, 'fsdp', [(i, (i + step) % count) for i in range(coun...  47.6 us
    pallas_call x2, Pallas kernels, attend_call(): pl.pallas_call(kernel, in_specs=[pl.BlockSpec(memory_space=pltpu.SMEM)] +...  44.6 us
    unnamed x180, local copies, waits for them, and re-layouts  28.8 us
  transfers between devices with their start and end apart: 108, of which 23 were waited for; matrix products, arithmetic and copies ran while one was open for 9% of the time, Pallas kernels for 40%

profile of v3, /device:TPU:0, one launch (start us, length us, event | category | flops | bytes accessed | tf_op | source)
XLA Modules:
  0.0 830.3 jit_solution(17752883560527411630)
XLA Ops:
  18.8 4.2 collective-permute-start.2
  24.3 22.1 %collective-permute-done.2.refs_4_.refs_11_ = bf16[128,2048]{1,0:T(8,128)(2,1)} collective-permute-done((bf16[128,2048]{1,0:T(8,128)(2,1)S(1)}, bf16[128,2048]{1,0:T(8,128)(2,1)}, u32[]{:S(2)}, u32[]{:S(2)}) %collective-permute-start.2) | collective-permute-done | bytes 524320 | tf_op jit(solution)/shard_map/ppermute | solution.py:57
  46.4 9.1 %collective-permute-done.1.refs_3_.refs_7_ = bf16[144,2048]{1,0:T(8,128)(2,1)S(1)} collective-permute-done((bf16[144,2048]{1,0:T(8,128)(2,1)S(1)}, bf16[144,2048]{1,0:T(8,128)(2,1)S(1)}, u32[]{:S(2)}, u32[]{:S(2)}) %collective-permute-start.1) | collective-permute-done | bytes 589856 | tf_op jit(solution)/shard_map/ppermute | solution.py:62
  69.6 3.7 all-to-all-start.1
  88.9 3.9 shard_map.222
  95.4 25.3 %collective-permute-done.11.refs_1_.refs_10_.refs_16_ = bf16[8,64,1024]{2,1,0:T(8,128)(2,1)} collective-permute-done((bf16[8,64,1024]{2,1,0:T(8,128)(2,1)}, bf16[8,64,1024]{2,1,0:T(8,128)(2,1)}, u32[]{:S(2)}, u32[]{:S(2)}) %collective-permute-start.11) | collective-permute-done | bytes 1048608 | tf_op jit(solution)/shard_map/ppermute | solution.py:62
  122.7 4.1 collective-permute-start.20
  131.5 3.9 collective-permute-done.14.refs_4_.refs_8_
  141.7 12.2 %shard_map.224 = (bf16[4,640,2048]{2,1,0:T(8,128)(2,1)}, f32[4,640,704]{2,1,0:T(8,128)}, bf16[8,4,64,128]{3,2,1,0:T(8,128)(2,1)}, f32[1024,128]{1,0:T(8,128)}, f32[64,1024]{1,0:T(8,128)}, /*index=5*/f32[4,1024]{1,0:T(4,128)}) custom-call(s32[4]{0:T(128)} %get-tuple-element.470.refs_0_, bf16[576,2048]{1,0:T(8,128)(2,1)} %get-tuple-element.238.refs_1_.refs_8_, ...), custom_call_target="tpu_custom_call" | custom-call | flops 3724541952 | bytes 20971520 | tf_op jit(solution)/shard_map/pallas_call | solution.py:817
  153.9 5.9 collective-permute-done.20.refs_5_.refs_8_
  170.7 19.3 %shard_map.226 = (bf16[512,2048]{1,0:T(8,128)(2,1)}, bf16[512,2048]{1,0:T(8,128)(2,1)}, bf16[1024,2048]{1,0:T(8,128)(2,1)}, bf16[1024,256]{1,0:T(8,128)(2,1)}, b...) custom-call(s32[1]{0:T(128)} %bitcast.12.refs_0_, ...), custom_call_target="tpu_custom_call" | custom-call | flops 5368709120 | bytes 30000000 | tf_op jit(solution)/shard_map/pallas_call | solution.py:706
  204.8 12.2 %shard_map.228 = (bf16[4,640,2048]{2,1,0:T(8,128)(2,1)}, f32[4,640,704]{2,1,0:T(8,128)}, bf16[8,4,64,128]{3,2,1,0:T(8,128)(2,1)}, f32[1024,128]{1,0:T(8,128)}, f32[64,1024]{1,0:T(8,128)}, /*index=5*/f32[4,1024]{1,0:T(4,128)}) custom-call(s32[4]{0:T(128)} %get-tuple-element.469.refs_0_, ...), custom_call_target="tpu_custom_call", output_to_operand_aliasing={{0}: (5, {}), {1}: (6, {}), {2}: (7, {})} | custom-call | flops 3724541952 | bytes 20971520 | tf_op jit(solution)/shard_map/pallas_call | solution.py:817
  220.5 5.1 shard_map.229
  230.4 4.7 collective-permute-done.33.refs_7_
  236.9 23.0 %collective-permute-done.32.refs_6_ = bf16[80,2048]{1,0:T(8,128)(2,1)S(1)} collective-permute-done((bf16[80,2048]{1,0:T(8,128)(2,1)}, bf16[80,2048]{1,0:T(8,128)(2,1)S(1)}, u32[]{:S(2)}, u32[]{:S(2)}) %collective-permute-start.32) | collective-permute-done | bytes 327712 | tf_op jit(solution)/shard_map/ppermute | solution.py:57
  274.4 12.2 %shard_map.231 = (bf16[4,640,2048]{2,1,0:T(8,128)(2,1)}, f32[4,640,704]{2,1,0:T(8,128)}, bf16[8,4,64,128]{3,2,1,0:T(8,128)(2,1)}, f32[1024,128]{1,0:T(8,128)}, f32[64,1024]{1,0:T(8,128)}, /*index=5*/f32[4,1024]{1,0:T(4,128)}) custom-call(s32[4]{0:T(128)} %get-tuple-element.468.refs_0_, ...), custom_call_target="tpu_custom_call", output_to_operand_aliasing={{0}: (5, {}), {1}: (6, {}), {2}: (7, {})} | custom-call | flops 3724541952 | bytes 20971520 | tf_op jit(solution)/shard_map/pallas_call | solution.py:817
  286.6 8.9 %collective-permute-done.37.refs_5_ = bf16[128,2048]{1,0:T(8,128)(2,1)} collective-permute-done((bf16[128,2048]{1,0:T(8,128)(2,1)S(1)}, bf16[128,2048]{1,0:T(8,128)(2,1)}, u32[]{:S(2)}, u32[]{:S(2)}) %collective-permute-start.37) | collective-permute-done | bytes 524320 | tf_op jit(solution)/shard_map/ppermute | solution.py:57
  304.8 12.2 %shard_map.233 = (bf16[4,640,2048]{2,1,0:T(8,128)(2,1)}, f32[4,640,704]{2,1,0:T(8,128)}, bf16[8,4,64,128]{3,2,1,0:T(8,128)(2,1)}, f32[1024,128]{1,0:T(8,128)}, f32[64,1024]{1,0:T(8,128)}, /*index=5*/f32[4,1024]{1,0:T(4,128)}) custom-call(s32[4]{0:T(128)} %get-tuple-element.455.refs_0_, ...), custom_call_target="tpu_custom_call", output_to_operand_aliasing={{0}: (5, {}), {1}: (6, {}), {2}: (7, {})} | custom-call | flops 3724541952 | bytes 20971520 | tf_op jit(solution)/shard_map/pallas_call | solution.py:817
  317.0 9.4 %collective-permute-done.42.refs_5_ = bf16[128,2048]{1,0:T(8,128)(2,1)} collective-permute-done((bf16[128,2048]{1,0:T(8,128)(2,1)}, bf16[128,2048]{1,0:T(8,128)(2,1)}, u32[]{:S(2)}, u32[]{:S(2)}) %collective-permute-start.42) | collective-permute-done | bytes 524320 | tf_op jit(solution)/shard_map/ppermute | solution.py:57
  336.7 27.7 %shard_map.235 = (bf16[4,640,2048]{2,1,0:T(8,128)(2,1)}, bf16[4,640,704]{2,1,0:T(8,128)(2,1)}, bf16[4,640,1408]{2,1,0:T(8,128)(2,1)}, bf16[576,2048]{1,0:T(8,128...) custom-call(s32[4]{0:T(128)} %get-tuple-element.470.refs_0_, ...), custom_call_target="tpu_custom_call" | custom-call | flops 12213813248 | bytes 36700160 | tf_op jit(solution)/shard_map/pallas_call | solution.py:817
  372.3 27.9 %shard_map.237 = (bf16[4,640,2048]{2,1,0:T(8,128)(2,1)}, bf16[4,640,704]{2,1,0:T(8,128)(2,1)}, bf16[4,640,1408]{2,1,0:T(8,128)(2,1)}, bf16[576,2048]{1,0:T(8,128...) custom-call(s32[4]{0:T(128)} %get-tuple-element.469.refs_0_, ...), custom_call_target="tpu_custom_call", output_to_operand_aliasing={{0}: (10, {}), {1}: (11, {}), {2}: (12, {})} | custom-call | flops 12213813248 | bytes 36700160 | tf_op jit(solution)/shard_map/pallas_call | solution.py:817
  401.7 5.1 shard_map.238
  410.9 28.1 %shard_map.239 = (bf16[4,640,2048]{2,1,0:T(8,128)(2,1)}, bf16[4,640,704]{2,1,0:T(8,128)(2,1)}, bf16[4,640,1408]{2,1,0:T(8,128)(2,1)}, bf16[576,2048]{1,0:T(8,128...) custom-call(s32[4]{0:T(128)} %get-tuple-element.468.refs_0_, ...), custom_call_target="tpu_custom_call", output_to_operand_aliasing={{0}: (10, {}), {1}: (11, {}), {2}: (12, {})} | custom-call | flops 12213813248 | bytes 36700160 | tf_op jit(solution)/shard_map/pallas_call | solution.py:817
  440.4 4.5 shard_map.240
  448.5 27.8 %shard_map.241 = (bf16[4,640,2048]{2,1,0:T(8,128)(2,1)}, bf16[4,640,704]{2,1,0:T(8,128)(2,1)}, bf16[4,640,1408]{2,1,0:T(8,128)(2,1)}, bf16[576,2048]{1,0:T(8,128...) custom-call(s32[4]{0:T(128)} %get-tuple-element.455.refs_0_, ...), custom_call_target="tpu_custom_call", output_to_operand_aliasing={{0}: (10, {}), {1}: (11, {}), {2}: (12, {})} | custom-call | flops 12213813248 | bytes 36700160 | tf_op jit(solution)/shard_map/pallas_call | solution.py:817
  477.8 4.5 shard_map.242
  487.5 13.7 %shard_map.243 = (bf16[4,640,2048]{2,1,0:T(8,128)(2,1)}, bf16[512,2048]{1,0:T(8,128)(2,1)}, bf16[512,2048]{1,0:T(8,128)(2,1)}) custom-call(s32[4]{0:T(128)} %get-tuple-element.469.refs_0_, bf16[4,640,704]{2,1,0:T(8,128)(2,1)} %get-tuple-element.337.refs_1_.left_ref, bf16[4,640,2048]{2,1,0:T(8,128)(2,1)} %get-tuple-element.338.refs_2_, ...), custom_call_target="tpu_custom_call" | custom-call | flops 3724541952 | bytes 20971520 | tf_op jit(solution)/shard_map/pallas_call | solution.py:817
  501.2 12.3 %collective-permute-done.65.refs_5_ = bf16[144,2048]{1,0:T(8,128)(2,1)} collective-permute-done((bf16[144,2048]{1,0:T(8,128)(2,1)}, bf16[144,2048]{1,0:T(8,128)(2,1)}, u32[]{:S(2)}, u32[]{:S(2)}) %collective-permute-start.65) | collective-permute-done | bytes 589856 | tf_op jit(solution)/shard_map/ppermute | solution.py:57
  514.9 4.5 shard_map.244
  526.8 13.6 %shard_map.245 = (bf16[4,640,2048]{2,1,0:T(8,128)(2,1)}, bf16[512,2048]{1,0:T(8,128)(2,1)}, bf16[512,2048]{1,0:T(8,128)(2,1)}) custom-call(s32[4]{0:T(128)} %get-tuple-element.468.refs_0_, bf16[4,640,704]{2,1,0:T(8,128)(2,1)} %get-tuple-element.337.refs_1_.left_ref, ...), custom_call_target="tpu_custom_call", output_to_operand_aliasing={{0}: (8, {})} | custom-call | flops 3724541952 | bytes 20971520 | tf_op jit(solution)/shard_map/pallas_call | solution.py:817
  540.4 11.5 %collective-permute-done.70.refs_5_ = bf16[144,2048]{1,0:T(8,128)(2,1)S(1)} collective-permute-done((bf16[144,2048]{1,0:T(8,128)(2,1)}, bf16[144,2048]{1,0:T(8,128)(2,1)S(1)}, u32[]{:S(2)}, u32[]{:S(2)}) %collective-permute-start.70) | collective-permute-done | bytes 589856 | tf_op jit(solution)/shard_map/ppermute | solution.py:57
  552.9 4.0 shard_map.246
  562.2 14.0 %shard_map.247 = (bf16[4,640,2048]{2,1,0:T(8,128)(2,1)}, bf16[512,2048]{1,0:T(8,128)(2,1)}, bf16[512,2048]{1,0:T(8,128)(2,1)}) custom-call(s32[4]{0:T(128)} %get-tuple-element.455.refs_0_, bf16[4,640,704]{2,1,0:T(8,128)(2,1)} %get-tuple-element.337.refs_1_.left_ref, ...), custom_call_target="tpu_custom_call", output_to_operand_aliasing={{0}: (8, {})} | custom-call | flops 3724541952 | bytes 20971520 | tf_op jit(solution)/shard_map/pallas_call | solution.py:817
  576.4 9.1 %collective-permute-done.75.refs_5_ = bf16[128,2048]{1,0:T(8,128)(2,1)} collective-permute-done((bf16[128,2048]{1,0:T(8,128)(2,1)}, bf16[128,2048]{1,0:T(8,128)(2,1)}, u32[]{:S(2)}, u32[]{:S(2)}) %collective-permute-start.75) | collective-permute-done | bytes 524320 | tf_op jit(solution)/shard_map/ppermute | solution.py:57
  585.6 4.1 shard_map.248
  597.2 13.6 %shard_map.249 = (bf16[4,640,2048]{2,1,0:T(8,128)(2,1)}, bf16[512,2048]{1,0:T(8,128)(2,1)}, bf16[512,2048]{1,0:T(8,128)(2,1)}) custom-call(s32[4]{0:T(128)} %get-tuple-element.470.refs_0_, bf16[4,640,704]{2,1,0:T(8,128)(2,1)} %get-tuple-element.337.refs_1_.left_ref, ...), custom_call_target="tpu_custom_call", output_to_operand_aliasing={{0}: (8, {})} | custom-call | flops 3724541952 | bytes 20971520 | tf_op jit(solution)/shard_map/pallas_call | solution.py:817
  610.8 9.3 %collective-permute-done.79.refs_4_ = bf16[128,2048]{1,0:T(8,128)(2,1)S(1)} collective-permute-done((bf16[128,2048]{1,0:T(8,128)(2,1)S(1)}, bf16[128,2048]{1,0:T(8,128)(2,1)S(1)}, u32[]{:S(2)}, u32[]{:S(2)}) %collective-permute-start.79) | collective-permute-done | bytes 524320 | tf_op jit(solution)/shard_map/ppermute | solution.py:57
  620.9 5.0 shard_map.250
  635.4 16.1 %shard_map.251 = (bf16[2048,256]{1,0:T(8,128)(2,1)}, f32[128,2048]{1,0:T(8,128)}) custom-call(bf16[512,2048]{1,0:T(8,128)(2,1)} %get-tuple-element.282.refs_1_.refs_0_, bf16[512,2048]{1,0:T(8,128)(2,1)} %copy-done.12, bf16[512,2048]{1,0:T(8,128)(2,1)} %get-tuple-element.292.refs_1_.refs_2_, bf16[512,2048]{1,0:T(8,128)(2,1)} %copy-done.8, ...), custom_call_target="tpu_custom_call" | custom-call | flops 6442450944 | bytes 33554432 | tf_op jit(solution)/shard_map/pallas_call | solution.py:1006
  659.4 3.8 all-to-all-start.3
  670.9 25.3 %shard_map.253 = (bf16[512,2048]{1,0:T(8,128)(2,1)}, bf16[512,2048]{1,0:T(8,128)(2,1)}, bf16[8,64,1024]{2,1,0:T(8,128)(2,1)}, bf16[8,64,1024]{2,1,0:T(8,128)(2,1...) custom-call(s32[1]{0:T(128)} %bitcast.12.refs_0_, f32[1024,128]{1,0:T(8,128)} %get-tuple-element.245.refs_2_.refs_1_, ...), custom_call_target="tpu_custom_call" | custom-call | flops 11274289152 | bytes 30000000 | tf_op jit(solution)/shard_map/pallas_call | solution.py:706
  696.3 4.5 collective-permute-done.90.refs_7_
  701.8 4.0 shard_map.254
  713.6 16.7 %shard_map.255.refs_1_ = f32[4,2048,1408]{2,1,0:T(8,128)} custom-call(bf16[4,640,2048]{2,1,0:T(8,128)(2,1)} %get-tuple-element.417.left_ref, bf16[4,640,1408]{2,1,0:T(8,128)(2,1)} %get-tuple-element.418.right_ref, f32[8,128]{1,0:T(8,128)} %get-tuple-element.416.refs_0_), custom_call_target="tpu_custom_call" | custom-call | flops 7381975040 | bytes 23068672 | tf_op jit(solution)/shard_map/pallas_call | solution.py:956
  735.8 5.8 shard_map.256
  750.1 16.7 %shard_map.257.refs_1_ = f32[4,2048,1408]{2,1,0:T(8,128)} custom-call(bf16[4,640,2048]{2,1,0:T(8,128)(2,1)} %get-tuple-element.417.left_ref, bf16[4,640,1408]{2,1,0:T(8,128)(2,1)} %get-tuple-element.418.right_ref, f32[4,2048,1408]{2,1,0:T(8,128)} %get-tuple-element.430.refs_0_, ...), custom_call_target="tpu_custom_call", output_to_operand_aliasing={{}: (2, {})} | custom-call | flops 7381975040 | bytes 23068672 | tf_op jit(solution)/shard_map/pallas_call | solution.py:956
  766.8 4.8 collective-permute-done.100.refs_5_
  782.8 16.6 %shard_map.259.refs_1_ = f32[4,704,2048]{2,1,0:T(8,128)} custom-call(bf16[4,640,704]{2,1,0:T(8,128)(2,1)} %get-tuple-element.337.refs_1_.left_ref, bf16[4,640,2048]{2,1,0:T(8,128)(2,1)} %get-tuple-element.439.right_ref, f32[8,128]{1,0:T(8,128)} %get-tuple-element.438.refs_0_), custom_call_target="tpu_custom_call" | custom-call | flops 7381975040 | bytes 23068672 | tf_op jit(solution)/shard_map/pallas_call | solution.py:956
  (472 shorter events, 271.6 us)
Async XLA Ops:
  7.1 48.5 %all-to-all-start = ((bf16[8,64,768]{2,1,0:T(8,128)(2,1)}), bf16[8,64,768]{2,1,0:T(8,128)(2,1)S(1)}, u32[]{:S(2)}, u32[]{:S(2)}) async-start(bf16[8,64,768]{2,1,0:T(8,128)(2,1)} %reshape.246), calls=%async_computation | async-start | bytes 1572864 | tf_op jit(solution)/shard_map/all_to_all | solution.py:1067
  11.1 35.3 %collective-permute-start.5 = (bf16[144,2048]{1,0:T(8,128)(2,1)S(1)}, bf16[144,2048]{1,0:T(8,128)(2,1)}, u32[]{:S(2)}, u32[]{:S(2)}) collective-permute-start(bf16[144,2048]{1,0:T(8,128)(2,1)S(1)} %fusion.14.refs_15_.refs_2_), channel_id=1, source_target_pairs={{0,16},{4,20},{8,24},{12,28},{16,0},{20,4},{24,8},{28,12},{1,17},{... | collective-permute-start | bytes 1769480 | tf_op jit(solution)/shard_map/ppermute | solution.py:57
  13.1 33.3 %collective-permute-start.4 = (bf16[144,2048]{1,0:T(8,128)(2,1)S(1)}, bf16[144,2048]{1,0:T(8,128)(2,1)}, u32[]{:S(2)}, u32[]{:S(2)}) collective-permute-start(bf16[144,2048]{1,0:T(8,128)(2,1)S(1)} %fusion.14.refs_15_.refs_2_), channel_id=1, source_target_pairs={{0,8},{4,12},{8,0},{12,4},{16,24},{20,28},{24,16},{28,20},{1,9},{5... | collective-permute-start | bytes 1769480 | tf_op jit(solution)/shard_map/ppermute | solution.py:57
  14.6 41.0 %collective-permute-start.1 = (bf16[144,2048]{1,0:T(8,128)(2,1)S(1)}, bf16[144,2048]{1,0:T(8,128)(2,1)S(1)}, u32[]{:S(2)}, u32[]{:S(2)}) collective-permute-start(bf16[144,2048]{1,0:T(8,128)(2,1)S(1)} %fusion.14.refs_15_.refs_2_), channel_id=1, source_target_pairs={{0,2},{1,3},{2,0},{3,1},{4,6},{5,7},{6,4},{7,5},{8,10},{9,11},{10,... | collective-permute-start | bytes 1769480 | tf_op jit(solution)/shard_map/ppermute | solution.py:62
  17.2 38.4 %collective-permute-start = (bf16[144,2048]{1,0:T(8,128)(2,1)S(1)}, bf16[144,2048]{1,0:T(8,128)(2,1)S(1)}, u32[]{:S(2)}, u32[]{:S(2)}) collective-permute-start(bf16[144,2048]{1,0:T(8,128)(2,1)S(1)} %fusion.14.refs_15_.refs_2_), channel_id=1, source_target_pairs={{0,1},{1,2},{2,3},{3,0},{4,5},{5,6},{6,7},{7,4},{8,9},{9,10},{10,1... | collective-permute-start | bytes 1769480 | tf_op jit(solution)/shard_map/ppermute | solution.py:62
  92.8 42.7 %collective-permute-start.13 = (bf16[576,2048]{1,0:T(8,128)(2,1)}, bf16[576,2048]{1,0:T(8,128)(2,1)S(1)}, u32[]{:S(2)}, u32[]{:S(2)}) collective-permute-start(bf16[576,2048]{1,0:T(8,128)(2,1)} %get-tuple-element.238.refs_1_.refs_8_), channel_id=1, source_target_pairs={{0,4},{4,0},{8,12},{12,8},{16,20},{20,16},{24,28},{28,24},{1,5},{5... | collective-permute-start | bytes 7077896 | tf_op jit(solution)/shard_map/ppermute | solution.py:57
  93.0 42.5 %collective-permute-start.12 = (bf16[512,2048]{1,0:T(8,128)(2,1)}, bf16[512,2048]{1,0:T(8,128)(2,1)}, u32[]{:S(2)}, u32[]{:S(2)}) collective-permute-start(bf16[512,2048]{1,0:T(8,128)(2,1)} %get-tuple-element.237.refs_6_), channel_id=1, source_target_pairs={{0,4},{4,0},{8,12},{12,8},{16,20},{20,16},{24,28},{28,24},{1,5},{5... | collective-permute-start | bytes 6291464 | tf_op jit(solution)/shard_map/ppermute | solution.py:57
  94.0 28.7 %collective-permute-start.15 = (bf16[144,2048]{1,0:T(8,128)(2,1)}, bf16[144,2048]{1,0:T(8,128)(2,1)}, u32[]{:S(2)}, u32[]{:S(2)}) collective-permute-start(bf16[144,2048]{1,0:T(8,128)(2,1)} %copy-done.25), channel_id=1, source_target_pairs={{0,16},{4,20},{8,24},{12,28},{16,0},{20,4},{24,8},{28,12},{1,17},{... | collective-permute-start | bytes 1769480 | tf_op jit(solution)/shard_map/ppermute | solution.py:57
  120.7 39.1 %collective-permute-start.16 = (bf16[8,64,1024]{2,1,0:T(8,128)(2,1)}, bf16[8,64,1024]{2,1,0:T(8,128)(2,1)}, u32[]{:S(2)}, u32[]{:S(2)}) collective-permute-start(bf16[8,64,1024]{2,1,0:T(8,128)(2,1)} %collective-permute-done.11.refs_1_.refs_10_.refs_16_), channel_id=1, source_target_pairs={{0,1},{1,2},{2,3},{3,0},{4,5},{5,6},{6,7},{7,4},{8,9},{9,10},{10,1... | collective-permute-start | bytes 3145736 | tf_op jit(solution)/shard_map/ppermute | solution.py:62
  122.7 37.1 %collective-permute-start.20 = (bf16[144,2048]{1,0:T(8,128)(2,1)S(1)}, bf16[144,2048]{1,0:T(8,128)(2,1)}, u32[]{:S(2)}, u32[]{:S(2)}) collective-permute-start(bf16[144,2048]{1,0:T(8,128)(2,1)S(1)} %copy-done.19), channel_id=1, source_target_pairs={{0,3},{1,0},{2,1},{3,2},{4,7},{5,4},{6,5},{7,6},{8,11},{9,8},{10,9... | collective-permute-start | bytes 1769480 | tf_op jit(solution)/shard_map/ppermute | solution.py:62
  163.2 30.2 %collective-permute-start.19 = (bf16[576,2048]{1,0:T(8,128)(2,1)}, bf16[576,2048]{1,0:T(8,128)(2,1)S(1)}, u32[]{:S(2)}, u32[]{:S(2)}) collective-permute-start(bf16[576,2048]{1,0:T(8,128)(2,1)} %get-tuple-element.252.refs_1_.refs_10_), channel_id=1, source_target_pairs={{0,4},{4,0},{8,12},{12,8},{16,20},{20,16},{24,28},{28,24},{1,5},{5... | collective-permute-start | bytes 7077896 | tf_op jit(solution)/shard_map/ppermute | solution.py:57
  163.3 30.2 %all-to-all-start.2 = ((bf16[32,64,176]{2,1,0:T(8,128)(2,1)}), bf16[32,64,176]{2,1,0:T(8,128)(2,1)}, u32[]{:S(2)}, u32[]{:S(2)}) async-start(bf16[32,64,176]{2,1,0:T(8,128)(2,1)} %get-tuple-element.251), calls=%async_computation.2 | async-start | bytes 2097152 | tf_op jit(solution)/shard_map/all_to_all | solution.py:225
  225.6 34.4 %collective-permute-start.28 = (bf16[576,2048]{1,0:T(8,128)(2,1)}, bf16[576,2048]{1,0:T(8,128)(2,1)S(1)}, u32[]{:S(2)}, u32[]{:S(2)}) collective-permute-start(bf16[576,2048]{1,0:T(8,128)(2,1)} %get-tuple-element.263.refs_1_.refs_12_), channel_id=1, source_target_pairs={{0,4},{4,0},{8,12},{12,8},{16,20},{20,16},{24,28},{28,24},{1,5},{5... | collective-permute-start | bytes 7077896 | tf_op jit(solution)/shard_map/ppermute | solution.py:57
  226.9 33.1 %collective-permute-start.29 = (bf16[128,2048]{1,0:T(8,128)(2,1)}, bf16[128,2048]{1,0:T(8,128)(2,1)S(1)}, u32[]{:S(2)}, u32[]{:S(2)}) collective-permute-start(bf16[128,2048]{1,0:T(8,128)(2,1)} %get-tuple-element.264), channel_id=1, source_target_pairs={{0,8},{4,12},{8,0},{12,4},{16,24},{20,28},{24,16},{28,20},{1,9},{5... | collective-permute-start | bytes 1572872 | tf_op jit(solution)/shard_map/ppermute | solution.py:57
  227.8 32.2 %collective-permute-start.30 = (bf16[128,2048]{1,0:T(8,128)(2,1)}, bf16[128,2048]{1,0:T(8,128)(2,1)S(1)}, u32[]{:S(2)}, u32[]{:S(2)}) collective-permute-start(bf16[128,2048]{1,0:T(8,128)(2,1)} %get-tuple-element.265), channel_id=1, source_target_pairs={{0,16},{4,20},{8,24},{12,28},{16,0},{20,4},{24,8},{28,12},{1,17},{... | collective-permute-start | bytes 1572872 | tf_op jit(solution)/shard_map/ppermute | solution.py:57
  229.0 31.1 %collective-permute-start.31 = (bf16[128,2048]{1,0:T(8,128)(2,1)}, bf16[128,2048]{1,0:T(8,128)(2,1)S(1)}, u32[]{:S(2)}, u32[]{:S(2)}) collective-permute-start(bf16[128,2048]{1,0:T(8,128)(2,1)} %get-tuple-element.266), channel_id=1, source_target_pairs={{0,24},{4,28},{8,16},{12,20},{16,8},{20,12},{24,0},{28,4},{1,25},{... | collective-permute-start | bytes 1572872 | tf_op jit(solution)/shard_map/ppermute | solution.py:57
  265.5 30.0 %collective-permute-start.35 = (bf16[576,2048]{1,0:T(8,128)(2,1)}, bf16[576,2048]{1,0:T(8,128)(2,1)S(1)}, u32[]{:S(2)}, u32[]{:S(2)}) collective-permute-start(bf16[576,2048]{1,0:T(8,128)(2,1)} %get-tuple-element.276.refs_1_.refs_14_), channel_id=1, source_target_pairs={{0,4},{4,0},{8,12},{12,8},{16,20},{20,16},{24,28},{28,24},{1,5},{5... | collective-permute-start | bytes 7077896 | tf_op jit(solution)/shard_map/ppermute | solution.py:57
  330.4 34.0 %collective-permute-start.44 = (bf16[512,2048]{1,0:T(8,128)(2,1)}, bf16[512,2048]{1,0:T(8,128)(2,1)S(1)}, u32[]{:S(2)}, u32[]{:S(2)}) collective-permute-start(bf16[512,2048]{1,0:T(8,128)(2,1)} %get-tuple-element.292.refs_1_.refs_2_), channel_id=1, source_target_pairs={{0,4},{4,0},{8,12},{12,8},{16,20},{20,16},{24,28},{28,24},{1,5},{5... | collective-permute-start | bytes 6291464 | tf_op jit(solution)/shard_map/ppermute | solution.py:57
  330.5 33.9 %collective-permute-start.48 = (bf16[128,2048]{1,0:T(8,128)(2,1)}, bf16[128,2048]{1,0:T(8,128)(2,1)}, u32[]{:S(2)}, u32[]{:S(2)}) collective-permute-start(bf16[128,2048]{1,0:T(8,128)(2,1)} %copy-done.33), channel_id=1, source_target_pairs={{0,24},{4,28},{8,16},{12,20},{16,8},{20,12},{24,0},{28,4},{1,25},{... | collective-permute-start | bytes 1572872 | tf_op jit(solution)/shard_map/ppermute | solution.py:57
  331.8 32.6 %collective-permute-start.47 = (bf16[128,2048]{1,0:T(8,128)(2,1)}, bf16[128,2048]{1,0:T(8,128)(2,1)}, u32[]{:S(2)}, u32[]{:S(2)}) collective-permute-start(bf16[128,2048]{1,0:T(8,128)(2,1)} %copy-done.33), channel_id=1, source_target_pairs={{0,16},{4,20},{8,24},{12,28},{16,0},{20,4},{24,8},{28,12},{1,17},{... | collective-permute-start | bytes 1572872 | tf_op jit(solution)/shard_map/ppermute | solution.py:57
  333.2 31.2 %collective-permute-start.46 = (bf16[128,2048]{1,0:T(8,128)(2,1)}, bf16[128,2048]{1,0:T(8,128)(2,1)}, u32[]{:S(2)}, u32[]{:S(2)}) collective-permute-start(bf16[128,2048]{1,0:T(8,128)(2,1)} %copy-done.33), channel_id=1, source_target_pairs={{0,8},{4,12},{8,0},{12,4},{16,24},{20,28},{24,16},{28,20},{1,9},{5... | collective-permute-start | bytes 1572872 | tf_op jit(solution)/shard_map/ppermute | solution.py:57
  334.1 30.4 %collective-permute-start.45 = (bf16[128,2048]{1,0:T(8,128)(2,1)}, bf16[128,2048]{1,0:T(8,128)(2,1)}, u32[]{:S(2)}, u32[]{:S(2)}) collective-permute-start(bf16[128,2048]{1,0:T(8,128)(2,1)} %copy-done.33), channel_id=1, source_target_pairs={{0,1},{1,2},{2,3},{3,0},{4,5},{5,6},{6,7},{7,4},{8,9},{9,10},{10,1... | collective-permute-start | bytes 1572872 | tf_op jit(solution)/shard_map/ppermute | solution.py:62
  368.2 32.0 %collective-permute-start.53 = (bf16[576,2048]{1,0:T(8,128)(2,1)}, bf16[576,2048]{1,0:T(8,128)(2,1)}, u32[]{:S(2)}, u32[]{:S(2)}) collective-permute-start(bf16[576,2048]{1,0:T(8,128)(2,1)} %get-tuple-element.303), channel_id=1, source_target_pairs={{0,4},{4,0},{8,12},{12,8},{16,20},{20,16},{24,28},{28,24},{1,5},{5... | collective-permute-start | bytes 7077896 | tf_op jit(solution)/shard_map/ppermute | solution.py:57
  368.3 31.9 %collective-permute-start.49 = (bf16[512,2048]{1,0:T(8,128)(2,1)}, bf16[512,2048]{1,0:T(8,128)(2,1)S(1)}, u32[]{:S(2)}, u32[]{:S(2)}) collective-permute-start(bf16[512,2048]{1,0:T(8,128)(2,1)} %get-tuple-element.302.refs_1_.refs_4_), channel_id=1, source_target_pairs={{0,4},{4,0},{8,12},{12,8},{16,20},{20,16},{24,28},{28,24},{1,5},{5... | collective-permute-start | bytes 6291464 | tf_op jit(solution)/shard_map/ppermute | solution.py:57
  368.8 31.4 %collective-permute-start.52 = (bf16[128,2048]{1,0:T(8,128)(2,1)}, bf16[128,2048]{1,0:T(8,128)(2,1)S(1)}, u32[]{:S(2)}, u32[]{:S(2)}) collective-permute-start(bf16[128,2048]{1,0:T(8,128)(2,1)} %collective-permute-done.45.refs_4_.refs_7_), channel_id=1, source_target_pairs={{0,24},{4,28},{8,16},{12,20},{16,8},{20,12},{24,0},{28,4},{1,25},{... | collective-permute-start | bytes 1572872 | tf_op jit(solution)/shard_map/ppermute | solution.py:57
  370.2 30.0 %collective-permute-start.51 = (bf16[128,2048]{1,0:T(8,128)(2,1)}, bf16[128,2048]{1,0:T(8,128)(2,1)}, u32[]{:S(2)}, u32[]{:S(2)}) collective-permute-start(bf16[128,2048]{1,0:T(8,128)(2,1)} %collective-permute-done.45.refs_4_.refs_7_), channel_id=1, source_target_pairs={{0,16},{4,20},{8,24},{12,28},{16,0},{20,4},{24,8},{28,12},{1,17},{... | collective-permute-start | bytes 1572872 | tf_op jit(solution)/shard_map/ppermute | solution.py:57
  406.8 32.2 %collective-permute-start.58 = (bf16[576,2048]{1,0:T(8,128)(2,1)}, bf16[576,2048]{1,0:T(8,128)(2,1)}, u32[]{:S(2)}, u32[]{:S(2)}) collective-permute-start(bf16[576,2048]{1,0:T(8,128)(2,1)} %get-tuple-element.319), channel_id=1, source_target_pairs={{0,4},{4,0},{8,12},{12,8},{16,20},{20,16},{24,28},{28,24},{1,5},{5... | collective-permute-start | bytes 7077896 | tf_op jit(solution)/shard_map/ppermute | solution.py:57
  406.9 32.1 %collective-permute-start.54 = (bf16[512,2048]{1,0:T(8,128)(2,1)}, bf16[512,2048]{1,0:T(8,128)(2,1)S(1)}, u32[]{:S(2)}, u32[]{:S(2)}) collective-permute-start(bf16[512,2048]{1,0:T(8,128)(2,1)} %get-tuple-element.314.refs_1_.refs_6_), channel_id=1, source_target_pairs={{0,4},{4,0},{8,12},{12,8},{16,20},{20,16},{24,28},{28,24},{1,5},{5... | collective-permute-start | bytes 6291464 | tf_op jit(solution)/shard_map/ppermute | solution.py:57
  407.4 31.6 %collective-permute-start.55 = (bf16[144,2048]{1,0:T(8,128)(2,1)}, bf16[144,2048]{1,0:T(8,128)(2,1)}, u32[]{:S(2)}, u32[]{:S(2)}) collective-permute-start(bf16[144,2048]{1,0:T(8,128)(2,1)} %get-tuple-element.315), channel_id=1, source_target_pairs={{0,8},{4,12},{8,0},{12,4},{16,24},{20,28},{24,16},{28,20},{1,9},{5... | collective-permute-start | bytes 1769480 | tf_op jit(solution)/shard_map/ppermute | solution.py:57
  408.8 30.2 %collective-permute-start.56 = (bf16[144,2048]{1,0:T(8,128)(2,1)}, bf16[144,2048]{1,0:T(8,128)(2,1)}, u32[]{:S(2)}, u32[]{:S(2)}) collective-permute-start(bf16[144,2048]{1,0:T(8,128)(2,1)} %get-tuple-element.316), channel_id=1, source_target_pairs={{0,16},{4,20},{8,24},{12,28},{16,0},{20,4},{24,8},{28,12},{1,17},{... | collective-permute-start | bytes 1769480 | tf_op jit(solution)/shard_map/ppermute | solution.py:57
  409.4 29.6 %collective-permute-start.57 = (bf16[144,2048]{1,0:T(8,128)(2,1)}, bf16[144,2048]{1,0:T(8,128)(2,1)}, u32[]{:S(2)}, u32[]{:S(2)}) collective-permute-start(bf16[144,2048]{1,0:T(8,128)(2,1)} %get-tuple-element.317), channel_id=1, source_target_pairs={{0,24},{4,28},{8,16},{12,20},{16,8},{20,12},{24,0},{28,4},{1,25},{... | collective-permute-start | bytes 1769480 | tf_op jit(solution)/shard_map/ppermute | solution.py:57
  444.9 31.5 %collective-permute-start.62 = (bf16[576,2048]{1,0:T(8,128)(2,1)}, bf16[576,2048]{1,0:T(8,128)(2,1)S(1)}, u32[]{:S(2)}, u32[]{:S(2)}) collective-permute-start(bf16[576,2048]{1,0:T(8,128)(2,1)} %get-tuple-element.334), channel_id=1, source_target_pairs={{0,4},{4,0},{8,12},{12,8},{16,20},{20,16},{24,28},{28,24},{1,5},{5... | collective-permute-start | bytes 7077896 | tf_op jit(solution)/shard_map/ppermute | solution.py:57
  445.0 31.4 %collective-permute-start.59 = (bf16[144,2048]{1,0:T(8,128)(2,1)}, bf16[144,2048]{1,0:T(8,128)(2,1)}, u32[]{:S(2)}, u32[]{:S(2)}) collective-permute-start(bf16[144,2048]{1,0:T(8,128)(2,1)} %get-tuple-element.330), channel_id=1, source_target_pairs={{0,8},{4,12},{8,0},{12,4},{16,24},{20,28},{24,16},{28,20},{1,9},{5... | collective-permute-start | bytes 1769480 | tf_op jit(solution)/shard_map/ppermute | solution.py:57
  446.4 29.9 %collective-permute-start.60 = (bf16[144,2048]{1,0:T(8,128)(2,1)}, bf16[144,2048]{1,0:T(8,128)(2,1)}, u32[]{:S(2)}, u32[]{:S(2)}) collective-permute-start(bf16[144,2048]{1,0:T(8,128)(2,1)} %get-tuple-element.331), channel_id=1, source_target_pairs={{0,16},{4,20},{8,24},{12,28},{16,0},{20,4},{24,8},{28,12},{1,17},{... | collective-permute-start | bytes 1769480 | tf_op jit(solution)/shard_map/ppermute | solution.py:57
  447.0 29.3 %collective-permute-start.61 = (bf16[144,2048]{1,0:T(8,128)(2,1)}, bf16[144,2048]{1,0:T(8,128)(2,1)}, u32[]{:S(2)}, u32[]{:S(2)}) collective-permute-start(bf16[144,2048]{1,0:T(8,128)(2,1)} %get-tuple-element.332), channel_id=1, source_target_pairs={{0,24},{4,28},{8,16},{12,20},{16,8},{20,12},{24,0},{28,4},{1,25},{... | collective-permute-start | bytes 1769480 | tf_op jit(solution)/shard_map/ppermute | solution.py:57
  482.4 31.2 %collective-permute-start.67 = (bf16[576,2048]{1,0:T(8,128)(2,1)}, bf16[576,2048]{1,0:T(8,128)(2,1)S(1)}, u32[]{:S(2)}, u32[]{:S(2)}) collective-permute-start(bf16[576,2048]{1,0:T(8,128)(2,1)} %get-tuple-element.348), channel_id=1, source_target_pairs={{0,4},{4,0},{8,12},{12,8},{16,20},{20,16},{24,28},{28,24},{1,5},{5... | collective-permute-start | bytes 7077896 | tf_op jit(solution)/shard_map/ppermute | solution.py:57
  519.5 32.4 %collective-permute-start.72 = (bf16[512,2048]{1,0:T(8,128)(2,1)}, bf16[512,2048]{1,0:T(8,128)(2,1)}, u32[]{:S(2)}, u32[]{:S(2)}) collective-permute-start(bf16[512,2048]{1,0:T(8,128)(2,1)} %get-tuple-element.361), channel_id=1, source_target_pairs={{0,4},{4,0},{8,12},{12,8},{16,20},{20,16},{24,28},{28,24},{1,5},{5... | collective-permute-start | bytes 6291464 | tf_op jit(solution)/shard_map/ppermute | solution.py:57
  589.7 30.5 %collective-permute-start.81 = (bf16[512,2048]{1,0:T(8,128)(2,1)}, bf16[512,2048]{1,0:T(8,128)(2,1)}, u32[]{:S(2)}, u32[]{:S(2)}) collective-permute-start(bf16[512,2048]{1,0:T(8,128)(2,1)} %get-tuple-element.383), channel_id=1, source_target_pairs={{0,4},{4,0},{8,12},{12,8},{16,20},{20,16},{24,28},{28,24},{1,5},{5... | collective-permute-start | bytes 6291464 | tf_op jit(solution)/shard_map/ppermute | solution.py:57
  626.0 30.8 %collective-permute-start.82 = (bf16[512,2048]{1,0:T(8,128)(2,1)}, bf16[512,2048]{1,0:T(8,128)(2,1)}, u32[]{:S(2)}, u32[]{:S(2)}) collective-permute-start(bf16[512,2048]{1,0:T(8,128)(2,1)} %get-tuple-element.392.refs_5_), channel_id=1, source_target_pairs={{0,4},{4,0},{8,12},{12,8},{16,20},{20,16},{24,28},{28,24},{1,5},{5... | collective-permute-start | bytes 6291464 | tf_op jit(solution)/shard_map/ppermute | solution.py:57
  654.7 46.1 %collective-permute-start.91 = (bf16[512,2048]{1,0:T(8,128)(2,1)}, bf16[512,2048]{1,0:T(8,128)(2,1)}, u32[]{:S(2)}, u32[]{:S(2)}) collective-permute-start(bf16[512,2048]{1,0:T(8,128)(2,1)} %get-tuple-element.414), channel_id=1, source_target_pairs={{0,4},{4,0},{8,12},{12,8},{16,20},{20,16},{24,28},{28,24},{1,5},{5... | collective-permute-start | bytes 6291464 | tf_op jit(solution)/shard_map/ppermute | solution.py:57
  659.4 41.4 %all-to-all-start.3 = ((bf16[32,64,256]{2,1,0:T(8,128)(2,1)}), bf16[32,64,256]{2,1,0:T(8,128)(2,1)S(1)}, u32[]{:S(2)}, u32[]{:S(2)}) async-start(bf16[32,64,256]{2,1,0:T(8,128)(2,1)} %get-tuple-element.408), calls=%async_computation.3 | async-start | bytes 2097152 | tf_op jit(solution)/shard_map/all_to_all | solution.py:225
  663.3 33.0 %collective-permute-start.88 = (bf16[128,2048]{1,0:T(8,128)(2,1)}, bf16[128,2048]{1,0:T(8,128)(2,1)S(1)}, u32[]{:S(2)}, u32[]{:S(2)}) collective-permute-start(bf16[128,2048]{1,0:T(8,128)(2,1)} %get-tuple-element.410), channel_id=1, source_target_pairs={{0,8},{4,12},{8,0},{12,4},{16,24},{20,28},{24,16},{28,20},{1,9},{5... | collective-permute-start | bytes 1572872 | tf_op jit(solution)/shard_map/ppermute | solution.py:57
  665.1 31.2 %collective-permute-start.89 = (bf16[128,2048]{1,0:T(8,128)(2,1)}, bf16[128,2048]{1,0:T(8,128)(2,1)}, u32[]{:S(2)}, u32[]{:S(2)}) collective-permute-start(bf16[128,2048]{1,0:T(8,128)(2,1)} %get-tuple-element.411), channel_id=1, source_target_pairs={{0,16},{4,20},{8,24},{12,28},{16,0},{20,4},{24,8},{28,12},{1,17},{... | collective-permute-start | bytes 1572872 | tf_op jit(solution)/shard_map/ppermute | solution.py:57
  666.6 34.3 %collective-permute-start.90 = (bf16[128,2048]{1,0:T(8,128)(2,1)}, bf16[128,2048]{1,0:T(8,128)(2,1)}, u32[]{:S(2)}, u32[]{:S(2)}) collective-permute-start(bf16[128,2048]{1,0:T(8,128)(2,1)} %get-tuple-element.412), channel_id=1, source_target_pairs={{0,24},{4,28},{8,16},{12,20},{16,8},{20,12},{24,0},{28,4},{1,25},{... | collective-permute-start | bytes 1572872 | tf_op jit(solution)/shard_map/ppermute | solution.py:57
  668.9 31.9 %collective-permute-start.87 = (bf16[128,2048]{1,0:T(8,128)(2,1)}, bf16[128,2048]{1,0:T(8,128)(2,1)}, u32[]{:S(2)}, u32[]{:S(2)}) collective-permute-start(bf16[128,2048]{1,0:T(8,128)(2,1)} %add_convert_fusion.6), channel_id=1, source_target_pairs={{0,1},{1,2},{2,3},{3,0},{4,5},{5,6},{6,7},{7,4},{8,9},{9,10},{10,1... | collective-permute-start | bytes 1572872 | tf_op jit(solution)/shard_map/ppermute | solution.py:62
  705.8 29.9 %collective-permute-start.93 = (bf16[512,2048]{1,0:T(8,128)(2,1)}, bf16[512,2048]{1,0:T(8,128)(2,1)}, u32[]{:S(2)}, u32[]{:S(2)}) collective-permute-start(bf16[512,2048]{1,0:T(8,128)(2,1)} %get-tuple-element.421), channel_id=1, source_target_pairs={{0,4},{4,0},{8,12},{12,8},{16,20},{20,16},{24,28},{28,24},{1,5},{5... | collective-permute-start | bytes 6291464 | tf_op jit(solution)/shard_map/ppermute | solution.py:57
  741.6 30.1 %collective-permute-start.98 = (bf16[512,1024]{1,0:T(8,128)(2,1)}, bf16[512,1024]{1,0:T(8,128)(2,1)S(1)}, u32[]{:S(2)}, u32[]{:S(2)}) collective-permute-start(bf16[512,1024]{1,0:T(8,128)(2,1)} %get-tuple-element.431), channel_id=1, source_target_pairs={{0,1},{1,2},{2,3},{3,0},{4,5},{5,6},{6,7},{7,4},{8,9},{9,10},{10,1... | collective-permute-start | bytes 3145736 | tf_op jit(solution)/shard_map/ppermute | solution.py:62
  745.1 34.6 %collective-permute-start.97 = (bf16[128,2048]{1,0:T(8,128)(2,1)}, bf16[128,2048]{1,0:T(8,128)(2,1)}, u32[]{:S(2)}, u32[]{:S(2)}) collective-permute-start(bf16[128,2048]{1,0:T(8,128)(2,1)} %add_convert_fusion.5), channel_id=1, source_target_pairs={{0,1},{1,2},{2,3},{3,0},{4,5},{5,6},{6,7},{7,4},{8,9},{9,10},{10,1... | collective-permute-start | bytes 1572872 | tf_op jit(solution)/shard_map/ppermute | solution.py:62
  (147 other events, 1902.1 us)

commit v4 on v3

--- a/solution.py
+++ b/solution.py
@@ -13,7 +13,7 @@
 BLOCK = 128
 EXTRA = 16
 GROUP = 4
-VMEM = 60 * 1024 * 1024
+VMEM = 64 * 1024 * 1024
 
 EPSILON = 1e-06
 ROPE_BASE = 10000.0
@@ -204,11 +204,12 @@
 
 
 def ring_sum(pieces):
-    total = pieces[min(1, len(pieces) - 1)]
-    for piece in pieces[2:] + (pieces[:1] if len(pieces) > 1 else []):
+    total = pieces[1]
+    for piece in pieces[2:]:
         rows = total.shape[0]
         (total,) = yield Step([turn(total)], [[(rows, [(0, 0), (1, 0)])]], [piece])
-    return total
+    (total,) = yield Step([turn(total)])
+    return pieces[0], total
 
 
 def staged_sum(parts):
@@ -834,6 +835,44 @@
 def weight_buffers(array):
     depth = min(2, array.shape[0])
     return [pltpu.VMEM((depth,) + array.shape[1:], array.dtype), pltpu.SemaphoreType.DMA((depth,))]
+
+
+def first_kernel(grads_ref, routes_ref, router_ref, qkv_ref, out_ref, parts_ref):
+    bf16, f32 = jnp.bfloat16, jnp.float32
+    amount, width = grads_ref.shape
+    blocks, _, three = parts_ref.shape
+    part = three // 3
+    for block in range(blocks):
+        for i in range(3):
+            start = i * (qkv_ref.shape[1] // 3) + block * part
+            parts_ref[block, :, i * part : (i + 1) * part] = qkv_ref[:, start : start + part]
+    out_ref[:amount, :] = grads_ref[...]
+    experts = lax.broadcasted_iota(jnp.int32, (EXPERTS, amount), 0)
+    named = jnp.zeros((EXPERTS, amount), f32)
+    for i in range(routes_ref.shape[0]):
+        named = named + (experts == routes_ref[i : i + 1, :]).astype(f32)
+    tokens = (amount, amount)
+    before = lax.broadcasted_iota(jnp.int32, tokens, 0) < lax.broadcasted_iota(jnp.int32, tokens, 1)
+    ranks = jnp.where(named > 0, dot(named.astype(bf16), before.astype(bf16)), -1.0).astype(bf16)
+    router = jnp.concatenate(
+        [router_ref[...], jnp.zeros((router_ref.shape[0], amount - EXPERTS), bf16)], axis=1
+    )
+    tiles = [ranks[at : at + EXTRA] for at in range(0, EXPERTS, EXTRA)]
+    tiles += [router[at : at + EXTRA] for at in range(0, router.shape[0], EXTRA)]
+    tiles.append(jnp.zeros((EXTRA, width - len(tiles) * amount), bf16))
+    out_ref[amount:, :] = jnp.concatenate(tiles, axis=1)
+
+
+def first_arrays(grads, routes, router, w_qkv, blocks):
+    rows, columns = w_qkv.shape
+    return pl.pallas_call(
+        first_kernel,
+        out_shape=[
+            jax.ShapeDtypeStruct((grads.shape[0] + EXTRA, grads.shape[1]), grads.dtype),
+            jax.ShapeDtypeStruct((blocks, rows, columns // blocks), w_qkv.dtype),
+        ],
+        compiler_params=pltpu.CompilerParams(vmem_limit_bytes=VMEM),
+    )(grads, routes, router, w_qkv)
 
 
 def early(k, planes, first, grads, count, w_down, s_down, kept, after):
@@ -973,29 +1012,35 @@
     )(left, right, *kept, after)
 
 
-def rows_of_columns_kernel(came_ref, weights_ref, rows_ref, sum_ref):
+def last_kernel(came_ref, weights_ref, gain_ref, residual_ref, own_ref, moved_ref, rows_ref, sum_ref, out_ref):
+    f32 = jnp.float32
     blocks, _, three = came_ref.shape
     part, width = three // 3, rows_ref.shape[1] // 3
     total = 0.0
     for block in range(blocks):
         for i in range(3):
             into = slice(i * width + block * part, i * width + (block + 1) * part)
-            values = came_ref[block, :, i * part : (i + 1) * part].astype(jnp.float32)
+            values = came_ref[block, :, i * part : (i + 1) * part].astype(f32)
             rows_ref[:, into] = values
-            weighted = values * weights_ref[:, into].astype(jnp.float32)
+            weighted = values * weights_ref[:, into].astype(f32)
             total = total + jnp.sum(weighted, axis=1, keepdims=True)
-    sum_ref[...] = total
-
-
-def rows_of_columns(came, weights):
+    sum_ref[...] = total / gain_ref[...]
+    for at in range(0, out_ref.shape[0], EXTRA):
+        rows = slice(at, at + EXTRA)
+        added = own_ref[rows, :].astype(f32) + moved_ref[rows, :].astype(f32)
+        out_ref[rows, :] = (residual_ref[rows, :] + added).astype(out_ref.dtype)
+
+
+def last_outputs(came, weights, gain, residual, own, moved):
     return pl.pallas_call(
-        rows_of_columns_kernel,
+        last_kernel,
         out_shape=[
             jax.ShapeDtypeStruct(weights.shape, jnp.float32),
             jax.ShapeDtypeStruct((weights.shape[0], 1), jnp.float32),
+            jax.ShapeDtypeStruct(residual.shape, jnp.bfloat16),
         ],
         compiler_params=pltpu.CompilerParams(vmem_limit_bytes=VMEM),
-    )(came, weights)
+    )(came, weights, gain, residual, own, moved)
 
 
 def shared_grads(rows_x, rows_g, hidden, joined, after):
@@ -1058,20 +1103,12 @@
 
     clock = Clock()
 
-    expert_ids = jnp.arange(EXPERTS, dtype=jnp.int32)
-    own_mask = jnp.sum((expert_ids[:, None, None] == routes[0].T[None]).astype(f32), axis=1)
-    before = (jnp.arange(amount)[:, None] < jnp.arange(amount)[None, :]).astype(bf16)
-    ranking = jnp.where(own_mask > 0, dot(own_mask.astype(bf16), before), -1.0)
-
-    qkv_part = w_qkv.reshape(rows, 3, n_ctx, part).transpose(2, 0, 1, 3).reshape(n_ctx, rows, 3 * part)
+    own_grads, qkv_part = first_arrays(cotangent[0], routes[0].T, w_router, w_qkv, n_ctx)
     qkv_part = lax.all_to_all(qkv_part, "ctx", split_axis=0, concat_axis=0, tiled=True)
     sequence = Transfer(gather_plane(tokens[0], False))
-    small = jnp.concatenate([ranking.astype(bf16), jnp.pad(w_router, ((0, 0), (0, amount - EXPERTS)))])
-    small = small.reshape(-1, EXTRA, amount).transpose(1, 0, 2).reshape(EXTRA, -1)
-    small = jnp.pad(small, ((0, 0), (0, width - small.shape[1])))
-    own_grads = jnp.concatenate([cotangent[0], small], axis=0)
     grads = [Transfer(gather_plane(own_grads, False))]
-    grad_blocks = [Transfer(turned(own_grads, k)) for k in range(1, min(3, planes))]
+    arrival = [0, 1, planes - 1, *range(2, planes - 1)][:planes]
+    grad_blocks = [Transfer(turned(own_grads, k)) for k in arrival[1:3]]
     (qkv_part,) = stage(clock, [sequence, *grads, *grad_blocks], [qkv_part])
 
     out_part = w_out.reshape(rows, n_ctx, part).transpose(1, 0, 2)
@@ -1109,36 +1146,37 @@
     first = [first_expert, device * per_owner // EXPERTS, ctx]
     back = lax.rem(plane - jnp.arange(planes, dtype=jnp.int32) + planes, planes)
     first = [jnp.stack([*first, back[k]]).astype(jnp.int32) for k in range(planes)]
-    ranks, slots = [], []
+    ranks, slots, dhs = {}, {}, {}
 
     lane = -(-units // BLOCK) * BLOCK
     s_down = jnp.pad(w_shared_down, ((0, lane - units), (0, 0)))
-    early_kept, dhs = [], []
+    early_kept = []
 
     def grads_stage(transfers, beside=(), work=True):
         nonlocal early_kept
-        k, made = len(dhs), []
-        if work and k < planes and k < len(grads) and grads[k].done:
+        i, made = len(dhs), []
+        if work and i < planes and i < len(grads) and grads[i].done:
+            k = arrival[i]
             early_kept, made = early(
-                k, planes, first[k], grads[k].result, rows, w_expert_down, s_down, early_kept, clock.token
+                k, planes, first[k], grads[i].result, rows, w_expert_down, s_down, early_kept, clock.token
             )
-            for some, one in zip((ranks, slots), made[1:], strict=True):
-                some.append(one)
+            ranks[k], slots[k] = made[1:]
         arrays = stage(clock, [*transfers, *grads, *grad_blocks], [*beside, *made[:1]])
-        dhs.extend(arrays[len(beside) :])
-        k = len(grads)
-        if 2 <= k < planes and grad_blocks[k - 1].done and grads[-1].step is not grads[-1].opening:
-            grads.append(Transfer(gather_plane(grad_blocks[k - 1].result, False)))
+        if made:
+            dhs[k] = arrays[-1]
+        i = len(grads)
+        if 2 <= i < planes and grad_blocks[i - 1].done and grads[-1].step is not grads[-1].opening:
+            grads.append(Transfer(gather_plane(grad_blocks[i - 1].result, False)))
             grads[-1].opening = grads[-1].step
             if len(grad_blocks) < planes - 1:
-                ahead = len(grad_blocks) + 1
-                source = own_grads if ahead == 3 else grad_blocks[-1].result
-                grad_blocks.append(Transfer(turned(source, ahead if ahead == 3 else 1)))
+                source = neighbour if len(grad_blocks) == 2 else grad_blocks[-1].result
+                grad_blocks.append(Transfer(turned(source)))
         return arrays[: len(beside)]
 
     grads[-1].opening = None
+    neighbour = grad_blocks[0].result
     while not ring_w.done:
-        shared_in, own_grads = grads_stage([ring_w], [shared_in, own_grads])
+        shared_in, neighbour = grads_stage([ring_w], [shared_in, neighbour])
     pieces = ring_w.result
     shared_in = Transfer(exchanged(shared_in))
     own_rows = tokens[0].astype(f32)
@@ -1147,13 +1185,13 @@
         plane_id, seq_rows, gain_one[None, :], tables, pieces, heads, clock.token
     )
     saved = [normed, query, key, value, mixed, tops, totals]
-    attended = grads_stage([shared_in], attended)
+    attended = grads_stage([], attended)
     attended = Transfer(scatter_plane(*attended))
+    grads_stage([attended])
+    while not (attended.done and shared_in.done):
+        grads_stage([attended, shared_in])
     shared_in = shared_in.result.reshape(width, 2, units)
     s_in = jnp.pad(shared_in, ((0, 0), (0, 0), (0, lane - units))).reshape(width, 2 * lane)
-    (s_in,) = grads_stage([attended], [s_in])
-    while not attended.done:
-        grads_stage([attended])
     residual = own_rows + attended.result.astype(f32)
     ffn_own = rms_scale(residual, gain_two).astype(bf16)
 
@@ -1172,18 +1210,18 @@
         )
         return list(pair)
 
-    def outs_stage(transfers, beside=(), moving=None, adding=True, opening=True):
+    def outs_stage(transfers, beside=(), moving=None, opening=True):
         nonlocal out_sum
         pair = do_late() if not beside else []
         if out_sum is None and len(out_parts) == planes and out_parts[0].done:
-            out_sum = Transfer(staged_sum(out_parts))
+            out_sum = Transfer(staged_sum(out_parts[:-1]))
         going = [t for t in out_parts if not t.done]
         fresh = [t for t in going if t.step is t.opening]
         going = [t for t in going if t not in fresh]
         fresh = fresh if opening else []
         if moving is not None:
             going = going[:moving]
-        sums = [out_sum] if out_sum and adding else []
+        sums = [out_sum] if out_sum else []
         arrays = stage(clock, [*transfers, *going, *fresh, *sums], [*beside, *pair])
         if pair:
             out_parts.append(Transfer(scatter_plane(*arrays)))
@@ -1197,7 +1235,7 @@
         if router_t is None and len(ranks) == planes:
             router_full = early_kept[2].reshape(width, amount)[:, :EXPERTS]
             router_t = router_full.T
-        if k < planes and ffn[k].done and len(dhs) > k and router_t is not None:
+        if k < planes and ffn[k].done and k in dhs and router_t is not None:
             mid_kept, pair, made = middle(
                 k, planes, first[k], ffn[k].result, router_t, ranks[k], slots[k], w_expert_in, s_in,
                 early_kept[1], dhs[k], mid_kept, clock.token,
@@ -1208,7 +1246,7 @@
         elif k == planes:
             outs_stage(going, moving=1 if d_parts[-1].done else 0)
         else:
-            grads_stage(going)
+            (s_in,) = grads_stage(going, [s_in])
         if len(ffn) < planes and block.done:
             ffn.append(Transfer(gather_plane(block.result)))
             if len(ffn) < planes:
@@ -1238,7 +1276,7 @@
             continue
         into, shared_down_grad = shared_grads(
             [side for t in ffn for side in t.result],
-            [side for t in grads for side in t.result],
+            [side for k in range(planes) for side in grads[arrival.index(k)].result],
             jnp.concatenate([made[2] for made in mids]),
             jnp.concatenate([made[3] for made in mids]),
             clock.token,
@@ -1262,26 +1300,27 @@
 
     first_half = -(-per_owner // 2)
     (dy,) = late_kept
-    work = [lambda kept: rows_grad(rows_in, d_joined, 0, first_half, kept, clock.token)]
+    work = [lambda kept: [rows_grad(rows_in, d_joined, 0, first_half, kept, clock.token)]]
     if first_half < per_owner:
         work.append(
-            lambda kept: rows_grad(
-                rows_in, d_joined, first_half, per_owner - first_half, kept, clock.token
-            )
+            lambda kept: [
+                rows_grad(rows_in, d_joined, first_half, per_owner - first_half, kept, clock.token)
+            ]
         )
-    work.append(lambda kept: rows_grad(hidden, dy, 0, per_owner, [], clock.token))
-    made = []
+    work.append(lambda kept: [rows_grad(hidden, dy, 0, per_owner, [], clock.token)])
+    made, last = [], None
     while work or not (ring_grad.done and d_normed.done):
+        one = work.pop(0)(made) if work else []
+        last = [out_sum.result] if not work and out_sum.done else []
+        *one, last = outs_stage([ring_grad, d_normed], [*one, *last], 1) if last else [
+            *outs_stage([ring_grad, d_normed], one, 1),
+            None,
+        ]
         if work:
-            one = work.pop(0)(made)
-            (one,) = outs_stage([ring_grad, d_normed], [one], 1, False)
-            if work:
-                made = [one]
-            else:
-                (expert_in_grad,), expert_down_grad = made, one
-        else:
-            outs_stage([ring_grad, d_normed], [], 1, False)
-    ring_grad = ring_grad.result.reshape(n_ctx, rows, 4 * part)
+            made = one
+        elif one:
+            (expert_in_grad,), (expert_down_grad,) = made, one
+    ring_grad = add(*ring_grad.result).reshape(n_ctx, rows, 4 * part)
     qkv_grad = lax.all_to_all(ring_grad[:, :, : 3 * part], "ctx", split_axis=0, concat_axis=0, tiled=True)
     out_grad = ring_grad[:, :, 3 * part :].transpose(1, 0, 2).reshape(rows, width).astype(f32)
     first_back = jax.vjp(lambda x: rms_scale(x, gain_one), own_rows)[1](d_normed.result.astype(f32))
@@ -1292,13 +1331,13 @@
     small = jnp.sum(shared[:, :, 2 * units :].astype(f32), axis=0)
     router_grad, gain_ffn_grad = small[:, :EXPERTS], small[:, EXPERTS]
     shared_down_grad = shared_down_grad[:units]
-    while out_sum is None or not out_sum.done:
-        if out_sum is None and out_parts[0].done:
-            out_sum = Transfer(staged_sum(out_parts))
-        stage(clock, [*out_parts, *([out_sum] if out_sum else [])])
-    result = (residual + out_sum.result.astype(f32)).astype(bf16)
-    qkv_grad, weighted = rows_of_columns(qkv_grad, w_qkv)
-    gain_attn_grad = weighted[:, 0] / gain_attn.astype(f32)
+    while not (out_sum.done and out_parts[-1].done):
+        stage(clock, [*out_parts, out_sum])
+        last = out_sum.result
+    qkv_grad, gain_attn_grad, result = last_outputs(
+        qkv_grad, w_qkv, gain_attn.astype(f32)[:, None], residual, out_parts[-1].result, turn(last)
+    )
+    gain_attn_grad = gain_attn_grad[:, 0]
     return (
         result[None],
         tokens_grad[None],

time: 839 us -> 829 us (0.988)
  local copies, waits for them, and re-layouts: 65.7 us -> 44.5 us
  other arithmetic: 39.2 us -> 49.4 us
    unnamed x180 -> x71, local copies, waits for them, and re-layouts: 28.8 us -> 9.41 us
    ppermute x18, waiting for transfers between devices: 47.6 us -> 34.5 us  [turn(): lax.ppermute(values, 'fsdp', [(i, (i + step) % count) for i in range(coun...]
  transfers between devices with their start and end apart: 108 -> 108, of which waited for: 23 -> 26; matrix products, arithmetic and copies ran while one was open for 9% -> 11% of each run, Pallas kernels for 40% -> 41%
where the time goes in v4:
time: 829 us; the launch traced here: 818 us
  Pallas kernels  407 us (49%)
  waiting for transfers between devices  182 us (22%)
  starting transfers between devices  129 us (16%)
  other arithmetic  49.4 us (6%)
  local copies, waits for them, and re-layouts  44.5 us (5%)
    pallas_call x12, Pallas kernels, expert_call(): pl.pallas_call(functools.partial(kernel, carried=len(kept) + 1), grid=(ow...  215 us
    ppermute x85, waiting for transfers between devices, swap(): return lax.ppermute(values, 'ctx', [(i, i ^ bit) for i in range(count)])  136 us
    ppermute x85, starting transfers between devices, swap(): return lax.ppermute(values, 'ctx', [(i, i ^ bit) for i in range(count)])  82.9 us
    pallas_call x22, Pallas kernels, stage(): pl.pallas_call(kernel, in_specs=[far] * (first + len(taken)), out_specs=[...  75.5 us
    pallas_call x3, Pallas kernels, rows_grad(): pl.pallas_call(rows_kernel, grid=(count,), in_specs=[pl.BlockSpec((1, amo...  50 us
    pallas_call x2, Pallas kernels, attend_call(): pl.pallas_call(kernel, in_specs=[pl.BlockSpec(memory_space=pltpu.SMEM)] +...  44.6 us
    ppermute x18, waiting for transfers between devices, turn(): lax.ppermute(values, 'fsdp', [(i, (i + step) % count) for i in range(coun...  34.5 us
    ppermute x18, starting transfers between devices, turn(): lax.ppermute(values, 'fsdp', [(i, (i + step) % count) for i in range(coun...  23.3 us
  transfers between devices with their start and end apart: 108, of which 26 were waited for; matrix products, arithmetic and copies ran while one was open for 11% of the time, Pallas kernels for 41%

profile of v4, /device:TPU:0, one launch (start us, length us, event | category | flops | bytes accessed | tf_op | source)
XLA Modules:
  0.0 818.1 jit_solution(12717717539173365710)
XLA Ops:
  7.5 4.3 all-to-all-start
  25.2 22.2 %collective-permute-done.2.refs_4_.refs_11_ = bf16[128,2048]{1,0:T(8,128)(2,1)} collective-permute-done((bf16[128,2048]{1,0:T(8,128)(2,1)}, bf16[128,2048]{1,0:T(8,128)(2,1)}, u32[]{:S(2)}, u32[]{:S(2)}) %collective-permute-start.2) | collective-permute-done | bytes 524320 | tf_op jit(solution)/shard_map/ppermute | solution.py:57
  74.4 4.9 all-to-all-done.1
  85.6 26.7 %collective-permute-done.11.refs_1_.refs_10_.refs_16_ = bf16[8,64,1024]{2,1,0:T(8,128)(2,1)} collective-permute-done((bf16[8,64,1024]{2,1,0:T(8,128)(2,1)}, bf16[8,64,1024]{2,1,0:T(8,128)(2,1)}, u32[]{:S(2)}, u32[]{:S(2)}) %collective-permute-start.11) | collective-permute-done | bytes 1048608 | tf_op jit(solution)/shard_map/ppermute | solution.py:62
  122.6 4.5 collective-permute-done.15.refs_5_.refs_9_
  132.2 12.2 %shard_map.225 = (bf16[4,640,2048]{2,1,0:T(8,128)(2,1)}, f32[4,640,704]{2,1,0:T(8,128)}, bf16[8,4,64,128]{3,2,1,0:T(8,128)(2,1)}, f32[1024,128]{1,0:T(8,128)}, f32[64,1024]{1,0:T(8,128)}, /*index=5*/f32[4,1024]{1,0:T(4,128)}) custom-call(s32[4]{0:T(128)} %get-tuple-element.478.refs_0_, bf16[576,2048]{1,0:T(8,128)(2,1)} %get-tuple-element.248.refs_1_.refs_8_, ...), custom_call_target="tpu_custom_call" | custom-call | flops 3724541952 | bytes 20971520 | tf_op jit(solution)/shard_map/pallas_call | solution.py:818
  151.3 19.2 %shard_map.227 = (bf16[512,2048]{1,0:T(8,128)(2,1)}, bf16[512,2048]{1,0:T(8,128)(2,1)}, bf16[1024,2048]{1,0:T(8,128)(2,1)}, bf16[1024,256]{1,0:T(8,128)(2,1)}, b...) custom-call(s32[1]{0:T(128)} %bitcast.refs_0_, ...), custom_call_target="tpu_custom_call" | custom-call | flops 5368709120 | bytes 30000000 | tf_op jit(solution)/shard_map/pallas_call | solution.py:707
  176.6 12.2 %shard_map.229 = (bf16[4,640,2048]{2,1,0:T(8,128)(2,1)}, f32[4,640,704]{2,1,0:T(8,128)}, bf16[8,4,64,128]{3,2,1,0:T(8,128)(2,1)}, f32[1024,128]{1,0:T(8,128)}, f32[64,1024]{1,0:T(8,128)}, /*index=5*/f32[4,1024]{1,0:T(4,128)}) custom-call(s32[4]{0:T(128)} %get-tuple-element.477.refs_0_, ...), custom_call_target="tpu_custom_call", output_to_operand_aliasing={{0}: (5, {}), {1}: (6, {}), {2}: (7, {})} | custom-call | flops 3724541952 | bytes 20971520 | tf_op jit(solution)/shard_map/pallas_call | solution.py:818
  190.5 4.8 collective-permute-done.25.refs_5_
  195.6 5.1 shard_map.230
  200.9 6.4 all-to-all-start.2
  212.6 12.4 %collective-permute-done.33.refs_8_ = bf16[64,2048]{1,0:T(8,128)(2,1)} collective-permute-done((bf16[64,2048]{1,0:T(8,128)(2,1)}, bf16[64,2048]{1,0:T(8,128)(2,1)}, u32[]{:S(2)}, u32[]{:S(2)}) %collective-permute-start.33) | collective-permute-done | bytes 262176 | tf_op jit(solution)/shard_map/ppermute | solution.py:57
  226.4 6.0 all-to-all-done.2.refs_1_
  232.3 18.5 %collective-permute-done.32.refs_7_ = bf16[80,2048]{1,0:T(8,128)(2,1)} collective-permute-done((bf16[80,2048]{1,0:T(8,128)(2,1)S(1)}, bf16[80,2048]{1,0:T(8,128)(2,1)}, u32[]{:S(2)}, u32[]{:S(2)}) %collective-permute-start.32) | collective-permute-done | bytes 327712 | tf_op jit(solution)/shard_map/ppermute | solution.py:57
  269.6 12.2 %shard_map.232 = (bf16[4,640,2048]{2,1,0:T(8,128)(2,1)}, f32[4,640,704]{2,1,0:T(8,128)}, bf16[8,4,64,128]{3,2,1,0:T(8,128)(2,1)}, f32[1024,128]{1,0:T(8,128)}, f32[64,1024]{1,0:T(8,128)}, /*index=5*/f32[4,1024]{1,0:T(4,128)}) custom-call(s32[4]{0:T(128)} %get-tuple-element.476.refs_0_, ...), custom_call_target="tpu_custom_call", output_to_operand_aliasing={{0}: (5, {}), {1}: (6, {}), {2}: (7, {})} | custom-call | flops 3724541952 | bytes 20971520 | tf_op jit(solution)/shard_map/pallas_call | solution.py:818
  281.8 5.5 collective-permute-done.37.refs_6_
  294.9 12.2 %shard_map.234 = (bf16[4,640,2048]{2,1,0:T(8,128)(2,1)}, f32[4,640,704]{2,1,0:T(8,128)}, bf16[8,4,64,128]{3,2,1,0:T(8,128)(2,1)}, f32[1024,128]{1,0:T(8,128)}, f32[64,1024]{1,0:T(8,128)}, /*index=5*/f32[4,1024]{1,0:T(4,128)}) custom-call(s32[4]{0:T(128)} %get-tuple-element.463.refs_0_, ...), custom_call_target="tpu_custom_call", output_to_operand_aliasing={{0}: (5, {}), {1}: (6, {}), {2}: (7, {})} | custom-call | flops 3724541952 | bytes 20971520 | tf_op jit(solution)/shard_map/pallas_call | solution.py:818
  307.1 9.6 %collective-permute-done.42.refs_6_ = bf16[128,2048]{1,0:T(8,128)(2,1)} collective-permute-done((bf16[128,2048]{1,0:T(8,128)(2,1)}, bf16[128,2048]{1,0:T(8,128)(2,1)}, u32[]{:S(2)}, u32[]{:S(2)}) %collective-permute-start.42) | collective-permute-done | bytes 524320 | tf_op jit(solution)/shard_map/ppermute | solution.py:57
  326.6 27.6 %shard_map.236 = (bf16[4,640,2048]{2,1,0:T(8,128)(2,1)}, bf16[4,640,704]{2,1,0:T(8,128)(2,1)}, bf16[4,640,1408]{2,1,0:T(8,128)(2,1)}, bf16[576,2048]{1,0:T(8,128...) custom-call(s32[4]{0:T(128)} %get-tuple-element.478.refs_0_, ...), custom_call_target="tpu_custom_call" | custom-call | flops 12213813248 | bytes 36700160 | tf_op jit(solution)/shard_map/pallas_call | solution.py:818
  360.8 27.8 %shard_map.238 = (bf16[4,640,2048]{2,1,0:T(8,128)(2,1)}, bf16[4,640,704]{2,1,0:T(8,128)(2,1)}, bf16[4,640,1408]{2,1,0:T(8,128)(2,1)}, bf16[576,2048]{1,0:T(8,128...) custom-call(s32[4]{0:T(128)} %get-tuple-element.477.refs_0_, ...), custom_call_target="tpu_custom_call", output_to_operand_aliasing={{0}: (10, {}), {1}: (11, {}), {2}: (12, {})} | custom-call | flops 12213813248 | bytes 36700160 | tf_op jit(solution)/shard_map/pallas_call | solution.py:818
  388.6 5.1 shard_map.239
  397.7 27.8 %shard_map.240 = (bf16[4,640,2048]{2,1,0:T(8,128)(2,1)}, bf16[4,640,704]{2,1,0:T(8,128)(2,1)}, bf16[4,640,1408]{2,1,0:T(8,128)(2,1)}, bf16[576,2048]{1,0:T(8,128...) custom-call(s32[4]{0:T(128)} %get-tuple-element.463.refs_0_, ...), custom_call_target="tpu_custom_call", output_to_operand_aliasing={{0}: (10, {}), {1}: (11, {}), {2}: (12, {})} | custom-call | flops 12213813248 | bytes 36700160 | tf_op jit(solution)/shard_map/pallas_call | solution.py:818
  425.6 4.5 shard_map.241
  433.8 28.1 %shard_map.242 = (bf16[4,640,2048]{2,1,0:T(8,128)(2,1)}, bf16[4,640,704]{2,1,0:T(8,128)(2,1)}, bf16[4,640,1408]{2,1,0:T(8,128)(2,1)}, bf16[576,2048]{1,0:T(8,128...) custom-call(s32[4]{0:T(128)} %get-tuple-element.476.refs_0_, ...), custom_call_target="tpu_custom_call", output_to_operand_aliasing={{0}: (10, {}), {1}: (11, {}), {2}: (12, {})} | custom-call | flops 12213813248 | bytes 36700160 | tf_op jit(solution)/shard_map/pallas_call | solution.py:818
  461.9 4.5 shard_map.243
  471.6 13.7 %shard_map.244 = (bf16[4,640,2048]{2,1,0:T(8,128)(2,1)}, bf16[512,2048]{1,0:T(8,128)(2,1)}, bf16[512,2048]{1,0:T(8,128)(2,1)}) custom-call(s32[4]{0:T(128)} %get-tuple-element.477.refs_0_, bf16[4,640,704]{2,1,0:T(8,128)(2,1)} %get-tuple-element.344.refs_1_.left_ref, bf16[4,640,2048]{2,1,0:T(8,128)(2,1)} %get-tuple-element.345.refs_2_, ...), custom_call_target="tpu_custom_call" | custom-call | flops 3724541952 | bytes 20971520 | tf_op jit(solution)/shard_map/pallas_call | solution.py:818
  485.3 11.9 %collective-permute-done.65.refs_5_ = bf16[144,2048]{1,0:T(8,128)(2,1)} collective-permute-done((bf16[144,2048]{1,0:T(8,128)(2,1)}, bf16[144,2048]{1,0:T(8,128)(2,1)}, u32[]{:S(2)}, u32[]{:S(2)}) %collective-permute-start.65) | collective-permute-done | bytes 589856 | tf_op jit(solution)/shard_map/ppermute | solution.py:57
  497.2 4.5 shard_map.245
  508.8 13.5 %shard_map.246 = (bf16[4,640,2048]{2,1,0:T(8,128)(2,1)}, bf16[512,2048]{1,0:T(8,128)(2,1)}, bf16[512,2048]{1,0:T(8,128)(2,1)}) custom-call(s32[4]{0:T(128)} %get-tuple-element.463.refs_0_, bf16[4,640,704]{2,1,0:T(8,128)(2,1)} %get-tuple-element.344.refs_1_.left_ref, ...), custom_call_target="tpu_custom_call", output_to_operand_aliasing={{0}: (8, {})} | custom-call | flops 3724541952 | bytes 20971520 | tf_op jit(solution)/shard_map/pallas_call | solution.py:818
  522.3 12.3 %collective-permute-done.70.refs_5_ = bf16[144,2048]{1,0:T(8,128)(2,1)} collective-permute-done((bf16[144,2048]{1,0:T(8,128)(2,1)}, bf16[144,2048]{1,0:T(8,128)(2,1)}, u32[]{:S(2)}, u32[]{:S(2)}) %collective-permute-start.70) | collective-permute-done | bytes 589856 | tf_op jit(solution)/shard_map/ppermute | solution.py:57
  544.9 13.8 %shard_map.248 = (bf16[4,640,2048]{2,1,0:T(8,128)(2,1)}, bf16[512,2048]{1,0:T(8,128)(2,1)}, bf16[512,2048]{1,0:T(8,128)(2,1)}) custom-call(s32[4]{0:T(128)} %get-tuple-element.476.refs_0_, bf16[4,640,704]{2,1,0:T(8,128)(2,1)} %get-tuple-element.344.refs_1_.left_ref, ...), custom_call_target="tpu_custom_call", output_to_operand_aliasing={{0}: (8, {})} | custom-call | flops 3724541952 | bytes 20971520 | tf_op jit(solution)/shard_map/pallas_call | solution.py:818
  561.0 6.8 collective-permute-done.75.refs_5_
  567.8 4.0 shard_map.249
  582.5 13.5 %shard_map.250 = (bf16[4,640,2048]{2,1,0:T(8,128)(2,1)}, bf16[512,2048]{1,0:T(8,128)(2,1)}, bf16[512,2048]{1,0:T(8,128)(2,1)}) custom-call(s32[4]{0:T(128)} %get-tuple-element.478.refs_0_, bf16[4,640,704]{2,1,0:T(8,128)(2,1)} %get-tuple-element.344.refs_1_.left_ref, ...), custom_call_target="tpu_custom_call", output_to_operand_aliasing={{0}: (8, {})} | custom-call | flops 3724541952 | bytes 20971520 | tf_op jit(solution)/shard_map/pallas_call | solution.py:818
  596.1 9.6 %collective-permute-done.79.refs_4_ = bf16[128,2048]{1,0:T(8,128)(2,1)} collective-permute-done((bf16[128,2048]{1,0:T(8,128)(2,1)}, bf16[128,2048]{1,0:T(8,128)(2,1)}, u32[]{:S(2)}, u32[]{:S(2)}) %collective-permute-start.79) | collective-permute-done | bytes 524320 | tf_op jit(solution)/shard_map/ppermute | solution.py:57
  605.7 4.9 shard_map.251
  621.5 16.0 %shard_map.252 = (bf16[2048,256]{1,0:T(8,128)(2,1)}, f32[128,2048]{1,0:T(8,128)}) custom-call(bf16[512,2048]{1,0:T(8,128)(2,1)} %get-tuple-element.289.refs_1_.refs_0_, bf16[512,2048]{1,0:T(8,128)(2,1)} %collective-permute-done.39.refs_3_.refs_2_.refs_1_, bf16[512,2048]{1,0:T(8,128)(2,1)} %get-tuple-element.299.refs_1_.refs_2_, ...), custom_call_target="tpu_custom_call" | custom-call | flops 6442450944 | bytes 33554432 | tf_op jit(solution)/shard_map/pallas_call | solution.py:1051
  657.9 25.4 %shard_map.254 = (bf16[512,2048]{1,0:T(8,128)(2,1)}, bf16[512,2048]{1,0:T(8,128)(2,1)}, bf16[8,64,1024]{2,1,0:T(8,128)(2,1)}, bf16[8,64,1024]{2,1,0:T(8,128)(2,1...) custom-call(s32[1]{0:T(128)} %bitcast.refs_0_, f32[1024,128]{1,0:T(8,128)} %get-tuple-element.242.refs_2_.refs_1_, ...), custom_call_target="tpu_custom_call" | custom-call | flops 11274289152 | bytes 30000000 | tf_op jit(solution)/shard_map/pallas_call | solution.py:707
  683.3 4.4 collective-permute-done.90.refs_7_
  687.6 4.0 shard_map.255
  702.1 16.7 %shard_map.256.refs_1_ = f32[4,2048,1408]{2,1,0:T(8,128)} custom-call(bf16[4,640,2048]{2,1,0:T(8,128)(2,1)} %get-tuple-element.425.left_ref, bf16[4,640,1408]{2,1,0:T(8,128)(2,1)} %get-tuple-element.426.right_ref, f32[8,128]{1,0:T(8,128)} %get-tuple-element.424.refs_0_), custom_call_target="tpu_custom_call" | custom-call | flops 7381975040 | bytes 23068672 | tf_op jit(solution)/shard_map/pallas_call | solution.py:995
  719.5 4.6 collective-permute-done.96.refs_8_
  724.2 5.8 shard_map.257
  736.9 16.7 %shard_map.258.refs_1_ = f32[4,2048,1408]{2,1,0:T(8,128)} custom-call(bf16[4,640,2048]{2,1,0:T(8,128)(2,1)} %get-tuple-element.425.left_ref, bf16[4,640,1408]{2,1,0:T(8,128)(2,1)} %get-tuple-element.426.right_ref, f32[4,2048,1408]{2,1,0:T(8,128)} %get-tuple-element.436.refs_0_, ...), custom_call_target="tpu_custom_call", output_to_operand_aliasing={{}: (2, {})} | custom-call | flops 7381975040 | bytes 23068672 | tf_op jit(solution)/shard_map/pallas_call | solution.py:995
  753.7 5.1 collective-permute-done.99.refs_5_
  768.8 16.6 %shard_map.260.refs_1_ = f32[4,704,2048]{2,1,0:T(8,128)} custom-call(bf16[4,640,704]{2,1,0:T(8,128)(2,1)} %get-tuple-element.344.refs_1_.left_ref, bf16[4,640,2048]{2,1,0:T(8,128)(2,1)} %get-tuple-element.446.right_ref, f32[8,128]{1,0:T(8,128)} %get-tuple-element.445.refs_0_), custom_call_target="tpu_custom_call" | custom-call | flops 7381975040 | bytes 23068672 | tf_op jit(solution)/shard_map/pallas_call | solution.py:995
  791.2 4.2 all-to-all-start.4
  808.0 4.9 collective-permute-done.102.moved_ref
  (359 shorter events, 258.7 us)
Async XLA Ops:
  7.5 40.0 %all-to-all-start = ((bf16[8,64,768]{2,1,0:T(8,128)(2,1)}), bf16[8,64,768]{2,1,0:T(8,128)(2,1)}, u32[]{:S(2)}, u32[]{:S(2)}) async-start(bf16[8,64,768]{2,1,0:T(8,128)(2,1)} %get-tuple-element.234), calls=%async_computation | async-start | bytes 1572864 | tf_op jit(solution)/shard_map/all_to_all | solution.py:1107
  11.8 35.6 %collective-permute-start.5 = (bf16[144,2048]{1,0:T(8,128)(2,1)}, bf16[144,2048]{1,0:T(8,128)(2,1)}, u32[]{:S(2)}, u32[]{:S(2)}) collective-permute-start(bf16[144,2048]{1,0:T(8,128)(2,1)} %get-tuple-element.235.refs_15_), channel_id=1, source_target_pairs={{0,16},{4,20},{8,24},{12,28},{16,0},{20,4},{24,8},{28,12},{1,17},{... | collective-permute-start | bytes 1769480 | tf_op jit(solution)/shard_map/ppermute | solution.py:57
  13.7 33.7 %collective-permute-start.4 = (bf16[144,2048]{1,0:T(8,128)(2,1)}, bf16[144,2048]{1,0:T(8,128)(2,1)}, u32[]{:S(2)}, u32[]{:S(2)}) collective-permute-start(bf16[144,2048]{1,0:T(8,128)(2,1)} %get-tuple-element.235.refs_15_), channel_id=1, source_target_pairs={{0,8},{4,12},{8,0},{12,4},{16,24},{20,28},{24,16},{28,20},{1,9},{5... | collective-permute-start | bytes 1769480 | tf_op jit(solution)/shard_map/ppermute | solution.py:57
  15.2 32.2 %collective-permute-start.1 = (bf16[144,2048]{1,0:T(8,128)(2,1)}, bf16[144,2048]{1,0:T(8,128)(2,1)}, u32[]{:S(2)}, u32[]{:S(2)}) collective-permute-start(bf16[144,2048]{1,0:T(8,128)(2,1)} %get-tuple-element.235.refs_15_), channel_id=1, source_target_pairs={{0,3},{1,0},{2,1},{3,2},{4,7},{5,4},{6,5},{7,6},{8,11},{9,8},{10,9... | collective-permute-start | bytes 1769480 | tf_op jit(solution)/shard_map/ppermute | solution.py:62
  18.8 28.6 %collective-permute-start = (bf16[144,2048]{1,0:T(8,128)(2,1)}, bf16[144,2048]{1,0:T(8,128)(2,1)}, u32[]{:S(2)}, u32[]{:S(2)}) collective-permute-start(bf16[144,2048]{1,0:T(8,128)(2,1)} %get-tuple-element.235.refs_15_), channel_id=1, source_target_pairs={{0,1},{1,2},{2,3},{3,0},{4,5},{5,6},{6,7},{7,4},{8,9},{9,10},{10,1... | collective-permute-start | bytes 1769480 | tf_op jit(solution)/shard_map/ppermute | solution.py:62
  18.8 28.6 %collective-permute-start.2 = (bf16[128,2048]{1,0:T(8,128)(2,1)}, bf16[128,2048]{1,0:T(8,128)(2,1)}, u32[]{:S(2)}, u32[]{:S(2)}) collective-permute-start(bf16[128,2048]{1,0:T(8,128)(2,1)} %bitcast.77), channel_id=1, source_target_pairs={{0,8},{4,12},{8,0},{12,4},{16,24},{20,28},{24,16},{28,20},{1,9},{5... | collective-permute-start | bytes 1572872 | tf_op jit(solution)/shard_map/ppermute | solution.py:57
  51.5 28.4 %collective-permute-start.6 = (bf16[8,64,1024]{2,1,0:T(8,128)(2,1)S(1)}, bf16[8,64,1024]{2,1,0:T(8,128)(2,1)}, u32[]{:S(2)}, u32[]{:S(2)}) collective-permute-start(bf16[8,64,1024]{2,1,0:T(8,128)(2,1)S(1)} %pad_maximum_fusion.1.refs_8_.refs_14_), channel_id=1, source_target_pairs={{0,1},{1,2},{2,3},{3,0},{4,5},{5,6},{6,7},{7,4},{8,9},{9,10},{10,1... | collective-permute-start | bytes 3145736 | tf_op jit(solution)/shard_map/ppermute | solution.py:62
  84.5 43.0 %collective-permute-start.13 = (bf16[576,2048]{1,0:T(8,128)(2,1)}, bf16[576,2048]{1,0:T(8,128)(2,1)}, u32[]{:S(2)}, u32[]{:S(2)}) collective-permute-start(bf16[576,2048]{1,0:T(8,128)(2,1)} %get-tuple-element.248.refs_1_.refs_8_), channel_id=1, source_target_pairs={{0,4},{4,0},{8,12},{12,8},{16,20},{20,16},{24,28},{28,24},{1,5},{5... | collective-permute-start | bytes 7077896 | tf_op jit(solution)/shard_map/ppermute | solution.py:57
  84.5 42.9 %collective-permute-start.12 = (bf16[512,2048]{1,0:T(8,128)(2,1)}, bf16[512,2048]{1,0:T(8,128)(2,1)}, u32[]{:S(2)}, u32[]{:S(2)}) collective-permute-start(bf16[512,2048]{1,0:T(8,128)(2,1)} %get-tuple-element.247.refs_6_), channel_id=1, source_target_pairs={{0,4},{4,0},{8,12},{12,8},{16,20},{20,16},{24,28},{28,24},{1,5},{5... | collective-permute-start | bytes 6291464 | tf_op jit(solution)/shard_map/ppermute | solution.py:57
  112.3 32.1 %collective-permute-start.16 = (bf16[8,64,1024]{2,1,0:T(8,128)(2,1)}, bf16[8,64,1024]{2,1,0:T(8,128)(2,1)}, u32[]{:S(2)}, u32[]{:S(2)}) collective-permute-start(bf16[8,64,1024]{2,1,0:T(8,128)(2,1)} %collective-permute-done.11.refs_1_.refs_10_.refs_16_), channel_id=1, source_target_pairs={{0,1},{1,2},{2,3},{3,0},{4,5},{5,6},{6,7},{7,4},{8,9},{9,10},{10,1... | collective-permute-start | bytes 3145736 | tf_op jit(solution)/shard_map/ppermute | solution.py:62
  200.8 50.1 %collective-permute-start.28 = (bf16[576,2048]{1,0:T(8,128)(2,1)}, bf16[576,2048]{1,0:T(8,128)(2,1)}, u32[]{:S(2)}, u32[]{:S(2)}) collective-permute-start(bf16[576,2048]{1,0:T(8,128)(2,1)} %get-tuple-element.269.refs_1_.refs_14_), channel_id=1, source_target_pairs={{0,4},{4,0},{8,12},{12,8},{16,20},{20,16},{24,28},{28,24},{1,5},{5... | collective-permute-start | bytes 7077896 | tf_op jit(solution)/shard_map/ppermute | solution.py:57
  200.9 31.5 %all-to-all-start.2 = ((bf16[32,64,176]{2,1,0:T(8,128)(2,1)}), bf16[32,64,176]{2,1,0:T(8,128)(2,1)}, u32[]{:S(2)}, u32[]{:S(2)}) async-start(bf16[32,64,176]{2,1,0:T(8,128)(2,1)} %get-tuple-element.268), calls=%async_computation.2 | async-start | bytes 2097152 | tf_op jit(solution)/shard_map/all_to_all | solution.py:226
  209.1 41.8 %collective-permute-start.29 = (bf16[128,2048]{1,0:T(8,128)(2,1)S(1)}, bf16[128,2048]{1,0:T(8,128)(2,1)}, u32[]{:S(2)}, u32[]{:S(2)}) collective-permute-start(bf16[128,2048]{1,0:T(8,128)(2,1)S(1)} %copy-done.29), channel_id=1, source_target_pairs={{0,8},{4,12},{8,0},{12,4},{16,24},{20,28},{24,16},{28,20},{1,9},{5... | collective-permute-start | bytes 1572872 | tf_op jit(solution)/shard_map/ppermute | solution.py:57
  209.4 41.5 %collective-permute-start.30 = (bf16[128,2048]{1,0:T(8,128)(2,1)S(1)}, bf16[128,2048]{1,0:T(8,128)(2,1)}, u32[]{:S(2)}, u32[]{:S(2)}) collective-permute-start(bf16[128,2048]{1,0:T(8,128)(2,1)S(1)} %copy-done.28), channel_id=1, source_target_pairs={{0,16},{4,20},{8,24},{12,28},{16,0},{20,4},{24,8},{28,12},{1,17},{... | collective-permute-start | bytes 1572872 | tf_op jit(solution)/shard_map/ppermute | solution.py:57
  211.1 39.8 %collective-permute-start.31 = (bf16[128,2048]{1,0:T(8,128)(2,1)S(1)}, bf16[128,2048]{1,0:T(8,128)(2,1)}, u32[]{:S(2)}, u32[]{:S(2)}) collective-permute-start(bf16[128,2048]{1,0:T(8,128)(2,1)S(1)} %copy-done.27), channel_id=1, source_target_pairs={{0,24},{4,28},{8,16},{12,20},{16,8},{20,12},{24,0},{28,4},{1,25},{... | collective-permute-start | bytes 1572872 | tf_op jit(solution)/shard_map/ppermute | solution.py:57
  254.5 32.8 %collective-permute-start.35 = (bf16[576,2048]{1,0:T(8,128)(2,1)}, bf16[576,2048]{1,0:T(8,128)(2,1)}, u32[]{:S(2)}, u32[]{:S(2)}) collective-permute-start(bf16[576,2048]{1,0:T(8,128)(2,1)} %get-tuple-element.282.refs_1_.refs_12_), channel_id=1, source_target_pairs={{0,4},{4,0},{8,12},{12,8},{16,20},{20,16},{24,28},{28,24},{1,5},{5... | collective-permute-start | bytes 7077896 | tf_op jit(solution)/shard_map/ppermute | solution.py:57
  319.2 35.1 %collective-permute-start.44 = (bf16[512,2048]{1,0:T(8,128)(2,1)}, bf16[512,2048]{1,0:T(8,128)(2,1)}, u32[]{:S(2)}, u32[]{:S(2)}) collective-permute-start(bf16[512,2048]{1,0:T(8,128)(2,1)} %get-tuple-element.299.refs_1_.refs_2_), channel_id=1, source_target_pairs={{0,4},{4,0},{8,12},{12,8},{16,20},{20,16},{24,28},{28,24},{1,5},{5... | collective-permute-start | bytes 6291464 | tf_op jit(solution)/shard_map/ppermute | solution.py:57
  319.3 34.9 %collective-permute-start.48 = (bf16[128,2048]{1,0:T(8,128)(2,1)}, bf16[128,2048]{1,0:T(8,128)(2,1)}, u32[]{:S(2)}, u32[]{:S(2)}) collective-permute-start(bf16[128,2048]{1,0:T(8,128)(2,1)} %collective-permute-done.40.refs_4_.refs_8_), channel_id=1, source_target_pairs={{0,24},{4,28},{8,16},{12,20},{16,8},{20,12},{24,0},{28,4},{1,25},{... | collective-permute-start | bytes 1572872 | tf_op jit(solution)/shard_map/ppermute | solution.py:57
  320.8 33.4 %collective-permute-start.47 = (bf16[128,2048]{1,0:T(8,128)(2,1)}, bf16[128,2048]{1,0:T(8,128)(2,1)}, u32[]{:S(2)}, u32[]{:S(2)}) collective-permute-start(bf16[128,2048]{1,0:T(8,128)(2,1)} %collective-permute-done.40.refs_4_.refs_8_), channel_id=1, source_target_pairs={{0,16},{4,20},{8,24},{12,28},{16,0},{20,4},{24,8},{28,12},{1,17},{... | collective-permute-start | bytes 1572872 | tf_op jit(solution)/shard_map/ppermute | solution.py:57
  321.8 32.4 %collective-permute-start.46 = (bf16[128,2048]{1,0:T(8,128)(2,1)}, bf16[128,2048]{1,0:T(8,128)(2,1)}, u32[]{:S(2)}, u32[]{:S(2)}) collective-permute-start(bf16[128,2048]{1,0:T(8,128)(2,1)} %collective-permute-done.40.refs_4_.refs_8_), channel_id=1, source_target_pairs={{0,8},{4,12},{8,0},{12,4},{16,24},{20,28},{24,16},{28,20},{1,9},{5... | collective-permute-start | bytes 1572872 | tf_op jit(solution)/shard_map/ppermute | solution.py:57
  322.8 31.4 %collective-permute-start.45 = (bf16[128,2048]{1,0:T(8,128)(2,1)}, bf16[128,2048]{1,0:T(8,128)(2,1)}, u32[]{:S(2)}, u32[]{:S(2)}) collective-permute-start(bf16[128,2048]{1,0:T(8,128)(2,1)} %collective-permute-done.40.refs_4_.refs_8_), channel_id=1, source_target_pairs={{0,1},{1,2},{2,3},{3,0},{4,5},{5,6},{6,7},{7,4},{8,9},{9,10},{10,1... | collective-permute-start | bytes 1572872 | tf_op jit(solution)/shard_map/ppermute | solution.py:62
  356.7 31.9 %collective-permute-start.53 = (bf16[576,2048]{1,0:T(8,128)(2,1)}, bf16[576,2048]{1,0:T(8,128)(2,1)}, u32[]{:S(2)}, u32[]{:S(2)}) collective-permute-start(bf16[576,2048]{1,0:T(8,128)(2,1)} %get-tuple-element.310), channel_id=1, source_target_pairs={{0,4},{4,0},{8,12},{12,8},{16,20},{20,16},{24,28},{28,24},{1,5},{5... | collective-permute-start | bytes 7077896 | tf_op jit(solution)/shard_map/ppermute | solution.py:57
  356.8 31.8 %collective-permute-start.49 = (bf16[512,2048]{1,0:T(8,128)(2,1)}, bf16[512,2048]{1,0:T(8,128)(2,1)}, u32[]{:S(2)}, u32[]{:S(2)}) collective-permute-start(bf16[512,2048]{1,0:T(8,128)(2,1)} %get-tuple-element.309.refs_1_.refs_4_), channel_id=1, source_target_pairs={{0,4},{4,0},{8,12},{12,8},{16,20},{20,16},{24,28},{28,24},{1,5},{5... | collective-permute-start | bytes 6291464 | tf_op jit(solution)/shard_map/ppermute | solution.py:57
  357.3 31.3 %collective-permute-start.52 = (bf16[128,2048]{1,0:T(8,128)(2,1)}, bf16[128,2048]{1,0:T(8,128)(2,1)}, u32[]{:S(2)}, u32[]{:S(2)}) collective-permute-start(bf16[128,2048]{1,0:T(8,128)(2,1)} %collective-permute-done.45.refs_4_.refs_7_), channel_id=1, source_target_pairs={{0,24},{4,28},{8,16},{12,20},{16,8},{20,12},{24,0},{28,4},{1,25},{... | collective-permute-start | bytes 1572872 | tf_op jit(solution)/shard_map/ppermute | solution.py:57
  358.8 29.8 %collective-permute-start.51 = (bf16[128,2048]{1,0:T(8,128)(2,1)}, bf16[128,2048]{1,0:T(8,128)(2,1)}, u32[]{:S(2)}, u32[]{:S(2)}) collective-permute-start(bf16[128,2048]{1,0:T(8,128)(2,1)} %collective-permute-done.45.refs_4_.refs_7_), channel_id=1, source_target_pairs={{0,16},{4,20},{8,24},{12,28},{16,0},{20,4},{24,8},{28,12},{1,17},{... | collective-permute-start | bytes 1572872 | tf_op jit(solution)/shard_map/ppermute | solution.py:57
  359.9 28.6 %collective-permute-start.50 = (bf16[128,2048]{1,0:T(8,128)(2,1)}, bf16[128,2048]{1,0:T(8,128)(2,1)}, u32[]{:S(2)}, u32[]{:S(2)}) collective-permute-start(bf16[128,2048]{1,0:T(8,128)(2,1)} %collective-permute-done.45.refs_4_.refs_7_), channel_id=1, source_target_pairs={{0,8},{4,12},{8,0},{12,4},{16,24},{20,28},{24,16},{28,20},{1,9},{5... | collective-permute-start | bytes 1572872 | tf_op jit(solution)/shard_map/ppermute | solution.py:57
  393.7 31.9 %collective-permute-start.58 = (bf16[576,2048]{1,0:T(8,128)(2,1)}, bf16[576,2048]{1,0:T(8,128)(2,1)}, u32[]{:S(2)}, u32[]{:S(2)}) collective-permute-start(bf16[576,2048]{1,0:T(8,128)(2,1)} %get-tuple-element.326), channel_id=1, source_target_pairs={{0,4},{4,0},{8,12},{12,8},{16,20},{20,16},{24,28},{28,24},{1,5},{5... | collective-permute-start | bytes 7077896 | tf_op jit(solution)/shard_map/ppermute | solution.py:57
  393.8 31.8 %collective-permute-start.54 = (bf16[512,2048]{1,0:T(8,128)(2,1)}, bf16[512,2048]{1,0:T(8,128)(2,1)}, u32[]{:S(2)}, u32[]{:S(2)}) collective-permute-start(bf16[512,2048]{1,0:T(8,128)(2,1)} %get-tuple-element.321.refs_1_.refs_6_), channel_id=1, source_target_pairs={{0,4},{4,0},{8,12},{12,8},{16,20},{20,16},{24,28},{28,24},{1,5},{5... | collective-permute-start | bytes 6291464 | tf_op jit(solution)/shard_map/ppermute | solution.py:57
  394.2 31.3 %collective-permute-start.55 = (bf16[144,2048]{1,0:T(8,128)(2,1)}, bf16[144,2048]{1,0:T(8,128)(2,1)}, u32[]{:S(2)}, u32[]{:S(2)}) collective-permute-start(bf16[144,2048]{1,0:T(8,128)(2,1)} %get-tuple-element.322), channel_id=1, source_target_pairs={{0,8},{4,12},{8,0},{12,4},{16,24},{20,28},{24,16},{28,20},{1,9},{5... | collective-permute-start | bytes 1769480 | tf_op jit(solution)/shard_map/ppermute | solution.py:57
  395.4 30.1 %collective-permute-start.56 = (bf16[144,2048]{1,0:T(8,128)(2,1)}, bf16[144,2048]{1,0:T(8,128)(2,1)}, u32[]{:S(2)}, u32[]{:S(2)}) collective-permute-start(bf16[144,2048]{1,0:T(8,128)(2,1)} %get-tuple-element.323), channel_id=1, source_target_pairs={{0,16},{4,20},{8,24},{12,28},{16,0},{20,4},{24,8},{28,12},{1,17},{... | collective-permute-start | bytes 1769480 | tf_op jit(solution)/shard_map/ppermute | solution.py:57
  396.3 29.3 %collective-permute-start.57 = (bf16[144,2048]{1,0:T(8,128)(2,1)}, bf16[144,2048]{1,0:T(8,128)(2,1)}, u32[]{:S(2)}, u32[]{:S(2)}) collective-permute-start(bf16[144,2048]{1,0:T(8,128)(2,1)} %get-tuple-element.324), channel_id=1, source_target_pairs={{0,24},{4,28},{8,16},{12,20},{16,8},{20,12},{24,0},{28,4},{1,25},{... | collective-permute-start | bytes 1769480 | tf_op jit(solution)/shard_map/ppermute | solution.py:57
  430.1 31.7 %collective-permute-start.62 = (bf16[576,2048]{1,0:T(8,128)(2,1)}, bf16[576,2048]{1,0:T(8,128)(2,1)}, u32[]{:S(2)}, u32[]{:S(2)}) collective-permute-start(bf16[576,2048]{1,0:T(8,128)(2,1)} %get-tuple-element.341), channel_id=1, source_target_pairs={{0,4},{4,0},{8,12},{12,8},{16,20},{20,16},{24,28},{28,24},{1,5},{5... | collective-permute-start | bytes 7077896 | tf_op jit(solution)/shard_map/ppermute | solution.py:57
  430.2 31.6 %collective-permute-start.59 = (bf16[144,2048]{1,0:T(8,128)(2,1)}, bf16[144,2048]{1,0:T(8,128)(2,1)}, u32[]{:S(2)}, u32[]{:S(2)}) collective-permute-start(bf16[144,2048]{1,0:T(8,128)(2,1)} %get-tuple-element.337), channel_id=1, source_target_pairs={{0,8},{4,12},{8,0},{12,4},{16,24},{20,28},{24,16},{28,20},{1,9},{5... | collective-permute-start | bytes 1769480 | tf_op jit(solution)/shard_map/ppermute | solution.py:57
  431.5 30.4 %collective-permute-start.60 = (bf16[144,2048]{1,0:T(8,128)(2,1)}, bf16[144,2048]{1,0:T(8,128)(2,1)}, u32[]{:S(2)}, u32[]{:S(2)}) collective-permute-start(bf16[144,2048]{1,0:T(8,128)(2,1)} %get-tuple-element.338), channel_id=1, source_target_pairs={{0,16},{4,20},{8,24},{12,28},{16,0},{20,4},{24,8},{28,12},{1,17},{... | collective-permute-start | bytes 1769480 | tf_op jit(solution)/shard_map/ppermute | solution.py:57
  432.3 29.5 %collective-permute-start.61 = (bf16[144,2048]{1,0:T(8,128)(2,1)}, bf16[144,2048]{1,0:T(8,128)(2,1)}, u32[]{:S(2)}, u32[]{:S(2)}) collective-permute-start(bf16[144,2048]{1,0:T(8,128)(2,1)} %get-tuple-element.339), channel_id=1, source_target_pairs={{0,24},{4,28},{8,16},{12,20},{16,8},{20,12},{24,0},{28,4},{1,25},{... | collective-permute-start | bytes 1769480 | tf_op jit(solution)/shard_map/ppermute | solution.py:57
  466.4 30.7 %collective-permute-start.67 = (bf16[576,2048]{1,0:T(8,128)(2,1)}, bf16[576,2048]{1,0:T(8,128)(2,1)}, u32[]{:S(2)}, u32[]{:S(2)}) collective-permute-start(bf16[576,2048]{1,0:T(8,128)(2,1)} %get-tuple-element.355), channel_id=1, source_target_pairs={{0,4},{4,0},{8,12},{12,8},{16,20},{20,16},{24,28},{28,24},{1,5},{5... | collective-permute-start | bytes 7077896 | tf_op jit(solution)/shard_map/ppermute | solution.py:57
  501.7 32.9 %collective-permute-start.72 = (bf16[512,2048]{1,0:T(8,128)(2,1)}, bf16[512,2048]{1,0:T(8,128)(2,1)}, u32[]{:S(2)}, u32[]{:S(2)}) collective-permute-start(bf16[512,2048]{1,0:T(8,128)(2,1)} %get-tuple-element.368), channel_id=1, source_target_pairs={{0,4},{4,0},{8,12},{12,8},{16,20},{20,16},{24,28},{28,24},{1,5},{5... | collective-permute-start | bytes 6291464 | tf_op jit(solution)/shard_map/ppermute | solution.py:57
  538.6 29.2 %collective-permute-start.77 = (bf16[512,2048]{1,0:T(8,128)(2,1)}, bf16[512,2048]{1,0:T(8,128)(2,1)}, u32[]{:S(2)}, u32[]{:S(2)}) collective-permute-start(bf16[512,2048]{1,0:T(8,128)(2,1)} %get-tuple-element.381), channel_id=1, source_target_pairs={{0,4},{4,0},{8,12},{12,8},{16,20},{20,16},{24,28},{28,24},{1,5},{5... | collective-permute-start | bytes 6291464 | tf_op jit(solution)/shard_map/ppermute | solution.py:57
  571.9 33.8 %collective-permute-start.81 = (bf16[512,2048]{1,0:T(8,128)(2,1)}, bf16[512,2048]{1,0:T(8,128)(2,1)}, u32[]{:S(2)}, u32[]{:S(2)}) collective-permute-start(bf16[512,2048]{1,0:T(8,128)(2,1)} %get-tuple-element.390), channel_id=1, source_target_pairs={{0,4},{4,0},{8,12},{12,8},{16,20},{20,16},{24,28},{28,24},{1,5},{5... | collective-permute-start | bytes 6291464 | tf_op jit(solution)/shard_map/ppermute | solution.py:57
  610.6 33.0 %collective-permute-start.82 = (bf16[512,2048]{1,0:T(8,128)(2,1)}, bf16[512,2048]{1,0:T(8,128)(2,1)}, u32[]{:S(2)}, u32[]{:S(2)}) collective-permute-start(bf16[512,2048]{1,0:T(8,128)(2,1)} %get-tuple-element.392.refs_5_), channel_id=1, source_target_pairs={{0,4},{4,0},{8,12},{12,8},{16,20},{20,16},{24,28},{28,24},{1,5},{5... | collective-permute-start | bytes 6291464 | tf_op jit(solution)/shard_map/ppermute | solution.py:57
  640.0 47.6 %collective-permute-start.91 = (bf16[512,2048]{1,0:T(8,128)(2,1)}, bf16[512,2048]{1,0:T(8,128)(2,1)}, u32[]{:S(2)}, u32[]{:S(2)}) collective-permute-start(bf16[512,2048]{1,0:T(8,128)(2,1)} %get-tuple-element.422), channel_id=1, source_target_pairs={{0,4},{4,0},{8,12},{12,8},{16,20},{20,16},{24,28},{28,24},{1,5},{5... | collective-permute-start | bytes 6291464 | tf_op jit(solution)/shard_map/ppermute | solution.py:57
  646.3 41.4 %all-to-all-start.3 = ((bf16[32,64,256]{2,1,0:T(8,128)(2,1)}), bf16[32,64,256]{2,1,0:T(8,128)(2,1)}, u32[]{:S(2)}, u32[]{:S(2)}) async-start(bf16[32,64,256]{2,1,0:T(8,128)(2,1)} %get-tuple-element.416), calls=%async_computation.3 | async-start | bytes 2097152 | tf_op jit(solution)/shard_map/all_to_all | solution.py:226
  650.2 33.0 %collective-permute-start.88 = (bf16[128,2048]{1,0:T(8,128)(2,1)}, bf16[128,2048]{1,0:T(8,128)(2,1)}, u32[]{:S(2)}, u32[]{:S(2)}) collective-permute-start(bf16[128,2048]{1,0:T(8,128)(2,1)} %get-tuple-element.418), channel_id=1, source_target_pairs={{0,8},{4,12},{8,0},{12,4},{16,24},{20,28},{24,16},{28,20},{1,9},{5... | collective-permute-start | bytes 1572872 | tf_op jit(solution)/shard_map/ppermute | solution.py:57
  652.0 31.3 %collective-permute-start.89 = (bf16[128,2048]{1,0:T(8,128)(2,1)}, bf16[128,2048]{1,0:T(8,128)(2,1)}, u32[]{:S(2)}, u32[]{:S(2)}) collective-permute-start(bf16[128,2048]{1,0:T(8,128)(2,1)} %get-tuple-element.419), channel_id=1, source_target_pairs={{0,16},{4,20},{8,24},{12,28},{16,0},{20,4},{24,8},{28,12},{1,17},{... | collective-permute-start | bytes 1572872 | tf_op jit(solution)/shard_map/ppermute | solution.py:57
  653.4 34.2 %collective-permute-start.90 = (bf16[128,2048]{1,0:T(8,128)(2,1)}, bf16[128,2048]{1,0:T(8,128)(2,1)}, u32[]{:S(2)}, u32[]{:S(2)}) collective-permute-start(bf16[128,2048]{1,0:T(8,128)(2,1)} %get-tuple-element.420), channel_id=1, source_target_pairs={{0,24},{4,28},{8,16},{12,20},{16,8},{20,12},{24,0},{28,4},{1,25},{... | collective-permute-start | bytes 1572872 | tf_op jit(solution)/shard_map/ppermute | solution.py:57
  655.7 31.9 %collective-permute-start.87 = (bf16[128,2048]{1,0:T(8,128)(2,1)}, bf16[128,2048]{1,0:T(8,128)(2,1)}, u32[]{:S(2)}, u32[]{:S(2)}) collective-permute-start(bf16[128,2048]{1,0:T(8,128)(2,1)} %add_convert_fusion.4), channel_id=1, source_target_pairs={{0,1},{1,2},{2,3},{3,0},{4,5},{5,6},{6,7},{7,4},{8,9},{9,10},{10,1... | collective-permute-start | bytes 1572872 | tf_op jit(solution)/shard_map/ppermute | solution.py:62
  691.6 32.5 %collective-permute-start.93 = (bf16[512,2048]{1,0:T(8,128)(2,1)}, bf16[512,2048]{1,0:T(8,128)(2,1)}, u32[]{:S(2)}, u32[]{:S(2)}) collective-permute-start(bf16[512,2048]{1,0:T(8,128)(2,1)} %get-tuple-element.429), channel_id=1, source_target_pairs={{0,4},{4,0},{8,12},{12,8},{16,20},{20,16},{24,28},{28,24},{1,5},{5... | collective-permute-start | bytes 6291464 | tf_op jit(solution)/shard_map/ppermute | solution.py:57
  729.9 28.8 %collective-permute-start.97 = (bf16[512,1024]{1,0:T(8,128)(2,1)}, bf16[512,1024]{1,0:T(8,128)(2,1)}, u32[]{:S(2)}, u32[]{:S(2)}) collective-permute-start(bf16[512,1024]{1,0:T(8,128)(2,1)} %get-tuple-element.437), channel_id=1, source_target_pairs={{0,1},{1,2},{2,3},{3,0},{4,5},{5,6},{6,7},{7,4},{8,9},{9,10},{10,1... | collective-permute-start | bytes 3145736 | tf_op jit(solution)/shard_map/ppermute | solution.py:62
  (93 other events, 1527.8 us)
